TPU v7x, 256 devices: a whole 4x4x8 slice. The times are simulated.
256 devices in a mesh: gx: 8 (over z), gy: 4 (over x), gz: 8 (over y, core).
Axes of the slice: x: 4, y: 4, z: 8, core: 2. Of those that a mesh axis runs over, the one named last changes fastest.
Arguments:
- pressure: float32 [16384, 512], P(('gx', 'gy', 'gz')), may hold values from -6 to 6
- rhs: float32 [16384, 512], P(('gx', 'gy', 'gz')), may hold values from -6 to 6
- jacobi: float32 [16384, 512], P(('gx', 'gy', 'gz')), may hold values from 0.05 to 0.5
- geom: float32 [3, 16384, 512], P(None, ('gx', 'gy', 'gz')), may hold values from 0.005 to 0.05
- velocity: float32 [3, 16384, 512], P(None, ('gx', 'gy', 'gz')), may hold values from -6 to 6
- force: float32 [3, 16384, 512], P(None, ('gx', 'gy', 'gz')), may hold values from -6 to 6
- mass: float32 [16384, 512], P(('gx', 'gy', 'gz')), may hold values from 0.2 to 2
- metric: float32 [3, 16384], P(None, ('gx', 'gy', 'gz')), may hold values from 0.05 to 0.5
- conn: int32 [16384, 512], P(('gx', 'gy', 'gz')), may hold values from 0 to 25991, as said below
- ent_peer: int32 [256, 8192], P(('gx', 'gy', 'gz')), may hold values from 0 to 31, as said below
- ent_slot: int32 [256, 8192], P(('gx', 'gy', 'gz')), may hold values from 0 to 255
- ent_node: int32 [256, 8192], P(('gx', 'gy', 'gz')), may hold values from 0 to 25991, as said below
- counts: int32 [256, 32], P(('gx', 'gy', 'gz')), may hold values from 0 to 256, as said below
- axial_nodes: int32 [256, 2, 2048], P(('gx', 'gy', 'gz')), may hold values from 0 to 25991, as said below
Outputs:
- new_pressure: float32 [16384, 512], P(('gx', 'gy', 'gz'))
- momentum_residual: float32 [3, 16384, 512], P(None, ('gx', 'gy', 'gz'))
Inputs may be any that keep to these rules, and one draw needn't show every extreme that they name: `conn`: each device's elements form a brick of 8 x 8 x 1 elements in some order, with nodes 0 to 25991 numbered in some order; every element point has one node. The pairs (ent_peer, ent_slot) of one device are all different. `ent_node`: each entry's node lies on the side of the device's brick (first or last node along its first or second direction); several entries may name the same node. counts is symmetric between two ranks of one slab and 0 towards a device's own rank; a nonzero count is 128 or more; each slab has a pair with 256. `axial_nodes`: the lower list (0) holds different nodes of the brick's first node layer along its third direction, the upper list (1) different nodes of its last layer; slot k of a device's upper list pairs with slot k of the lower list of the same rank in the next slab.
All inputs are finite; a program needn't handle non-finite values.
Results may differ from a plain program's by a relative error of at most 0.0001.
Values sent between devices are 32-bit elements; how exact they have to be, the bound alone decides.
No kernel may reach another device: no remote copies, remote signals or barrier semaphores. Data moves between devices by JAX's collectives and lax.ppermute only.
A program may use at most 128 MiB of HBM per device.

v0:
```python
import jax
import jax.numpy as jnp
import numpy as np
from jax import lax
from jax.sharding import PartitionSpec as P

NODES = 25992
SLOTS = 256


VISCOSITY = 0.2
CHEB_THETA = 1.1
CHEB_DELTA = 0.9
RHO_FIRST = 9.0 / 11.0
RHO_NEXT = 99.0 / 161.0


def padded(cells, sides, width):
    for axis, dim in sides:
        count = lax.axis_size(axis)
        head = lax.slice_in_dim(cells, 0, width, axis=dim)
        tail = lax.slice_in_dim(cells, cells.shape[dim] - width, cells.shape[dim], axis=dim)
        cells = jnp.concatenate(
            [
                lax.ppermute(tail, axis, [(i, (i + 1) % count) for i in range(count)]),
                cells,
                lax.ppermute(head, axis, [((i + 1) % count, i) for i in range(count)]),
            ],
            axis=dim,
        )
    return cells


def deriv_table():
    points = np.array(
        [
            -1.0,
            -0.8717401485096066,
            -0.5917001814331423,
            -0.2092992179024789,
            0.2092992179024789,
            0.5917001814331423,
            0.8717401485096066,
            1.0,
        ]
    )
    before = np.ones(8)
    legendre = points.copy()
    for degree in range(1, 7):
        after = ((2 * degree + 1) * points * legendre - degree * before) / (degree + 1)
        before = legendre
        legendre = after
    spread = points[:, None] - points[None, :]
    safe = np.where(spread == 0.0, 1.0, spread)
    deriv = legendre[:, None] / (legendre[None, :] * safe)
    deriv = np.where(spread == 0.0, 0.0, deriv)
    deriv[0, 0] = -14.0
    deriv[7, 7] = 14.0
    return deriv


def kron_tables():
    deriv = deriv_table()
    eye_one = np.eye(8)
    eye_two = np.eye(64)
    first_dir = np.kron(deriv, eye_two)
    second_dir = np.kron(eye_one, np.kron(deriv, eye_one))
    third_dir = np.kron(eye_two, deriv)
    return [jnp.asarray(table, jnp.float32) for table in (first_dir, second_dir, third_dir)]


def forward(field, table):
    return jnp.matmul(field, table.T, precision=lax.Precision.HIGHEST)


def backward(field, table):
    return jnp.matmul(field, table, precision=lax.Precision.HIGHEST)


def laplace(field, geom, tables):
    result = jnp.zeros_like(field)
    for axis in range(3):
        result = result + backward(geom[axis] * forward(field, tables[axis]), tables[axis])
    return result


def momentum_terms(velocity, force, mass, metric, geom, tables):
    convect = jnp.zeros_like(velocity)
    diffuse = jnp.zeros_like(velocity)
    for axis in range(3):
        grad = forward(velocity, tables[axis])
        convect = convect + metric[axis][:, None] * velocity[axis] * grad
        diffuse = diffuse + backward(geom[axis] * grad, tables[axis])
    return mass * (force - convect) - VISCOSITY * diffuse


def gather_scatter(stack, conn, ent_peer, ent_slot, ent_node, counts, axial_nodes):
    width = stack.shape[0]
    node_ids = conn.reshape(-1)
    local = jax.vmap(lambda row: jax.ops.segment_sum(row, node_ids, num_segments=NODES))(
        stack.reshape(width, -1)
    )
    peer = ent_peer[0]
    slot = ent_slot[0]
    node = ent_node[0]
    valid = (slot < jnp.take(counts[0], peer)).astype(jnp.float32)
    sent = local[:, node] * valid
    ranks = counts.shape[1]
    buffer = jnp.zeros((width, ranks, SLOTS), jnp.float32).at[:, peer, slot].set(sent)
    arrived = lax.all_to_all(buffer, ("gy", "gz"), split_axis=1, concat_axis=1, tiled=True)
    received = arrived[:, peer, slot] * valid
    faces = axial_nodes[0]
    rims = local[:, faces]
    extended = padded(rims, (("gx", 1),), 1)
    total = local.at[:, node].add(received)
    total = total.at[:, faces[0]].add(extended[:, 0])
    total = total.at[:, faces[1]].add(extended[:, 3])
    return total[:, node_ids].reshape(stack.shape)


def on_device(
    pressure,
    rhs,
    jacobi,
    geom,
    velocity,
    force,
    mass,
    metric,
    conn,
    ent_peer,
    ent_slot,
    ent_node,
    counts,
    axial_nodes,
):
    tables = kron_tables()

    def assemble(stack):
        return gather_scatter(stack, conn, ent_peer, ent_slot, ent_node, counts, axial_nodes)

    applied = assemble(laplace(pressure, geom, tables)[None])[0]
    start_res = rhs - applied
    step_first = jacobi * start_res / CHEB_THETA
    first = pressure + step_first
    next_res = start_res - assemble(laplace(step_first, geom, tables)[None])[0]
    step_next = RHO_NEXT * RHO_FIRST * step_first + 2.0 * RHO_NEXT / CHEB_DELTA * jacobi * next_res
    new_pressure = first + step_next
    momentum_residual = assemble(momentum_terms(velocity, force, mass, metric, geom, tables))
    return (new_pressure, momentum_residual)


def solution(mesh):
    return jax.shard_map(
        on_device,
        mesh=mesh,
        in_specs=(
            P(("gx", "gy", "gz"), None),
            P(("gx", "gy", "gz"), None),
            P(("gx", "gy", "gz"), None),
            P(None, ("gx", "gy", "gz"), None),
            P(None, ("gx", "gy", "gz"), None),
            P(None, ("gx", "gy", "gz"), None),
            P(("gx", "gy", "gz"), None),
            P(None, ("gx", "gy", "gz")),
            P(("gx", "gy", "gz"), None),
            P(("gx", "gy", "gz"), None),
            P(("gx", "gy", "gz"), None),
            P(("gx", "gy", "gz"), None),
            P(("gx", "gy", "gz"), None),
            P(("gx", "gy", "gz"), None, None),
        ),
        out_specs=(P(("gx", "gy", "gz"), None), P(None, ("gx", "gy", "gz"), None)),
        check_vma=False,
    )
```

profile of v0, /device:TPU:1, one launch (start us, length us, event | category | flops | bytes accessed | tf_op | source)
XLA Modules:
  0.0 2020.4 jit_solution(5163158368521846254)
XLA Ops:
  21.3 179.8 %scatter_custom_fusion.8 = f32[3,25992]{0,1:T(8,128)} fusion(s32[32768]{0:T(1024)S(1)} %bitcast.212, f32[32768,3]{1,0:T(8,128)} %bitcast.190, f32[]{:T(128)} %constant.20.clone.1), kind=kCustom, calls=%fused_computation.27 | custom fusion | flops 98304 | bytes 312416 | tf_op jit(solution)/shard_map/vmap()/scatter-add | solution.py:100
  201.2 19.0 gather_fusion.8
  242.2 171.1 %scatter_custom_fusion = f32[25992]{0:T(1024)S(1)} fusion(s32[32768]{0:T(1024)} %bitcast.213, f32[32768]{0:T(1024)} %bitcast.216, f32[]{:T(128)} %constant.20.clone.1), kind=kCustom, calls=%fused_computation.90 | custom fusion | flops 32768 | bytes 104480 | tf_op jit(solution)/shard_map/vmap()/scatter-add | solution.py:100
  413.4 45.5 %gather_fusion = f32[8192]{0:T(1024)S(1)} fusion(f32[25992]{0:T(1024)S(1)} %scatter_custom_fusion, s32[8192]{0:T(1024)S(1)} %get-tuple-element.66), kind=kCustom, calls=%fused_computation | custom fusion | bytes 98304 | tf_op jit(solution)/shard_map/gather | solution.py:107
  458.9 20.0 fusion.46
  479.0 31.0 %scatter_custom_fusion.12 = f32[8192]{0:T(1024)} fusion(s32[8192]{0:T(1024)S(1)} %get-tuple-element.67, f32[8192]{0:T(1024)S(1)} %broadcast_select_fusion.3, f32[]{:T(128)} %constant.20.clone.1), kind=kCustom, calls=%fused_computation.111 | custom fusion | bytes 32772
  518.1 40.5 %gather_fusion.2 = f32[4096]{0:T(1024)} fusion(f32[25992]{0:T(1024)S(1)} %scatter_custom_fusion, s32[4096]{0:T(1024)S(1)} %broadcast_clamp_fusion.2), kind=kCustom, calls=%fused_computation.2 | custom fusion | bytes 49152 | tf_op jit(solution)/shard_map/gather | solution.py:113
  563.9 72.9 %scatter_custom_fusion.14 = f32[3,8192]{0,1:T(8,128)} fusion(s32[8192]{0:T(1024)} %copy-done.25, f32[8192]{0:T(1024)S(1)} %get-tuple-element.9, f32[]{:T(128)} %constant.20.clone.1, f32[3,25992]{0,1:T(8,128)} %scatter_custom_fusion.8, s32[8192]{0:T(1024)S(1)} %get-tuple-element.66), kind=kCustom, calls=%fused_computation.29 | custom fusion | flops 24576 | bytes 13472256
  645.3 100.1 %gather_fusion.1 = f32[8192]{0:T(1024)} fusion(f32[32,256]{1,0:T(8,128)S(1)} %bitcast.184, s32[8192]{0:T(1024)S(1)} %bitcast.186), kind=kCustom, calls=%fused_computation.1 | custom fusion | bytes 131072 | tf_op jit(solution)/shard_map/gather | solution.py:111
  746.1 44.1 %scatter_fusion = f32[25992]{0:T(1024)S(1)} fusion(f32[25992]{0:T(1024)S(1)} %scatter_custom_fusion, s32[8192]{0:T(1024)S(1)} %bitcast.194, f32[8192]{0:T(1024)S(1)} %broadcast_select_fusion.2), kind=kCustom, calls=%fused_computation.13 | custom fusion | flops 8192 | bytes 131072 | tf_op jit(solution)/shard_map/scatter-add | solution.py:115
  802.0 12.1 scatter_fusion.2
  814.1 320.7 %gather_fusion.3 = f32[32768]{0:T(1024)} fusion(f32[25992]{0:T(1024)S(1)} %scatter_fusion.2, s32[32768]{0:T(1024)S(1)} %broadcast_clamp_fusion), kind=kCustom, calls=%fused_computation.3 | custom fusion | bytes 393216 | tf_op jit(solution)/shard_map/gather | solution.py:118
  1145.9 171.2 %scatter_custom_fusion.4 = f32[25992]{0:T(1024)S(1)} fusion(s32[32768]{0:T(1024)} %bitcast.214, f32[32768]{0:T(1024)S(1)} %bitcast.215, f32[]{:T(128)} %constant.20.clone.1), kind=kCustom, calls=%fused_computation.88 | custom fusion | flops 32768 | bytes 104480 | tf_op jit(solution)/shard_map/vmap()/scatter-add | solution.py:100
  1317.2 45.5 %gather_fusion.4 = f32[8192]{0:T(1024)S(1)} fusion(f32[25992]{0:T(1024)S(1)} %scatter_custom_fusion.4, s32[8192]{0:T(1024)S(1)} %get-tuple-element.66), kind=kCustom, calls=%fused_computation.4 | custom fusion | bytes 98304 | tf_op jit(solution)/shard_map/gather | solution.py:107
  1362.7 23.0 %gather_fusion.6 = f32[4096]{0:T(1024)S(1)} fusion(f32[25992]{0:T(1024)S(1)} %scatter_custom_fusion.4, s32[4096]{0:T(1024)S(1)} %broadcast_clamp_fusion.2), kind=kCustom, calls=%fused_computation.6 | custom fusion | bytes 49152 | tf_op jit(solution)/shard_map/gather | solution.py:113
  1385.7 31.2 %scatter_custom_fusion.13 = f32[8192]{0:T(1024)} fusion(s32[8192]{0:T(1024)} %copy-done.25, f32[8192]{0:T(1024)S(1)} %broadcast_select_fusion.1, f32[]{:T(128)} %constant.20.clone.1), kind=kCustom, calls=%fused_computation.105 | custom fusion | bytes 33280
  1436.1 65.0 %gather_fusion.5 = f32[8192]{0:T(1024)S(1)} fusion(f32[32,256]{1,0:T(8,128)S(1)} %bitcast.185, s32[8192]{0:T(1024)S(1)} %bitcast.187), kind=kCustom, calls=%fused_computation.5 | custom fusion | bytes 131072 | tf_op jit(solution)/shard_map/gather | solution.py:111
  1501.1 44.1 %scatter_fusion.3 = f32[25992]{0:T(1024)S(1)} fusion(f32[25992]{0:T(1024)S(1)} %scatter_custom_fusion.4, s32[8192]{0:T(1024)S(1)} %bitcast.195, f32[8192]{0:T(1024)S(1)} %broadcast_select_fusion), kind=kCustom, calls=%fused_computation.17 | custom fusion | flops 8192 | bytes 131072 | tf_op jit(solution)/shard_map/scatter-add | solution.py:115
  1545.3 11.7 scatter_fusion.4
  1568.5 180.5 %gather_fusion.7 = f32[32768]{0:T(1024)S(1)} fusion(f32[25992]{0:T(1024)S(1)} %scatter_fusion.5, s32[32768]{0:T(1024)S(1)} %copy-done.12), kind=kCustom, calls=%fused_computation.7 | custom fusion | bytes 393216 | tf_op jit(solution)/shard_map/gather | solution.py:118
  1752.5 103.5 %scatter_custom_fusion.9 = f32[3,25992]{0,1:T(8,128)} fusion(f32[3,25992]{0,1:T(8,128)} %scatter_custom_fusion.8, s32[8192]{0:T(1024)S(1)} %bitcast.196, f32[8192]{0:T(1024)S(1)} %copy-done.18, f32[3,32,256]{0,2,1:T(8,128)} %copy.25, s32[8192]{0:T(1024)S(1)} %bitcast.188), kind=kCustom, calls=%fused_computation.31 | custom fusion | flops 49152 | bytes 4571744 | tf_op jit(solution)/shard_map/scatter-add | solution.py:115
  1856.0 20.2 %scatter_fusion.6 = f32[3,25992]{0,1:T(8,128)} fusion(f32[3,25992]{0,1:T(8,128)} %scatter_custom_fusion.9, s32[2048]{0:T(1024)S(1)} %bitcast.209, f32[2048,3]{1,0:T(8,128)} %copy.27), kind=kCustom, calls=%fused_computation.22 | custom fusion | flops 6144 | bytes 81920 | tf_op jit(solution)/shard_map/scatter-add | solution.py:116
  1876.2 20.2 %scatter_fusion.7 = f32[3,25992]{0,1:T(8,128)} fusion(f32[3,25992]{0,1:T(8,128)} %scatter_fusion.6, s32[2048]{0:T(1024)S(1)} %bitcast.206, f32[2048,3]{1,0:T(8,128)} %copy.28), kind=kCustom, calls=%fused_computation.23 | custom fusion | flops 6144 | bytes 81920 | tf_op jit(solution)/shard_map/scatter-add | solution.py:117
  1896.4 113.1 %gather_fusion.9 = f32[32768,3]{1,0:T(8,128)} fusion(f32[3,25992]{0,1:T(8,128)} %scatter_fusion.7, s32[32768]{0:T(1024)S(1)} %copy-done.12), kind=kCustom, calls=%fused_computation.11 | custom fusion | bytes 917504 | tf_op jit(solution)/shard_map/gather | solution.py:118
  (137 shorter events, 132.6 us)
Async XLA Ops:
  21.3 208.3 %copy-start.15 = (s32[1,32]{1,0:T(1,128)S(1)}, s32[1,32]{1,0:T(1,128)}, u32[]{:S(2)}) copy-start(s32[1,32]{1,0:T(1,128)} %param.31) | copy-start | bytes 388
  21.3 209.8 %copy-start.21 = (s32[1,8192]{1,0:T(1,128)S(1)}, s32[1,8192]{1,0:T(1,128)}, u32[]{:S(2)}) copy-start(s32[1,8192]{1,0:T(1,128)} %param.29) | copy-start | bytes 98308
  21.3 210.7 %copy-start.27 = (s32[2]{0:T(128)S(1)}, s32[2]{0:T(128)}, u32[]{:S(2)}) copy-start(s32[2]{0:T(128)} %constant.66) | copy-start | bytes 28
  21.3 210.8 %copy-start.26 = (s32[2]{0:T(128)S(1)}, s32[2]{0:T(128)}, u32[]{:S(2)}) copy-start(s32[2]{0:T(128)} %constant.69) | copy-start | bytes 28
  21.3 211.8 %copy-start = (f32[512,512]{1,0:T(8,128)S(1)}, f32[512,512]{1,0:T(8,128)}, u32[]{:S(2)}) copy-start(f32[512,512]{1,0:T(8,128)} %constant.15.clone) | copy-start | bytes 3145732
  21.3 211.8 %copy-start.9 = (f32[64,512]{1,0:T(8,128)S(1)}, f32[64,512]{1,0:T(8,128)}, u32[]{:S(2)}) copy-start(f32[64,512]{1,0:T(8,128)} %param.19) | copy-start | bytes 393220
  201.1 36.8 %copy-start.1 = (f32[512,512]{1,0:T(8,128)S(1)}, f32[512,512]{1,0:T(8,128)}, u32[]{:S(2)}) copy-start(f32[512,512]{1,0:T(8,128)} %constant.17.clone) | copy-start | bytes 3145732
  223.0 417.3 %collective-permute-start.4 = (f32[3,1,2048]{2,1,0:T(1,128)}, f32[3,1,2048]{2,1,0:T(1,128)}, u32[]{:S(2)}, u32[]{:S(2)}) collective-permute-start(f32[3,1,2048]{2,1,0:T(1,128)} %get-tuple-element.18), channel_id=1, source_target_pairs={{0,32},{32,64},{64,96},{96,128},{128,160},{160,192},{192,224},{224... | collective-permute-start | bytes 73736 | tf_op jit(solution)/shard_map/ppermute | solution.py:25
  225.5 416.9 %collective-permute-start.5 = (f32[3,1,2048]{2,1,0:T(1,128)}, f32[3,1,2048]{2,1,0:T(1,128)}, u32[]{:S(2)}, u32[]{:S(2)}) collective-permute-start(f32[3,1,2048]{2,1,0:T(1,128)} %get-tuple-element.17), channel_id=1, source_target_pairs={{32,0},{64,32},{96,64},{128,96},{160,128},{192,160},{224,192},{0,2... | collective-permute-start | bytes 73736 | tf_op jit(solution)/shard_map/ppermute | solution.py:27
  413.3 65.6 %copy-start.25 = (s32[8192]{0:T(1024)}, s32[8192]{0:T(1024)S(1)}, u32[]{:S(2)}) copy-start(s32[8192]{0:T(1024)S(1)} %get-tuple-element.67) | copy-start | bytes 98308
  413.3 45.6 %copy-start.22 = (s32[1,8192]{1,0:T(1,128)S(1)}, s32[1,8192]{1,0:T(1,128)}, u32[]{:S(2)}) copy-start(s32[1,8192]{1,0:T(1,128)} %param.29) | copy-start | bytes 98308
  413.3 45.6 %copy-start.23 = (s32[1,8192]{1,0:T(1,128)S(1)}, s32[1,8192]{1,0:T(1,128)}, u32[]{:S(2)}) copy-start(s32[1,8192]{1,0:T(1,128)} %param.28) | copy-start | bytes 98308
  478.9 85.0 %copy-start.17 = (f32[8192]{0:T(1024)}, f32[8192]{0:T(1024)S(1)}, u32[]{:S(2)}) copy-start(f32[8192]{0:T(1024)S(1)} %get-tuple-element.9) | copy-start | bytes 98308
  510.0 134.5 %all-to-all-start = ((f32[1,32,256]{2,0,1:T(1,128)}), f32[1,32,256]{2,0,1:T(1,128)}, u32[]{:S(2)}, u32[]{:S(2)}) async-start(f32[1,32,256]{2,0,1:T(1,128)} %bitcast.45), calls=%async_computation | async-start | bytes 65536 | tf_op jit(solution)/shard_map/all_to_all | solution.py:110
  518.1 44.7 %copy-start.14 = (s32[64,512]{1,0:T(8,128)S(1)}, s32[64,512]{1,0:T(8,128)}, u32[]{:S(2)}) copy-start(s32[64,512]{1,0:T(8,128)} %param.27) | copy-start | bytes 393220
  559.9 230.4 %collective-permute-start = (f32[1,1,2048]{2,1,0:T(1,128)}, f32[1,1,2048]{2,1,0:T(1,128)}, u32[]{:S(2)}, u32[]{:S(2)}) collective-permute-start(f32[1,1,2048]{2,1,0:T(1,128)} %get-tuple-element.25), channel_id=1, source_target_pairs={{0,32},{32,64},{64,96},{96,128},{128,160},{160,192},{192,224},{224... | collective-permute-start | bytes 24584 | tf_op jit(solution)/shard_map/ppermute | solution.py:25
  559.9 242.0 %collective-permute-start.1 = (f32[1,1,2048]{2,1,0:T(1,128)}, f32[1,1,2048]{2,1,0:T(1,128)}, u32[]{:S(2)}, u32[]{:S(2)}) collective-permute-start(f32[1,1,2048]{2,1,0:T(1,128)} %get-tuple-element.24), channel_id=1, source_target_pairs={{32,0},{64,32},{96,64},{128,96},{160,128},{192,160},{224,192},{0,2... | collective-permute-start | bytes 24584 | tf_op jit(solution)/shard_map/ppermute | solution.py:27
  563.1 251.0 %copy-start.11 = (s32[32768]{0:T(1024)}, s32[32768]{0:T(1024)S(1)}, u32[]{:S(2)}) copy-start(s32[32768]{0:T(1024)S(1)} %broadcast_clamp_fusion) | copy-start | bytes 393220
  1416.9 15.2 all-to-all-start.1
  1424.9 120.3 %collective-permute-start.2 = (f32[1,1,2048]{2,1,0:T(1,128)S(1)}, f32[1,1,2048]{2,1,0:T(1,128)S(1)}, u32[]{:S(2)}, u32[]{:S(2)}) collective-permute-start(f32[1,1,2048]{2,1,0:T(1,128)S(1)} %get-tuple-element.23), channel_id=1, source_target_pairs={{0,32},{32,64},{64,96},{96,128},{128,160},{160,192},{192,224},{224... | collective-permute-start | bytes 24584 | tf_op jit(solution)/shard_map/ppermute | solution.py:25
  1425.0 131.9 %collective-permute-start.3 = (f32[1,1,2048]{2,1,0:T(1,128)S(1)}, f32[1,1,2048]{2,1,0:T(1,128)S(1)}, u32[]{:S(2)}, u32[]{:S(2)}) collective-permute-start(f32[1,1,2048]{2,1,0:T(1,128)S(1)} %get-tuple-element.22), channel_id=1, source_target_pairs={{32,0},{64,32},{96,64},{128,96},{160,128},{192,160},{224,192},{0,2... | collective-permute-start | bytes 24584 | tf_op jit(solution)/shard_map/ppermute | solution.py:27
  1432.2 317.7 %all-to-all-start.2 = ((f32[3,32,256]{2,0,1:T(4,128)}), f32[3,32,256]{2,0,1:T(4,128)S(1)}, u32[]{:S(2)}, u32[]{:S(2)}) async-start(f32[3,32,256]{2,0,1:T(4,128)} %copy.24), calls=%async_computation.2 | async-start | bytes 262144 | tf_op jit(solution)/shard_map/all_to_all | solution.py:110
  1568.5 180.6 %copy-start.8 = (f32[64,512]{1,0:T(8,128)S(1)}, f32[64,512]{1,0:T(8,128)}, u32[]{:S(2)}) copy-start(f32[64,512]{1,0:T(8,128)} %param.21) | copy-start | bytes 393220
  1568.5 180.6 %copy-start.10 = (f32[64,512]{1,0:T(8,128)S(1)}, f32[64,512]{1,0:T(8,128)}, u32[]{:S(2)}) copy-start(f32[64,512]{1,0:T(8,128)} %param.19) | copy-start | bytes 393220
  (13 other events, 115.9 us)
where the time goes:
time: 2030 us; the launch traced here: 2020 us
  local copies, waits for them, and re-layouts  1060 us (52%)
  other arithmetic  900 us (44%)
  starting transfers between devices  32.1 us (2%)
  matrix products  27.2 us (1%)
    gather x3, local copies, waits for them, and re-layouts, gather_scatter(): return total[:, node_ids].reshape(stack.shape)  614 us
    scatter-add x3, other arithmetic, gather_scatter(): jax.ops.segment_sum(row, node_ids, num_segments=NODES)  522 us
    scatter-add x3, other arithmetic, gather_scatter(): total = local.at[:, node].add(received)  192 us
    gather x2, local copies, waits for them, and re-layouts, gather_scatter(): received = arrived[:, peer, slot] * valid  165 us
    gather x2, local copies, waits for them, and re-layouts, gather_scatter(): sent = local[:, node] * valid  91.1 us
    gather x6, local copies, waits for them, and re-layouts, gather_scatter(): rims = local[:, faces]  85.5 us
    unnamed x68, local copies, waits for them, and re-layouts  76.8 us
    unnamed x4, other arithmetic  73.2 us
  transfers between devices with their start and end apart: 9, of which 1 were waited for; matrix products, arithmetic and copies ran while one was open for 43% of the time, Pallas kernels for 0%

commit v1 on v0

v1 whole, which is shorter than its diff:
```python
import jax
import jax.numpy as jnp
import ml_dtypes
import numpy as np
from jax import lax
from jax.experimental import pallas as pl
from jax.experimental.pallas import tpu as pltpu
from jax.sharding import PartitionSpec as P

F32 = jnp.float32
BF16 = jnp.bfloat16
I32 = jnp.int32

VISCOSITY = 0.2
CHEB_THETA = 1.1
CHEB_DELTA = 0.9
RHO_FIRST = 9.0 / 11.0
RHO_NEXT = 99.0 / 161.0

HI = 208
VMEM_LIMIT = 48 * 1024 * 1024


def deriv_table():
    points = np.array(
        [
            -1.0,
            -0.8717401485096066,
            -0.5917001814331423,
            -0.2092992179024789,
            0.2092992179024789,
            0.5917001814331423,
            0.8717401485096066,
            1.0,
        ]
    )
    before = np.ones(8)
    legendre = points.copy()
    for degree in range(1, 7):
        after = ((2 * degree + 1) * points * legendre - degree * before) / (degree + 1)
        before = legendre
        legendre = after
    spread = points[:, None] - points[None, :]
    safe = np.where(spread == 0.0, 1.0, spread)
    deriv = legendre[:, None] / (legendre[None, :] * safe)
    deriv = np.where(spread == 0.0, 0.0, deriv)
    deriv[0, 0] = -14.0
    deriv[7, 7] = 14.0
    return deriv


def np_split(table):
    rest = table.astype(np.float32)
    parts = []
    for _ in range(3):
        part = rest.astype(ml_dtypes.bfloat16)
        parts.append(part)
        rest = rest - part.astype(np.float32)
    return parts


def const_tables():
    d32 = deriv_table().astype(np.float32)
    along_j = np.kron(np.eye(2), np.kron(d32, np.eye(8))).astype(np.float32)
    along_k = np.kron(np.eye(16), d32).astype(np.float32)
    fwd = np.concatenate([along_j.T, along_k.T], axis=1)
    bwd = np.concatenate([along_j, along_k], axis=0)
    fh, fm, fl = np_split(fwd)
    bh, bm, bl = np_split(bwd)
    tab_f = np.concatenate([fh, fh, fm, fm, fl, fh], axis=0)
    tab_b = np.concatenate([bh, bm, bl], axis=0)
    coef = np.zeros((64, 128), np.float32)
    for way, mat in enumerate((d32, d32.T)):
        for to in range(4):
            for src in range(4):
                for half in range(2):
                    lanes = slice(64 * half, 64 * half + 64)
                    row = way * 32 + (to * 4 + src) * 2
                    coef[row, lanes] = mat[2 * to + half, 2 * src + half]
                    coef[row + 1, lanes] = mat[2 * to + half, 2 * src + 1 - half]
    return tab_f, tab_b, coef


def iota(shape, dim):
    return lax.broadcasted_iota(I32, shape, dim)


def split(x, count):
    parts = []
    for at in range(count):
        part = x.astype(BF16)
        parts.append(part)
        if at + 1 < count:
            x = x - part.astype(F32)
    return parts


def dot(a, b):
    return lax.dot_general(a, b, (((1,), (0,)), ((), ())), preferred_element_type=F32)


def dot_nt(a, b):
    return lax.dot_general(a, b, (((1,), (1,)), ((), ())), preferred_element_type=F32)


def one_hot(row, count):
    return (iota((count, row.shape[1]), 0) == row).astype(F32).astype(BF16)


def chunks_of(x):
    return [x[:, 128 * c : 128 * c + 128] for c in range(4)]


def along_i(chunks, coef_ref, way):
    turned = [pltpu.roll(x, 64, 1) for x in chunks]
    out = []
    for to in range(4):
        total = None
        for src in range(4):
            row = way * 32 + (to * 4 + src) * 2
            term = coef_ref[row : row + 1, :] * chunks[src] + coef_ref[row + 1 : row + 2, :] * turned[src]
            total = term if total is None else total + term
        out.append(total)
    return out


def grads(chunks, tab_f_ref, coef_ref):
    rows = chunks[0].shape[0]
    g_i = along_i(chunks, coef_ref, 0)
    h, m, l = split(jnp.concatenate(chunks, axis=0), 3)
    hm = jnp.concatenate([h, m], axis=1)
    hl = jnp.concatenate([h, l], axis=1)
    g_jk = dot(hm, tab_f_ref[0:256, :]) + (dot(hm, tab_f_ref[256:512, :]) + dot(hl, tab_f_ref[512:768, :]))
    g_j = [g_jk[rows * c : rows * c + rows, 0:128] for c in range(4)]
    g_k = [g_jk[rows * c : rows * c + rows, 128:256] for c in range(4)]
    return g_i, g_j, g_k


def divergence(u_i, u_j, u_k, tab_b_ref, coef_ref):
    rows = u_i[0].shape[0]
    out_i = along_i(u_i, coef_ref, 1)
    u = jnp.concatenate([jnp.concatenate(u_j, axis=0), jnp.concatenate(u_k, axis=0)], axis=1)
    h, m, l = split(u, 3)
    b_h = tab_b_ref[0:256, :]
    b_m = tab_b_ref[256:512, :]
    b_l = tab_b_ref[512:768, :]
    wide = jnp.concatenate([b_h, b_m], axis=1)
    both = dot(h, wide) + dot(m, wide)
    small = dot(h, b_l) + dot(l, b_h)
    total = both[:, 0:128] + (both[:, 128:256] + small)
    return [out_i[c] + total[rows * c : rows * c + rows] for c in range(4)]


def tiled(x, times):
    return x if times == 1 else jnp.concatenate([x] * times, axis=0)


def laplace(chunks, geom_ref, tab_f_ref, tab_b_ref, coef_ref):
    g_i, g_j, g_k = grads(chunks, tab_f_ref, coef_ref)
    geom = [chunks_of(geom_ref[a]) for a in range(3)]
    return divergence(
        [geom[0][c] * g_i[c] for c in range(4)],
        [geom[1][c] * g_j[c] for c in range(4)],
        [geom[2][c] * g_k[c] for c in range(4)],
        tab_b_ref,
        coef_ref,
    )


def permute(perm, chunks):
    parts = split(jnp.concatenate(chunks, axis=1), 3)
    return chunks_of(dot(perm, jnp.concatenate(parts, axis=0)))


def assemble_local(w):
    lane = iota((64, 128), 1)
    row = iota((64, 128), 0)
    bx = row & 7
    jj = (lane >> 3) & 7
    w = list(w)
    low = pltpu.roll(pltpu.roll(w[0], 64, 1), 63, 0)
    high = pltpu.roll(pltpu.roll(w[3], 64, 1), 1, 0)
    w[3] = w[3] + jnp.where((lane >= 64) & (bx < 7), low, 0.0)
    w[0] = w[0] + jnp.where((lane < 64) & (bx > 0), high, 0.0)
    out = []
    zero = jnp.zeros((8, 128), F32)
    for x in w:
        nxt = jnp.concatenate([pltpu.roll(x[8:64], 56, 1), zero], axis=0)
        prv = jnp.concatenate([zero, pltpu.roll(x[0:56], 72, 1)], axis=0)
        out.append(x + jnp.where(jj == 7, nxt, 0.0) + jnp.where(jj == 0, prv, 0.0))
    return out


def pack_sides(w):
    lane1 = iota((1, 128), 1)
    rows = [
        jnp.where(lane1 < 64, w[0][8 * by : 8 * by + 1], w[3][8 * by + 7 : 8 * by + 8]) for by in range(8)
    ]
    x_side = jnp.concatenate(rows, axis=0)
    jj = (iota((8, 128), 1) >> 3) & 7
    y_side = jnp.zeros((8, 128), F32)
    for c in range(4):
        y_side = jnp.where(jj == 2 * c, pltpu.roll(w[c][0:8], 16 * c, 1), y_side)
        y_side = jnp.where(jj == 2 * c + 1, pltpu.roll(w[c][56:64], (16 * c - 48) % 128, 1), y_side)
    return jnp.concatenate([x_side, y_side], axis=0)


def pack_faces(w):
    kk = iota((64, 128), 1) & 7
    face = jnp.zeros((64, 128), F32)
    for c in range(4):
        face = jnp.where(kk == 2 * c, pltpu.roll(w[c], 2 * c, 1), face)
        face = jnp.where(kk == 2 * c + 1, pltpu.roll(w[c], (2 * c - 6) % 128, 1), face)
    return face


def add_back(w, side, face):
    lane = iota((64, 128), 1)
    sub = iota((64, 128), 0) & 7
    kk = lane & 7
    jj = (iota((8, 128), 1) >> 3) & 7
    x_rows = jnp.concatenate(
        [jnp.broadcast_to(side[by : by + 1], (8, 128)) for by in range(8)], axis=0
    )
    y_side = side[8:16]
    out = []
    for c in range(4):
        x = w[c]
        if c == 0:
            x = x + jnp.where((sub == 0) & (lane < 64), x_rows, 0.0)
        if c == 3:
            x = x + jnp.where((sub == 7) & (lane >= 64), x_rows, 0.0)
        x = x + jnp.where(kk == 0, pltpu.roll(face, (-2 * c) % 128, 1), 0.0)
        x = x + jnp.where(kk == 7, pltpu.roll(face, (6 - 2 * c) % 128, 1), 0.0)
        first = x[0:8] + jnp.where(jj == 0, pltpu.roll(y_side, (-16 * c) % 128, 1), 0.0)
        last = x[56:64] + jnp.where(jj == 7, pltpu.roll(y_side, (48 - 16 * c) % 128, 1), 0.0)
        out.append(jnp.concatenate([first, x[8:56], last], axis=0))
    return out


def block_row(block):
    return jnp.concatenate([block[t : t + 1] for t in range(8)], axis=1)


def gather_tables(tables, idx_block, hi_count):
    row = block_row(idx_block)
    lows = one_hot(row & 127, 128)
    parts = []
    for table in tables:
        parts += split(table, 2)
    got = dot(jnp.concatenate(parts, axis=0), lows)
    mask = iota((hi_count, 1024), 0) == (row >> 7)
    out = []
    for at in range(len(tables)):
        both = got[2 * at * hi_count : (2 * at + 1) * hi_count] + got[(2 * at + 1) * hi_count : (2 * at + 2) * hi_count]
        out.append(jnp.sum(jnp.where(mask, both, 0.0), axis=0, keepdims=True))
    return out


def scatter_tables(rows, idx_block, hi_count):
    row = block_row(idx_block)
    lows = one_hot(row & 127, 128)
    mask = iota((hi_count, 1024), 0) == (row >> 7)
    parts = []
    for values in rows:
        for part in split(values, 2):
            spread = jnp.broadcast_to(part.astype(F32), (hi_count, 1024))
            parts.append(jnp.where(mask, spread, 0.0).astype(BF16))
    return dot_nt(jnp.concatenate(parts, axis=0), lows)


def send_values(local_fields, sidx_ref, fidx_ref, msg_ref, up_ref, down_ref, base, stride, face_base):
    sides = [pack_sides(w) for w in local_fields]
    faces = [pack_faces(w) for w in local_fields]
    for g in range(8):
        got = gather_tables(sides, sidx_ref[8 * g : 8 * g + 8, :], 16)
        for f, values in enumerate(got):
            for t in range(8):
                peer, half = (8 * g + t) // 2, t % 2
                at = peer * stride + base + 2 * f + half
                msg_ref[at : at + 1, :] = values[:, 128 * t : 128 * t + 128]
    for g in range(4):
        got = gather_tables(faces, fidx_ref[8 * g : 8 * g + 8, :], 64)
        out_ref = down_ref if g < 2 else up_ref
        for f, values in enumerate(got):
            for t in range(8):
                at = face_base + 16 * f + 8 * (g % 2) + t
                out_ref[at : at + 1, :] = values[:, 128 * t : 128 * t + 128]


def take_values(count, sidx_ref, fidx_ref, msg_ref, low_refs, upp_refs, stride):
    side = None
    for g in range(8):
        rows = []
        for f in range(count):
            cells = []
            for t in range(8):
                at = (8 * g + t) // 2 * stride + 2 * f + t % 2
                cells.append(msg_ref[at : at + 1, :])
            rows.append(jnp.concatenate(cells, axis=1))
        part = scatter_tables(rows, sidx_ref[8 * g : 8 * g + 8, :], 16)
        side = part if side is None else side + part
    face = None
    for g in range(4):
        refs = low_refs if g < 2 else upp_refs
        rows = [block_row(refs[f][0][refs[f][1] + 8 * (g % 2) : refs[f][1] + 8 * (g % 2) + 8, :]) for f in range(count)]
        part = scatter_tables(rows, fidx_ref[8 * g : 8 * g + 8, :], 64)
        face = part if face is None else face + part
    sides = [side[32 * f : 32 * f + 16] + side[32 * f + 16 : 32 * f + 32] for f in range(count)]
    faces = [face[128 * f : 128 * f + 64] + face[128 * f + 64 : 128 * f + 128] for f in range(count)]
    return sides, faces


def chain_place(left):
    eye = (iota((64, 64), 0) == iota((64, 64), 1)).astype(F32)
    l1 = left.astype(BF16)
    l2 = dot(l1, l1)
    m1 = eye + left
    l2b = l2.astype(BF16)
    l4 = dot(l2b, l2b)
    m2 = m1 + dot(l2b, m1.astype(BF16))
    m4 = m2 + dot(l4.astype(BF16), m2.astype(BF16))
    return jnp.sum(m4, axis=1, keepdims=True) - 1.0


def brick_places(conn):
    same = iota((64, 64), 0) == iota((64, 64), 1)

    def as_row(col):
        return jnp.sum(jnp.where(same, col, 0), axis=0, keepdims=True)

    end_x = as_row(conn[:, 475:476])
    end_y = as_row(conn[:, 251:252])
    left_x = (conn[:, 27:28] == end_x).astype(F32)
    left_y = (conn[:, 195:196] == end_y).astype(F32)
    return (chain_place(left_y) * 8.0 + chain_place(left_x)).astype(I32)


def place_table(hi_ref, lo_ref, acc_ref, blocks, hi_count):
    lane = (iota((1, 128), 1)).astype(F32)
    acc_ref[...] = jnp.zeros((HI, 256), F32)

    def step(g, carry):
        hi_block = hi_ref[pl.ds(pl.multiple_of(8 * g, 8), 8), :]
        lo_block = lo_ref[pl.ds(pl.multiple_of(8 * g, 8), 8), :]
        top = one_hot(block_row(hi_block), HI)
        low, high = [], []
        for t in range(8):
            hit = iota((128, 128), 0) == lo_block[t : t + 1]
            base = ((8 * g + t) * 128).astype(F32)
            low.append(jnp.where(hit, jnp.broadcast_to(lane, (128, 128)), 0.0).astype(BF16))
            high.append(jnp.where(hit, base, 0.0).astype(BF16))
        both = jnp.concatenate([jnp.concatenate(low, axis=1), jnp.concatenate(high, axis=1)], axis=0)
        acc_ref[...] += dot_nt(top, both)
        return carry

    lax.fori_loop(0, blocks, step, 0)


def look_up(table, row):
    low = one_hot(row & 127, 128)
    got = dot(table, jnp.concatenate([low, low], axis=0))
    mask = iota((HI, row.shape[1]), 0) == (row >> 7)
    return jnp.sum(jnp.where(mask, got, 0.0), axis=0, keepdims=True)


def tables_body(conn_ref, peer_ref, slot_ref, node_ref, counts_ref, axial_ref, sidx_ref, fidx_ref, perm_ref, back_ref, scratch):
    acc_s, acc_f, s_hi, s_lo, f_hi, f_lo, nodes = scratch
    conn = conn_ref[...]
    place = brick_places(conn)
    lane3 = iota((64, 192), 1) & 63
    place_row = jnp.sum(jnp.where(lane3 == iota((64, 192), 0), place, 0), axis=0, keepdims=True)
    perm_ref[...] = (iota((64, 192), 0) == place_row).astype(F32).astype(BF16)
    back_ref[...] = (lane3 == place).astype(F32).astype(BF16)
    perm = perm_ref[:, 0:64]

    ids = jnp.concatenate([(conn >> 7).astype(F32), (conn & 127).astype(F32)], axis=1).astype(BF16)
    ids = dot(perm, ids)
    hi_c = chunks_of(ids[:, 0:512])
    lo_c = chunks_of(ids[:, 512:1024])
    lane8 = iota((8, 128), 1)
    row8 = iota((8, 128), 0)
    keep_x = (((lane8 >> 3) & 7) < 7) | (row8 == 7)
    i_y = 2 * (((lane8 >> 3) & 7) >> 1) + (lane8 >> 6)
    keep_y = (i_y < 7) & ((row8 > 0) | (i_y > 0))
    lane = iota((64, 128), 1)
    row = iota((64, 128), 0)
    i_f = 2 * ((lane & 7) >> 1) + (lane >> 6)
    keep_f = ((i_f < 7) | ((row & 7) == 7)) & ((((lane >> 3) & 7) < 7) | ((row >> 3) == 7))
    side_hi = pack_sides(hi_c)
    s_hi[0:8, :] = jnp.where(keep_x, side_hi[0:8], -1.0).astype(I32)
    s_hi[8:16, :] = jnp.where(keep_y, side_hi[8:16], -1.0).astype(I32)
    s_lo[...] = pack_sides(lo_c).astype(I32)
    f_hi[...] = jnp.where(keep_f, pack_faces(hi_c), -1.0).astype(I32)
    f_lo[...] = pack_faces(lo_c).astype(I32)
    place_table(s_hi, s_lo, acc_s, 2, 16)
    place_table(f_hi, f_lo, acc_f, 8, 64)

    nodes[...] = jnp.zeros((128, 128), F32)

    def invert(g, carry):
        at = pl.ds(pl.multiple_of(1024 * g, 1024), 1024)
        peer = peer_ref[:, at]
        slot = slot_ref[:, at]
        node = node_ref[:, at]
        hit = iota((64, 1024), 0) == (peer * 2 + (slot >> 7))
        first = jnp.where(hit, (node >> 7).astype(F32), 0.0).astype(BF16)
        second = jnp.where(hit, (node & 127).astype(F32), 0.0).astype(BF16)
        nodes[...] += dot_nt(jnp.concatenate([first, second], axis=0), one_hot(slot & 127, 128))
        return carry

    lax.fori_loop(0, 8, invert, 0)
    ordered = (nodes[0:64, :] * 128.0 + nodes[64:128, :]).astype(I32)
    table_s = acc_s[...].astype(BF16)
    for g in range(8):
        places = look_up(table_s, block_row(ordered[8 * g : 8 * g + 8]))
        for t in range(8):
            sidx_ref[8 * g + t : 8 * g + t + 1, :] = places[:, 128 * t : 128 * t + 128].astype(I32)
    table_f = acc_f[...].astype(BF16)
    for g in range(4):
        cells = axial_ref[g // 2 : g // 2 + 1, 1024 * (g % 2) : 1024 * (g % 2) + 1024]
        places = look_up(table_f, cells)
        for t in range(8):
            fidx_ref[8 * g + t : 8 * g + t + 1, :] = places[:, 128 * t : 128 * t + 128].astype(I32)
    limit = jnp.sum(
        jnp.where(iota((64, 32), 1) == (iota((64, 32), 0) >> 1), counts_ref[...], 0), axis=1, keepdims=True
    )
    slots = (iota((64, 128), 0) & 1) * 128 + iota((64, 128), 1)
    sidx_ref[...] = jnp.where(slots < limit, sidx_ref[...], -1)


def first_kernel(
    conn_ref, peer_ref, slot_ref, node_ref, counts_ref, axial_ref, pressure_ref, geom_ref, tab_f_ref, tab_b_ref, coef_ref,
    msg_ref, up_ref, down_ref, w_ref, sidx_ref, fidx_ref, perm_ref, back_ref, *scratch,
):
    tables_body(
        conn_ref, peer_ref, slot_ref, node_ref, counts_ref, axial_ref, sidx_ref, fidx_ref, perm_ref, back_ref, scratch
    )
    out = laplace(chunks_of(pressure_ref[...]), geom_ref, tab_f_ref, tab_b_ref, coef_ref)
    w = permute(perm_ref[...], out)
    for c in range(4):
        w_ref[:, 128 * c : 128 * c + 128] = w[c]
    send_values([assemble_local(w)], sidx_ref, fidx_ref, msg_ref, up_ref, down_ref, 0, 2, 0)


def momentum_kernel(
    velocity_ref, force_ref, mass_ref, metric_ref, geom_ref, tab_f_ref, tab_b_ref, coef_ref, perm_ref, sidx_ref, fidx_ref,
    msg_ref, up_ref, down_ref, w_ref,
):
    parts = [chunks_of(velocity_ref[a]) for a in range(3)]
    stacked = [jnp.concatenate([parts[a][c] for a in range(3)], axis=0) for c in range(4)]
    grad = grads(stacked, tab_f_ref, coef_ref)
    same = iota((64, 64), 0) == iota((64, 64), 1)
    scale = [jnp.sum(jnp.where(same, metric_ref[a : a + 1, :], 0.0), axis=1, keepdims=True) for a in range(3)]
    convect = []
    flux = [[], [], []]
    for c in range(4):
        total = None
        for a in range(3):
            speed = tiled(scale[a] * parts[a][c], 3)
            term = speed * grad[a][c]
            total = term if total is None else total + term
            flux[a].append(tiled(geom_ref[a, :, 128 * c : 128 * c + 128], 3) * grad[a][c])
        convect.append(total)
    diffuse = divergence(flux[0], flux[1], flux[2], tab_b_ref, coef_ref)
    fields = []
    for f in range(3):
        rows = slice(64 * f, 64 * f + 64)
        out = []
        for c in range(4):
            lanes = slice(128 * c, 128 * c + 128)
            out.append(
                mass_ref[:, lanes] * (force_ref[f, :, lanes] - convect[c][rows]) - VISCOSITY * diffuse[c][rows]
            )
        w = permute(perm_ref[...], out)
        for c in range(4):
            w_ref[f, :, 128 * c : 128 * c + 128] = w[c]
        fields.append(assemble_local(w))
    send_values(fields, sidx_ref, fidx_ref, msg_ref, up_ref, down_ref, 0, 6, 0)


def second_kernel(
    msg_in_ref, low_ref, upp_ref, w_in_ref, pressure_ref, rhs_ref, jacobi_ref, geom_ref, tab_f_ref, tab_b_ref, coef_ref,
    perm_ref, back_ref, sidx_ref, fidx_ref, msg_m_ref, up_m_ref, down_m_ref,
    msg_ref, up_ref, down_ref, w_ref, base_ref, res_ref,
):
    sides, faces = take_values(1, sidx_ref, fidx_ref, msg_in_ref, [(low_ref, 0)], [(upp_ref, 0)], 2)
    w = add_back(chunks_of(w_in_ref[...]), sides[0], faces[0])
    applied = permute(back_ref[...], assemble_local(w))
    step = []
    for c in range(4):
        lanes = slice(128 * c, 128 * c + 128)
        jac = jacobi_ref[:, lanes]
        res = rhs_ref[:, lanes] - applied[c]
        step.append(jac * res / CHEB_THETA)
        first = pressure_ref[:, lanes] + step[c]
        base_ref[:, lanes] = first + RHO_NEXT * RHO_FIRST * step[c]
        res_ref[:, lanes] = res
    out = laplace(step, geom_ref, tab_f_ref, tab_b_ref, coef_ref)
    w = permute(perm_ref[...], out)
    for c in range(4):
        w_ref[:, 128 * c : 128 * c + 128] = w[c]
    send_values([assemble_local(w)], sidx_ref, fidx_ref, msg_ref, up_ref, down_ref, 0, 8, 0)
    for peer in range(32):
        msg_ref[8 * peer + 2 : 8 * peer + 8, :] = msg_m_ref[6 * peer : 6 * peer + 6, :]
    up_ref[16:64, :] = up_m_ref[...]
    down_ref[16:64, :] = down_m_ref[...]


def last_kernel(
    msg_in_ref, low_ref, upp_ref, w_in_ref, w_m_ref, jacobi_ref, base_ref, res_ref, back_ref, sidx_ref, fidx_ref,
    pressure_ref, momentum_ref,
):
    low = [(low_ref, 16 * f) for f in range(4)]
    upp = [(upp_ref, 16 * f) for f in range(4)]
    sides, faces = take_values(4, sidx_ref, fidx_ref, msg_in_ref, low, upp, 8)
    for f in range(4):
        held = w_in_ref[...] if f == 0 else w_m_ref[f - 1]
        w = add_back(chunks_of(held), sides[f], faces[f])
        applied = permute(back_ref[...], assemble_local(w))
        for c in range(4):
            lanes = slice(128 * c, 128 * c + 128)
            if f == 0:
                pressure_ref[:, lanes] = base_ref[:, lanes] + 2.0 * RHO_NEXT / CHEB_DELTA * jacobi_ref[:, lanes] * (
                    res_ref[:, lanes] - applied[c]
                )
            else:
                momentum_ref[f - 1, :, lanes] = applied[c]


def shape(*dims, dtype=F32):
    return jax.ShapeDtypeStruct(dims, dtype)


def call(kernel, outs, args, scratch=(), name=None):
    vmem = pl.BlockSpec(memory_space=pltpu.VMEM)
    return pl.pallas_call(
        kernel,
        out_shape=outs,
        in_specs=[vmem] * len(args),
        out_specs=[vmem] * len(outs),
        scratch_shapes=list(scratch),
        compiler_params=pltpu.CompilerParams(vmem_limit_bytes=VMEM_LIMIT),
        name=name,
    )(*args)


def consts():
    return [jnp.asarray(t) for t in const_tables()]


def run_first(conn, peer, slot, node, counts, axial, pressure, geom):
    return call(
        first_kernel,
        [shape(64, 128), shape(16, 128), shape(16, 128), shape(64, 512), shape(64, 128, dtype=I32),
         shape(32, 128, dtype=I32), shape(64, 192, dtype=BF16), shape(64, 192, dtype=BF16)],
        [conn, peer, slot, node, counts, axial, pressure, geom, *consts()],
        [pltpu.VMEM((HI, 256), F32), pltpu.VMEM((HI, 256), F32), pltpu.VMEM((16, 128), I32), pltpu.VMEM((16, 128), I32),
         pltpu.VMEM((64, 128), I32), pltpu.VMEM((64, 128), I32), pltpu.VMEM((128, 128), F32)],
        "first",
    )


def run_momentum(velocity, force, mass, metric, geom, perm, sidx, fidx):
    return call(
        momentum_kernel,
        [shape(192, 128), shape(48, 128), shape(48, 128), shape(3, 64, 512)],
        [velocity, force, mass, metric, geom, *consts(), perm, sidx, fidx],
        name="momentum",
    )


def run_second(msg, low, upp, w, pressure, rhs, jacobi, geom, perm, back, sidx, fidx, msg_m, up_m, down_m):
    return call(
        second_kernel,
        [shape(256, 128), shape(64, 128), shape(64, 128), shape(64, 512), shape(64, 512), shape(64, 512)],
        [msg, low, upp, w, pressure, rhs, jacobi, geom, *consts(), perm, back, sidx, fidx, msg_m, up_m, down_m],
        name="second",
    )


def run_last(msg, low, upp, w, w_m, jacobi, base, res, back, sidx, fidx):
    return call(
        last_kernel,
        [shape(64, 512), shape(3, 64, 512)],
        [msg, low, upp, w, w_m, jacobi, base, res, back, sidx, fidx],
        name="last",
    )


def exchange(msg, up, down):
    rows = msg.shape[0] // 32
    arrived = lax.all_to_all(msg.reshape(32, rows, 128), ("gy", "gz"), split_axis=0, concat_axis=0, tiled=True)
    count = lax.axis_size("gx")
    from_low = lax.ppermute(up, "gx", [(i, (i + 1) % count) for i in range(count)])
    from_upp = lax.ppermute(down, "gx", [((i + 1) % count, i) for i in range(count)])
    return arrived.reshape(32 * rows, 128), from_low, from_upp


def on_device(
    pressure, rhs, jacobi, geom, velocity, force, mass, metric, conn, ent_peer, ent_slot, ent_node, counts, axial_nodes
):
    msg, up, down, w, sidx, fidx, perm, back = run_first(
        conn, ent_peer, ent_slot, ent_node, counts, axial_nodes[0], pressure, geom
    )
    got = exchange(msg, up, down)
    msg_m, up_m, down_m, w_m = run_momentum(velocity, force, mass, metric, geom, perm, sidx, fidx)
    msg, up, down, w, base, res = run_second(
        *got, w, pressure, rhs, jacobi, geom, perm, back, sidx, fidx, msg_m, up_m, down_m
    )
    got = exchange(msg, up, down)
    return tuple(run_last(*got, w, w_m, jacobi, base, res, back, sidx, fidx))


def solution(mesh):
    both = P(("gx", "gy", "gz"), None)
    three = P(None, ("gx", "gy", "gz"), None)
    return jax.shard_map(
        on_device,
        mesh=mesh,
        in_specs=(
            both, both, both, three, three, three, both, P(None, ("gx", "gy", "gz")), both, both, both, both, both,
            P(("gx", "gy", "gz"), None, None),
        ),
        out_specs=(both, three),
        check_vma=False,
    )
```

time: 2030 us -> 67 us (0.03)
  local copies, waits for them, and re-layouts: 1060 us -> 11.7 us
  other arithmetic: 900 us -> 0 us
  matrix products: 27.2 us -> 0 us
  Pallas kernels: 0 us -> 23.7 us
    gather x15 -> x0, local copies, waits for them, and re-layouts: 957 us -> none  [the longest x3 614 us: gather_scatter(): return total[:, node_ids].reshape(stack.shape)]
    scatter-add x12 -> x0, other arithmetic: 801 us -> none  [the longest x3 522 us: gather_scatter(): jax.ops.segment_sum(row, node_ids, num_segments=NODES)]
    unnamed x4 -> x0, other arithmetic: 73.2 us -> none
    unnamed x68 -> x44, local copies, waits for them, and re-layouts: 76.8 us -> 11.7 us
    dot_general x18 -> x0, matrix products: 27.2 us -> none  [the longest x9 19.9 us: forward(): return jnp.matmul(field, table.T, precision=lax.Precision.HIGHEST)]
    pallas_call x0 -> x4, Pallas kernels: none -> 23.7 us  [call(): pl.pallas_call(kernel, out_shape=outs, in_specs=[vmem] * len(args), out_s...]
  transfers between devices with their start and end apart: 9 -> 6, of which waited for: 1 -> 2; matrix products, arithmetic and copies ran while one was open for 43% -> 0% of each run, Pallas kernels for 0% -> 6%
where the time goes in v1:
time: 67 us; the launch traced here: 66.1 us
  starting transfers between devices  25.1 us (37%)
  Pallas kernels  23.7 us (35%)
  local copies, waits for them, and re-layouts  11.7 us (17%)
  waiting for transfers between devices  4.95 us (7%)
  between operations  0.77 us (1%)
    pallas_call x4, Pallas kernels, call(): pl.pallas_call(kernel, out_shape=outs, in_specs=[vmem] * len(args), out_s...  23.7 us
    all_to_all x2, starting transfers between devices, exchange(): lax.all_to_all(msg.reshape(32, rows, 128), ('gy', 'gz'), split_axis=0, co...  16.4 us
    unnamed x44, local copies, waits for them, and re-layouts  11.7 us
    ppermute x2, starting transfers between devices, exchange(): lax.ppermute(down, 'gx', [((i + 1) % count, i) for i in range(count)])  6.87 us
    all_to_all x2, waiting for transfers between devices, exchange(): lax.all_to_all(msg.reshape(32, rows, 128), ('gy', 'gz'), split_axis=0, co...  3.35 us
    ppermute x2, starting transfers between devices, exchange(): lax.ppermute(up, 'gx', [(i, (i + 1) % count) for i in range(count)])  1.79 us
    ppermute x2, waiting for transfers between devices, exchange(): lax.ppermute(up, 'gx', [(i, (i + 1) % count) for i in range(count)])  1.6 us
  transfers between devices with their start and end apart: 6, of which 2 were waited for; matrix products, arithmetic and copies ran while one was open for 0% of the time, Pallas kernels for 6%

profile of v1, /device:TPU:1, one launch (start us, length us, event | category | flops | bytes accessed | tf_op | source)
XLA Modules:
  0.0 66.1 jit_solution(6840359543015411188)
XLA Ops:
  1.3 1.0 %copy-done = f32[3,64,512]{2,1,0:T(8,128)S(1)} copy-done((f32[3,64,512]{2,1,0:T(8,128)S(1)}, f32[3,64,512]{2,1,0:T(8,128)}, u32[]{:S(2)}) %copy-start) | copy-done | bytes 393240
  2.3 1.0 %copy-done.2 = bf16[768,256]{1,0:T(8,128)(2,1)S(1)} copy-done((bf16[768,256]{1,0:T(8,128)(2,1)S(1)}, bf16[768,256]{1,0:T(8,128)(2,1)}, u32[]{:S(2)}) %copy-start.2) | copy-done | bytes 393240
  3.3 0.9 %copy-done.4 = bf16[768,128]{1,0:T(8,128)(2,1)S(1)} copy-done((bf16[768,128]{1,0:T(8,128)(2,1)S(1)}, bf16[768,128]{1,0:T(8,128)(2,1)}, u32[]{:S(2)}) %copy-start.4) | copy-done | bytes 196632
  4.2 0.9 %copy-done.6 = f32[64,512]{1,0:T(8,128)S(1)} copy-done((f32[64,512]{1,0:T(8,128)S(1)}, f32[64,512]{1,0:T(8,128)}, u32[]{:S(2)}) %copy-start.6) | copy-done | bytes 131096
  5.1 0.8 %copy-done.11 = f32[64,128]{1,0:T(8,128)S(1)} copy-done((f32[64,128]{1,0:T(8,128)S(1)}, f32[64,128]{1,0:T(8,128)}, u32[]{:S(2)}) %copy-start.11) | copy-done | bytes 32792
  5.9 0.9 %copy-done.14 = s32[64,512]{1,0:T(8,128)S(1)} copy-done((s32[64,512]{1,0:T(8,128)S(1)}, s32[64,512]{1,0:T(8,128)}, u32[]{:S(2)}) %copy-start.14) | copy-done | bytes 131096
  6.8 0.8 %copy-done.16 = s32[1,8192]{1,0:T(1,128)S(1)} copy-done((s32[1,8192]{1,0:T(1,128)S(1)}, s32[1,8192]{1,0:T(1,128)}, u32[]{:S(2)}) %copy-start.16) | copy-done | bytes 32792
  7.5 0.8 %copy-done.17 = s32[1,8192]{1,0:T(1,128)S(1)} copy-done((s32[1,8192]{1,0:T(1,128)S(1)}, s32[1,8192]{1,0:T(1,128)}, u32[]{:S(2)}) %copy-start.17) | copy-done | bytes 32792
  8.3 0.8 %copy-done.18 = s32[1,8192]{1,0:T(1,128)S(1)} copy-done((s32[1,8192]{1,0:T(1,128)S(1)}, s32[1,8192]{1,0:T(1,128)}, u32[]{:S(2)}) %copy-start.18) | copy-done | bytes 32792
  9.1 0.7 %copy-done.19 = s32[1,2,2048]{2,1,0:T(2,128)S(1)} copy-done((s32[1,2,2048]{2,1,0:T(2,128)S(1)}, s32[1,2,2048]{2,1,0:T(2,128)}, u32[]{:S(2)}) %copy-start.19) | copy-done | bytes 16408
  9.8 11.6 %first.1 = (f32[64,128]{1,0:T(8,128)}, f32[16,128]{1,0:T(8,128)S(1)}, f32[16,128]{1,0:T(8,128)S(1)}, f32[64,512]{1,0:T(8,128)S(1)}, s32[64,128]{1,0:T(8,128)S(1)...) custom-call(s32[64,512]{1,0:T(8,128)S(1)} %copy-done.14, ...), custom_call_target="tpu_custom_call" | custom-call | tf_op jit(solution)/shard_map/first/pallas_call | solution.py:537
  21.4 8.7 %all-to-all-start = ((f32[32,2,128]{2,1,0:T(2,128)}), f32[32,2,128]{2,1,0:T(2,128)S(1)}, u32[]{:S(2)}, u32[]{:S(2)}) async-start(f32[32,2,128]{2,1,0:T(2,128)} %bitcast.1), calls=%async_computation | async-start | bytes 65536 | tf_op jit(solution)/shard_map/all_to_all | solution.py:593
  30.1 1.7 %collective-permute-start = (f32[16,128]{1,0:T(8,128)S(1)}, f32[16,128]{1,0:T(8,128)S(1)}, u32[]{:S(2)}, u32[]{:S(2)}) collective-permute-start(f32[16,128]{1,0:T(8,128)S(1)} %get-tuple-element.21), channel_id=1, source_target_pairs={{0,32},{32,64},{64,96},{96,128},{128,160},{160,192},{192,224},{224... | collective-permute-start | bytes 24584 | tf_op jit(solution)/shard_map/ppermute | solution.py:595
  31.9 4.2 %collective-permute-start.1 = (f32[16,128]{1,0:T(8,128)S(1)}, f32[16,128]{1,0:T(8,128)S(1)}, u32[]{:S(2)}, u32[]{:S(2)}) collective-permute-start(f32[16,128]{1,0:T(8,128)S(1)} %get-tuple-element.22), channel_id=1, source_target_pairs={{32,0},{64,32},{96,64},{128,96},{160,128},{192,160},{224,192},{0,2... | collective-permute-start | bytes 24584 | tf_op jit(solution)/shard_map/ppermute | solution.py:596
  36.1 0.6 copy-done.20
  36.7 1.0 %copy-done.10 = f32[3,64,512]{2,1,0:T(8,128)S(1)} copy-done((f32[3,64,512]{2,1,0:T(8,128)S(1)}, f32[3,64,512]{2,1,0:T(8,128)}, u32[]{:S(2)}) %copy-start.10) | copy-done | bytes 393240
  37.7 0.9 %copy-done.15 = f32[64,512]{1,0:T(8,128)S(1)} copy-done((f32[64,512]{1,0:T(8,128)S(1)}, f32[64,512]{1,0:T(8,128)}, u32[]{:S(2)}) %copy-start.15) | copy-done | bytes 131096
  38.7 3.9 %momentum.1 = (f32[192,128]{1,0:T(8,128)S(1)}, f32[48,128]{1,0:T(8,128)S(1)}, f32[48,128]{1,0:T(8,128)S(1)}, f32[3,64,512]{2,1,0:T(8,128)S(1)}) custom-call(f32[3,64,512]{2,1,0:T(8,128)S(1)} %copy-done.9, f32[3,64,512]{2,1,0:T(8,128)S(1)} %copy-done.10, f32[64,512]{1,0:T(8,128)S(1)} %copy-done.15, f32[3,64]{1,0:T(4,128)S(1)} %copy-done.20, ...), custom_call_target="tpu_custom_call" | custom-call | tf_op jit(solution)/shard_map/momentum/pallas_call | solution.py:537
  42.6 4.6 %second.1 = (f32[256,128]{1,0:T(8,128)}, f32[64,128]{1,0:T(8,128)S(1)}, f32[64,128]{1,0:T(8,128)S(1)}, f32[64,512]{1,0:T(8,128)S(1)}, f32[64,512]{1,0:T(8,128)S(1)}, /*index=5*/f32[64,512]{1,0:T(8,128)S(1)}) custom-call(f32[64,128]{1,0:T(8,128)S(1)} %bitcast.6, f32[16,128]{1,0:T(8,128)S(1)} %collective-permute-done.low_ref, ...), custom_call_target="tpu_custom_call" | custom-call | tf_op jit(solution)/shard_map/second/pallas_call | solution.py:537
  47.3 7.7 %all-to-all-start.1 = ((f32[32,8,128]{2,1,0:T(8,128)}), f32[32,8,128]{2,1,0:T(8,128)S(1)}, u32[]{:S(2)}, u32[]{:S(2)}) async-start(f32[32,8,128]{2,1,0:T(8,128)} %bitcast.3), calls=%async_computation.1 | async-start | bytes 262144 | tf_op jit(solution)/shard_map/all_to_all | solution.py:593
  55.0 2.7 %collective-permute-start.3 = (f32[64,128]{1,0:T(8,128)S(1)}, f32[64,128]{1,0:T(8,128)S(1)}, u32[]{:S(2)}, u32[]{:S(2)}) collective-permute-start(f32[64,128]{1,0:T(8,128)S(1)} %get-tuple-element.33), channel_id=1, source_target_pairs={{32,0},{64,32},{96,64},{128,96},{160,128},{192,160},{224,192},{0,2... | collective-permute-start | bytes 98312 | tf_op jit(solution)/shard_map/ppermute | solution.py:596
  57.7 1.6 %collective-permute-done.2.low_ref = f32[64,128]{1,0:T(8,128)S(1)} collective-permute-done((f32[64,128]{1,0:T(8,128)S(1)}, f32[64,128]{1,0:T(8,128)S(1)}, u32[]{:S(2)}, u32[]{:S(2)}) %collective-permute-start.2) | collective-permute-done | bytes 32800 | tf_op jit(solution)/shard_map/ppermute | solution.py:595
  59.3 3.4 %all-to-all-done.1 = f32[32,8,128]{2,1,0:T(8,128)S(1)} async-done(((f32[32,8,128]{2,1,0:T(8,128)}), f32[32,8,128]{2,1,0:T(8,128)S(1)}, u32[]{:S(2)}, u32[]{:S(2)}) %all-to-all-start.1) | async-done | bytes 131104 | tf_op jit(solution)/shard_map/all_to_all | solution.py:593
  62.6 3.5 %last.1 = (f32[64,512]{1,0:T(8,128)}, f32[3,64,512]{2,1,0:T(8,128)}) custom-call(f32[256,128]{1,0:T(8,128)S(1)} %bitcast.5, f32[64,128]{1,0:T(8,128)S(1)} %collective-permute-done.2.low_ref, f32[64,128]{1,0:T(8,128)S(1)} %collective-permute-done.3.upp_ref, f32[64,512]{1,0:T(8,128)S(1)} %get-tuple-element.34.w_in_ref, ...), custom_call_target="tpu_custom_call" | custom-call | tf_op jit(solution)/shard_map/last/pallas_call | solution.py:537
  (36 shorter events, 0.8 us)
Async XLA Ops:
  1.3 1.0 %copy-start = (f32[3,64,512]{2,1,0:T(8,128)S(1)}, f32[3,64,512]{2,1,0:T(8,128)}, u32[]{:S(2)}) copy-start(f32[3,64,512]{2,1,0:T(8,128)} %geom_ref.5) | copy-start | bytes 1179652
  2.3 1.0 %copy-start.2 = (bf16[768,256]{1,0:T(8,128)(2,1)S(1)}, bf16[768,256]{1,0:T(8,128)(2,1)}, u32[]{:S(2)}) copy-start(bf16[768,256]{1,0:T(8,128)(2,1)} %constant.6.clone.tab_f_ref) | copy-start | bytes 1179652
  3.3 0.9 %copy-start.4 = (bf16[768,128]{1,0:T(8,128)(2,1)S(1)}, bf16[768,128]{1,0:T(8,128)(2,1)}, u32[]{:S(2)}) copy-start(bf16[768,128]{1,0:T(8,128)(2,1)} %constant.7.clone.tab_b_ref) | copy-start | bytes 589828
  4.2 0.9 %copy-start.6 = (f32[64,512]{1,0:T(8,128)S(1)}, f32[64,512]{1,0:T(8,128)}, u32[]{:S(2)}) copy-start(f32[64,512]{1,0:T(8,128)} %pressure_ref.3) | copy-start | bytes 393220
  5.1 0.8 %copy-start.11 = (f32[64,128]{1,0:T(8,128)S(1)}, f32[64,128]{1,0:T(8,128)}, u32[]{:S(2)}) copy-start(f32[64,128]{1,0:T(8,128)} %constant.8.clone.coef_ref) | copy-start | bytes 98308
  5.9 0.9 %copy-start.14 = (s32[64,512]{1,0:T(8,128)S(1)}, s32[64,512]{1,0:T(8,128)}, u32[]{:S(2)}) copy-start(s32[64,512]{1,0:T(8,128)} %conn_ref.1) | copy-start | bytes 393220
  6.8 0.8 %copy-start.16 = (s32[1,8192]{1,0:T(1,128)S(1)}, s32[1,8192]{1,0:T(1,128)}, u32[]{:S(2)}) copy-start(s32[1,8192]{1,0:T(1,128)} %peer_ref.1) | copy-start | bytes 98308
  7.5 0.8 %copy-start.17 = (s32[1,8192]{1,0:T(1,128)S(1)}, s32[1,8192]{1,0:T(1,128)}, u32[]{:S(2)}) copy-start(s32[1,8192]{1,0:T(1,128)} %slot_ref.1) | copy-start | bytes 98308
  9.8 26.3 %copy-start.1 = (f32[3,64,512]{2,1,0:T(8,128)S(1)}, f32[3,64,512]{2,1,0:T(8,128)}, u32[]{:S(2)}) copy-start(f32[3,64,512]{2,1,0:T(8,128)} %geom_ref.5) | copy-start | bytes 1179652
  9.8 26.3 %copy-start.3 = (bf16[768,256]{1,0:T(8,128)(2,1)S(1)}, bf16[768,256]{1,0:T(8,128)(2,1)}, u32[]{:S(2)}) copy-start(bf16[768,256]{1,0:T(8,128)(2,1)} %constant.6.clone.tab_f_ref) | copy-start | bytes 1179652
  9.8 26.3 %copy-start.5 = (bf16[768,128]{1,0:T(8,128)(2,1)S(1)}, bf16[768,128]{1,0:T(8,128)(2,1)}, u32[]{:S(2)}) copy-start(bf16[768,128]{1,0:T(8,128)(2,1)} %constant.7.clone.tab_b_ref) | copy-start | bytes 589828
  9.8 26.3 %copy-start.9 = (f32[3,64,512]{2,1,0:T(8,128)S(1)}, f32[3,64,512]{2,1,0:T(8,128)}, u32[]{:S(2)}) copy-start(f32[3,64,512]{2,1,0:T(8,128)} %velocity_ref.1) | copy-start | bytes 1179652
  21.4 14.7 %copy-start.12 = (f32[64,128]{1,0:T(8,128)S(1)}, f32[64,128]{1,0:T(8,128)}, u32[]{:S(2)}) copy-start(f32[64,128]{1,0:T(8,128)} %constant.8.clone.coef_ref) | copy-start | bytes 98308
  21.4 21.2 %all-to-all-start = ((f32[32,2,128]{2,1,0:T(2,128)}), f32[32,2,128]{2,1,0:T(2,128)S(1)}, u32[]{:S(2)}, u32[]{:S(2)}) async-start(f32[32,2,128]{2,1,0:T(2,128)} %bitcast.1), calls=%async_computation | async-start | bytes 65536 | tf_op jit(solution)/shard_map/all_to_all | solution.py:593
  30.1 12.4 %collective-permute-start = (f32[16,128]{1,0:T(8,128)S(1)}, f32[16,128]{1,0:T(8,128)S(1)}, u32[]{:S(2)}, u32[]{:S(2)}) collective-permute-start(f32[16,128]{1,0:T(8,128)S(1)} %get-tuple-element.21), channel_id=1, source_target_pairs={{0,32},{32,64},{64,96},{96,128},{128,160},{160,192},{192,224},{224... | collective-permute-start | bytes 24584 | tf_op jit(solution)/shard_map/ppermute | solution.py:595
  31.9 10.7 %collective-permute-start.1 = (f32[16,128]{1,0:T(8,128)S(1)}, f32[16,128]{1,0:T(8,128)S(1)}, u32[]{:S(2)}, u32[]{:S(2)}) collective-permute-start(f32[16,128]{1,0:T(8,128)S(1)} %get-tuple-element.22), channel_id=1, source_target_pairs={{32,0},{64,32},{96,64},{128,96},{160,128},{192,160},{224,192},{0,2... | collective-permute-start | bytes 24584 | tf_op jit(solution)/shard_map/ppermute | solution.py:596
  36.7 1.0 %copy-start.10 = (f32[3,64,512]{2,1,0:T(8,128)S(1)}, f32[3,64,512]{2,1,0:T(8,128)}, u32[]{:S(2)}) copy-start(f32[3,64,512]{2,1,0:T(8,128)} %force_ref.1) | copy-start | bytes 1179652
  37.7 0.9 %copy-start.15 = (f32[64,512]{1,0:T(8,128)S(1)}, f32[64,512]{1,0:T(8,128)}, u32[]{:S(2)}) copy-start(f32[64,512]{1,0:T(8,128)} %mass_ref.1) | copy-start | bytes 393220
  38.6 4.0 %copy-start.7 = (f32[64,512]{1,0:T(8,128)S(1)}, f32[64,512]{1,0:T(8,128)}, u32[]{:S(2)}) copy-start(f32[64,512]{1,0:T(8,128)} %pressure_ref.3) | copy-start | bytes 393220
  38.6 4.0 %copy-start.8 = (f32[64,512]{1,0:T(8,128)S(1)}, f32[64,512]{1,0:T(8,128)}, u32[]{:S(2)}) copy-start(f32[64,512]{1,0:T(8,128)} %jacobi_ref.3) | copy-start | bytes 393220
  38.6 4.0 %copy-start.13 = (f32[64,512]{1,0:T(8,128)S(1)}, f32[64,512]{1,0:T(8,128)}, u32[]{:S(2)}) copy-start(f32[64,512]{1,0:T(8,128)} %rhs_ref.1) | copy-start | bytes 393220
  47.3 15.4 %all-to-all-start.1 = ((f32[32,8,128]{2,1,0:T(8,128)}), f32[32,8,128]{2,1,0:T(8,128)S(1)}, u32[]{:S(2)}, u32[]{:S(2)}) async-start(f32[32,8,128]{2,1,0:T(8,128)} %bitcast.3), calls=%async_computation.1 | async-start | bytes 262144 | tf_op jit(solution)/shard_map/all_to_all | solution.py:593
  54.9 4.3 %collective-permute-start.2 = (f32[64,128]{1,0:T(8,128)S(1)}, f32[64,128]{1,0:T(8,128)S(1)}, u32[]{:S(2)}, u32[]{:S(2)}) collective-permute-start(f32[64,128]{1,0:T(8,128)S(1)} %get-tuple-element.32), channel_id=1, source_target_pairs={{0,32},{32,64},{64,96},{96,128},{128,160},{160,192},{192,224},{224... | collective-permute-start | bytes 98312 | tf_op jit(solution)/shard_map/ppermute | solution.py:595
  55.0 4.3 %collective-permute-start.3 = (f32[64,128]{1,0:T(8,128)S(1)}, f32[64,128]{1,0:T(8,128)S(1)}, u32[]{:S(2)}, u32[]{:S(2)}) collective-permute-start(f32[64,128]{1,0:T(8,128)S(1)} %get-tuple-element.33), channel_id=1, source_target_pairs={{32,0},{64,32},{96,64},{128,96},{160,128},{192,160},{224,192},{0,2... | collective-permute-start | bytes 98312 | tf_op jit(solution)/shard_map/ppermute | solution.py:596
  (4 other events, 2.8 us)

commit v2 on v1

--- a/solution.py
+++ b/solution.py
@@ -1,6 +1,5 @@
 import jax
 import jax.numpy as jnp
-import ml_dtypes
 import numpy as np
 from jax import lax
 from jax.experimental import pallas as pl
@@ -49,26 +48,12 @@
     return deriv
 
 
-def np_split(table):
-    rest = table.astype(np.float32)
-    parts = []
-    for _ in range(3):
-        part = rest.astype(ml_dtypes.bfloat16)
-        parts.append(part)
-        rest = rest - part.astype(np.float32)
-    return parts
-
-
 def const_tables():
     d32 = deriv_table().astype(np.float32)
     along_j = np.kron(np.eye(2), np.kron(d32, np.eye(8))).astype(np.float32)
     along_k = np.kron(np.eye(16), d32).astype(np.float32)
     fwd = np.concatenate([along_j.T, along_k.T], axis=1)
     bwd = np.concatenate([along_j, along_k], axis=0)
-    fh, fm, fl = np_split(fwd)
-    bh, bm, bl = np_split(bwd)
-    tab_f = np.concatenate([fh, fh, fm, fm, fl, fh], axis=0)
-    tab_b = np.concatenate([bh, bm, bl], axis=0)
     coef = np.zeros((64, 128), np.float32)
     for way, mat in enumerate((d32, d32.T)):
         for to in range(4):
@@ -78,7 +63,7 @@
                     row = way * 32 + (to * 4 + src) * 2
                     coef[row, lanes] = mat[2 * to + half, 2 * src + half]
                     coef[row + 1, lanes] = mat[2 * to + half, 2 * src + 1 - half]
-    return tab_f, tab_b, coef
+    return fwd, bwd, coef
 
 
 def iota(shape, dim):
@@ -242,14 +227,12 @@
     return jnp.concatenate([block[t : t + 1] for t in range(8)], axis=1)
 
 
-def gather_tables(tables, idx_block, hi_count):
-    row = block_row(idx_block)
-    lows = one_hot(row & 127, 128)
+def gather_tables(tables, hi_block, lows, hi_count):
     parts = []
     for table in tables:
         parts += split(table, 2)
     got = dot(jnp.concatenate(parts, axis=0), lows)
-    mask = iota((hi_count, 1024), 0) == (row >> 7)
+    mask = iota((hi_count, 1024), 0) == block_row(hi_block)
     out = []
     for at in range(len(tables)):
         both = got[2 * at * hi_count : (2 * at + 1) * hi_count] + got[(2 * at + 1) * hi_count : (2 * at + 2) * hi_count]
@@ -257,10 +240,8 @@
     return out
 
 
-def scatter_tables(rows, idx_block, hi_count):
-    row = block_row(idx_block)
-    lows = one_hot(row & 127, 128)
-    mask = iota((hi_count, 1024), 0) == (row >> 7)
+def scatter_tables(rows, hi_block, lows, hi_count):
+    mask = iota((hi_count, 1024), 0) == block_row(hi_block)
     parts = []
     for values in rows:
         for part in split(values, 2):
@@ -269,26 +250,33 @@
     return dot_nt(jnp.concatenate(parts, axis=0), lows)
 
 
-def send_values(local_fields, sidx_ref, fidx_ref, msg_ref, up_ref, down_ref, base, stride, face_base):
+def lanes_of(g):
+    return slice(1024 * g, 1024 * g + 1024)
+
+
+def rows_of(g):
+    return slice(8 * g, 8 * g + 8)
+
+
+def send_values(local_fields, shi_ref, fhi_ref, slow_ref, flow_ref, msg_ref, up_ref, down_ref, stride):
     sides = [pack_sides(w) for w in local_fields]
     faces = [pack_faces(w) for w in local_fields]
     for g in range(8):
-        got = gather_tables(sides, sidx_ref[8 * g : 8 * g + 8, :], 16)
+        got = gather_tables(sides, shi_ref[rows_of(g), :], slow_ref[:, lanes_of(g)], 16)
         for f, values in enumerate(got):
             for t in range(8):
-                peer, half = (8 * g + t) // 2, t % 2
-                at = peer * stride + base + 2 * f + half
+                at = (8 * g + t) // 2 * stride + 2 * f + t % 2
                 msg_ref[at : at + 1, :] = values[:, 128 * t : 128 * t + 128]
     for g in range(4):
-        got = gather_tables(faces, fidx_ref[8 * g : 8 * g + 8, :], 64)
+        got = gather_tables(faces, fhi_ref[rows_of(g), :], flow_ref[:, lanes_of(g)], 64)
         out_ref = down_ref if g < 2 else up_ref
         for f, values in enumerate(got):
             for t in range(8):
-                at = face_base + 16 * f + 8 * (g % 2) + t
+                at = 16 * f + 8 * (g % 2) + t
                 out_ref[at : at + 1, :] = values[:, 128 * t : 128 * t + 128]
 
 
-def take_values(count, sidx_ref, fidx_ref, msg_ref, low_refs, upp_refs, stride):
+def take_values(count, shi_ref, fhi_ref, slow_ref, flow_ref, msg_ref, low_ref, upp_ref, stride):
     side = None
     for g in range(8):
         rows = []
@@ -298,13 +286,13 @@
                 at = (8 * g + t) // 2 * stride + 2 * f + t % 2
                 cells.append(msg_ref[at : at + 1, :])
             rows.append(jnp.concatenate(cells, axis=1))
-        part = scatter_tables(rows, sidx_ref[8 * g : 8 * g + 8, :], 16)
+        part = scatter_tables(rows, shi_ref[rows_of(g), :], slow_ref[:, lanes_of(g)], 16)
         side = part if side is None else side + part
     face = None
     for g in range(4):
-        refs = low_refs if g < 2 else upp_refs
-        rows = [block_row(refs[f][0][refs[f][1] + 8 * (g % 2) : refs[f][1] + 8 * (g % 2) + 8, :]) for f in range(count)]
-        part = scatter_tables(rows, fidx_ref[8 * g : 8 * g + 8, :], 64)
+        ref = low_ref if g < 2 else upp_ref
+        rows = [block_row(ref[16 * f + 8 * (g % 2) : 16 * f + 8 * (g % 2) + 8, :]) for f in range(count)]
+        part = scatter_tables(rows, fhi_ref[rows_of(g), :], flow_ref[:, lanes_of(g)], 64)
         face = part if face is None else face + part
     sides = [side[32 * f : 32 * f + 16] + side[32 * f + 16 : 32 * f + 32] for f in range(count)]
     faces = [face[128 * f : 128 * f + 64] + face[128 * f + 64 : 128 * f + 128] for f in range(count)]
@@ -336,115 +324,141 @@
     return (chain_place(left_y) * 8.0 + chain_place(left_x)).astype(I32)
 
 
-def place_table(hi_ref, lo_ref, acc_ref, blocks, hi_count):
-    lane = (iota((1, 128), 1)).astype(F32)
-    acc_ref[...] = jnp.zeros((HI, 256), F32)
-
-    def step(g, carry):
-        hi_block = hi_ref[pl.ds(pl.multiple_of(8 * g, 8), 8), :]
-        lo_block = lo_ref[pl.ds(pl.multiple_of(8 * g, 8), 8), :]
-        top = one_hot(block_row(hi_block), HI)
-        low, high = [], []
+def place_table(hi, lo, count):
+    lane = 1.0 + iota((128, 128), 1).astype(F32) * (1.0 / 128.0)
+    total = None
+    for g in range(count // 8):
+        top = one_hot(block_row(hi[rows_of(g)]), HI)
+        low = []
         for t in range(8):
-            hit = iota((128, 128), 0) == lo_block[t : t + 1]
-            base = ((8 * g + t) * 128).astype(F32)
-            low.append(jnp.where(hit, jnp.broadcast_to(lane, (128, 128)), 0.0).astype(BF16))
-            high.append(jnp.where(hit, base, 0.0).astype(BF16))
-        both = jnp.concatenate([jnp.concatenate(low, axis=1), jnp.concatenate(high, axis=1)], axis=0)
-        acc_ref[...] += dot_nt(top, both)
-        return carry
-
-    lax.fori_loop(0, blocks, step, 0)
+            hit = iota((128, 128), 0) == lo[8 * g + t : 8 * g + t + 1]
+            low.append(jnp.where(hit, lane * (2.0 ** (8 * g + t - count // 2)), 0.0).astype(BF16))
+        part = dot_nt(jnp.concatenate(low, axis=1), top)
+        total = part if total is None else total + part
+    return total.astype(BF16)
 
 
 def look_up(table, row):
-    low = one_hot(row & 127, 128)
-    got = dot(table, jnp.concatenate([low, low], axis=0))
-    mask = iota((HI, row.shape[1]), 0) == (row >> 7)
+    got = dot(table, one_hot(row >> 7, HI))
+    mask = iota((128, row.shape[1]), 0) == (row & 127)
     return jnp.sum(jnp.where(mask, got, 0.0), axis=0, keepdims=True)
 
 
-def tables_body(conn_ref, peer_ref, slot_ref, node_ref, counts_ref, axial_ref, sidx_ref, fidx_ref, perm_ref, back_ref, scratch):
-    acc_s, acc_f, s_hi, s_lo, f_hi, f_lo, nodes = scratch
-    conn = conn_ref[...]
+def decode(x, count):
+    x = x * (2.0 ** (count // 2))
+    row = jnp.zeros(x.shape, I32)
+    jump = count // 2
+    while jump:
+        big = x >= 2.0**jump
+        row = row + jnp.where(big, jump, 0)
+        x = jnp.where(big, x * (2.0**-jump), x)
+        jump //= 2
+    return row, (x * 128.0).astype(I32) - 128
+
+
+def put_rows(ref, at, values):
+    for t in range(8):
+        ref[at + t : at + t + 1, :] = values[:, 128 * t : 128 * t + 128]
+
+
+def build_perm(conn, perm_ref, back_ref):
     place = brick_places(conn)
     lane3 = iota((64, 192), 1) & 63
     place_row = jnp.sum(jnp.where(lane3 == iota((64, 192), 0), place, 0), axis=0, keepdims=True)
     perm_ref[...] = (iota((64, 192), 0) == place_row).astype(F32).astype(BF16)
     back_ref[...] = (lane3 == place).astype(F32).astype(BF16)
-    perm = perm_ref[:, 0:64]
-
+
+
+def node_places(conn, perm):
     ids = jnp.concatenate([(conn >> 7).astype(F32), (conn & 127).astype(F32)], axis=1).astype(BF16)
     ids = dot(perm, ids)
     hi_c = chunks_of(ids[:, 0:512])
     lo_c = chunks_of(ids[:, 512:1024])
-    lane8 = iota((8, 128), 1)
-    row8 = iota((8, 128), 0)
-    keep_x = (((lane8 >> 3) & 7) < 7) | (row8 == 7)
+    lane8 = iota((16, 128), 1)
+    row8 = iota((16, 128), 0)
+    in_x = (((lane8 >> 3) & 7) < 7) | (row8 == 7)
     i_y = 2 * (((lane8 >> 3) & 7) >> 1) + (lane8 >> 6)
-    keep_y = (i_y < 7) & ((row8 > 0) | (i_y > 0))
+    in_y = (i_y < 7) & ((row8 > 8) | (i_y > 0))
+    keep_s = ((row8 < 8) & in_x) | ((row8 >= 8) & in_y)
     lane = iota((64, 128), 1)
     row = iota((64, 128), 0)
     i_f = 2 * ((lane & 7) >> 1) + (lane >> 6)
     keep_f = ((i_f < 7) | ((row & 7) == 7)) & ((((lane >> 3) & 7) < 7) | ((row >> 3) == 7))
-    side_hi = pack_sides(hi_c)
-    s_hi[0:8, :] = jnp.where(keep_x, side_hi[0:8], -1.0).astype(I32)
-    s_hi[8:16, :] = jnp.where(keep_y, side_hi[8:16], -1.0).astype(I32)
-    s_lo[...] = pack_sides(lo_c).astype(I32)
-    f_hi[...] = jnp.where(keep_f, pack_faces(hi_c), -1.0).astype(I32)
-    f_lo[...] = pack_faces(lo_c).astype(I32)
-    place_table(s_hi, s_lo, acc_s, 2, 16)
-    place_table(f_hi, f_lo, acc_f, 8, 64)
-
-    nodes[...] = jnp.zeros((128, 128), F32)
-
-    def invert(g, carry):
-        at = pl.ds(pl.multiple_of(1024 * g, 1024), 1024)
-        peer = peer_ref[:, at]
+    table_s = place_table(
+        jnp.where(keep_s, pack_sides(hi_c), -1.0).astype(I32), pack_sides(lo_c).astype(I32), 16
+    )
+    table_f = place_table(
+        jnp.where(keep_f, pack_faces(hi_c), -1.0).astype(I32), pack_faces(lo_c).astype(I32), 64
+    )
+    return table_s, table_f
+
+
+def side_lists(table_s, peer_ref, slot_ref, node_ref, counts, shi_ref, slow_ref):
+    total = None
+    for g in range(8):
+        at = lanes_of(g)
         slot = slot_ref[:, at]
-        node = node_ref[:, at]
-        hit = iota((64, 1024), 0) == (peer * 2 + (slot >> 7))
-        first = jnp.where(hit, (node >> 7).astype(F32), 0.0).astype(BF16)
-        second = jnp.where(hit, (node & 127).astype(F32), 0.0).astype(BF16)
-        nodes[...] += dot_nt(jnp.concatenate([first, second], axis=0), one_hot(slot & 127, 128))
-        return carry
-
-    lax.fori_loop(0, 8, invert, 0)
-    ordered = (nodes[0:64, :] * 128.0 + nodes[64:128, :]).astype(I32)
-    table_s = acc_s[...].astype(BF16)
+        places = look_up(table_s, node_ref[:, at])
+        hit = iota((64, 1024), 0) == (peer_ref[:, at] * 2 + (slot >> 7))
+        part = dot_nt(jnp.where(hit, places, 0.0).astype(BF16), one_hot(slot & 127, 128))
+        total = part if total is None else total + part
+    row, lane = decode(total, 16)
+    limit = jnp.sum(jnp.where(iota((64, 32), 1) == (iota((64, 32), 0) >> 1), counts, 0), axis=1, keepdims=True)
+    slots = (iota((64, 128), 0) & 1) * 128 + iota((64, 128), 1)
+    shi_ref[...] = jnp.where(slots < limit, row, -1)
     for g in range(8):
-        places = look_up(table_s, block_row(ordered[8 * g : 8 * g + 8]))
-        for t in range(8):
-            sidx_ref[8 * g + t : 8 * g + t + 1, :] = places[:, 128 * t : 128 * t + 128].astype(I32)
-    table_f = acc_f[...].astype(BF16)
+        slow_ref[:, lanes_of(g)] = one_hot(block_row(lane[rows_of(g)]), 128)
+
+
+def face_lists(table_f, axial_ref, coded_ref, fhi_ref, flow_ref):
     for g in range(4):
-        cells = axial_ref[g // 2 : g // 2 + 1, 1024 * (g % 2) : 1024 * (g % 2) + 1024]
-        places = look_up(table_f, cells)
-        for t in range(8):
-            fidx_ref[8 * g + t : 8 * g + t + 1, :] = places[:, 128 * t : 128 * t + 128].astype(I32)
-    limit = jnp.sum(
-        jnp.where(iota((64, 32), 1) == (iota((64, 32), 0) >> 1), counts_ref[...], 0), axis=1, keepdims=True
-    )
-    slots = (iota((64, 128), 0) & 1) * 128 + iota((64, 128), 1)
-    sidx_ref[...] = jnp.where(slots < limit, sidx_ref[...], -1)
-
-
-def first_kernel(
-    conn_ref, peer_ref, slot_ref, node_ref, counts_ref, axial_ref, pressure_ref, geom_ref, tab_f_ref, tab_b_ref, coef_ref,
-    msg_ref, up_ref, down_ref, w_ref, sidx_ref, fidx_ref, perm_ref, back_ref, *scratch,
-):
-    tables_body(
-        conn_ref, peer_ref, slot_ref, node_ref, counts_ref, axial_ref, sidx_ref, fidx_ref, perm_ref, back_ref, scratch
-    )
+        put_rows(coded_ref, 8 * g, look_up(table_f, axial_ref[0, g // 2 : g // 2 + 1, lanes_of(g % 2)]))
+    row, lane = decode(coded_ref[...], 64)
+    fhi_ref[...] = row
+    for g in range(4):
+        flow_ref[:, lanes_of(g)] = one_hot(block_row(lane[rows_of(g)]), 128)
+
+
+def first_kernel(*refs):
+    (conn_h, peer_h, slot_h, node_h, counts_h, axial_h, pressure_h, geom_h, fwd_h, bwd_h, coef_h) = refs[:11]
+    later_h = refs[11:17]
+    (msg_ref, up_ref, down_ref, w_ref, shi_ref, fhi_ref, slow_ref, flow_ref, perm_ref, back_ref) = refs[17:27]
+    (tab_f_ref, tab_b_ref, coef_ref, pressure_ref, geom_ref) = refs[27:32]
+    later = refs[32:38]
+    (conn_ref, peer_ref, slot_ref, node_ref, counts_ref, axial_ref, fwd_ref, bwd_ref, coded_ref, sems) = refs[38:]
+    pairs = [
+        (conn_h, conn_ref), (pressure_h, pressure_ref), (fwd_h, fwd_ref), (bwd_h, bwd_ref), (coef_h, coef_ref),
+        (geom_h, geom_ref), (node_h, node_ref), (peer_h, peer_ref), (slot_h, slot_ref), (counts_h, counts_ref),
+        (axial_h, axial_ref), *zip(later_h, later),
+    ]
+    copies = [pltpu.make_async_copy(src, dst, sems.at[at]) for at, (src, dst) in enumerate(pairs)]
+    for copy in copies:
+        copy.start()
+    copies[0].wait()
+    conn = conn_ref[...]
+    build_perm(conn, perm_ref, back_ref)
+    for copy in copies[1:11]:
+        copy.wait()
+    fh, fm, fl = split(fwd_ref[...], 3)
+    for at, part in enumerate([fh, fh, fm, fm, fl, fh]):
+        tab_f_ref[128 * at : 128 * at + 128, :] = part
+    for at, part in enumerate(split(bwd_ref[...], 3)):
+        tab_b_ref[256 * at : 256 * at + 256, :] = part
+    table_s, table_f = node_places(conn, perm_ref[:, 0:64])
     out = laplace(chunks_of(pressure_ref[...]), geom_ref, tab_f_ref, tab_b_ref, coef_ref)
     w = permute(perm_ref[...], out)
     for c in range(4):
         w_ref[:, 128 * c : 128 * c + 128] = w[c]
-    send_values([assemble_local(w)], sidx_ref, fidx_ref, msg_ref, up_ref, down_ref, 0, 2, 0)
+    side_lists(table_s, peer_ref, slot_ref, node_ref, counts_ref[...], shi_ref, slow_ref)
+    face_lists(table_f, axial_ref, coded_ref, fhi_ref, flow_ref)
+    send_values([assemble_local(w)], shi_ref, fhi_ref, slow_ref, flow_ref, msg_ref, up_ref, down_ref, 2)
+    for copy in copies[11:]:
+        copy.wait()
 
 
 def momentum_kernel(
-    velocity_ref, force_ref, mass_ref, metric_ref, geom_ref, tab_f_ref, tab_b_ref, coef_ref, perm_ref, sidx_ref, fidx_ref,
+    velocity_ref, force_ref, mass_ref, metric_ref, geom_ref, tab_f_ref, tab_b_ref, coef_ref, perm_ref, shi_ref, fhi_ref,
+    slow_ref, flow_ref,
     msg_ref, up_ref, down_ref, w_ref,
 ):
     parts = [chunks_of(velocity_ref[a]) for a in range(3)]
@@ -476,15 +490,15 @@
         for c in range(4):
             w_ref[f, :, 128 * c : 128 * c + 128] = w[c]
         fields.append(assemble_local(w))
-    send_values(fields, sidx_ref, fidx_ref, msg_ref, up_ref, down_ref, 0, 6, 0)
+    send_values(fields, shi_ref, fhi_ref, slow_ref, flow_ref, msg_ref, up_ref, down_ref, 6)
 
 
 def second_kernel(
     msg_in_ref, low_ref, upp_ref, w_in_ref, pressure_ref, rhs_ref, jacobi_ref, geom_ref, tab_f_ref, tab_b_ref, coef_ref,
-    perm_ref, back_ref, sidx_ref, fidx_ref, msg_m_ref, up_m_ref, down_m_ref,
+    perm_ref, back_ref, shi_ref, fhi_ref, slow_ref, flow_ref, msg_m_ref, up_m_ref, down_m_ref,
     msg_ref, up_ref, down_ref, w_ref, base_ref, res_ref,
 ):
-    sides, faces = take_values(1, sidx_ref, fidx_ref, msg_in_ref, [(low_ref, 0)], [(upp_ref, 0)], 2)
+    sides, faces = take_values(1, shi_ref, fhi_ref, slow_ref, flow_ref, msg_in_ref, low_ref, upp_ref, 2)
     w = add_back(chunks_of(w_in_ref[...]), sides[0], faces[0])
     applied = permute(back_ref[...], assemble_local(w))
     step = []
@@ -500,7 +514,7 @@
     w = permute(perm_ref[...], out)
     for c in range(4):
         w_ref[:, 128 * c : 128 * c + 128] = w[c]
-    send_values([assemble_local(w)], sidx_ref, fidx_ref, msg_ref, up_ref, down_ref, 0, 8, 0)
+    send_values([assemble_local(w)], shi_ref, fhi_ref, slow_ref, flow_ref, msg_ref, up_ref, down_ref, 8)
     for peer in range(32):
         msg_ref[8 * peer + 2 : 8 * peer + 8, :] = msg_m_ref[6 * peer : 6 * peer + 6, :]
     up_ref[16:64, :] = up_m_ref[...]
@@ -508,83 +522,106 @@
 
 
 def last_kernel(
-    msg_in_ref, low_ref, upp_ref, w_in_ref, w_m_ref, jacobi_ref, base_ref, res_ref, back_ref, sidx_ref, fidx_ref,
-    pressure_ref, momentum_ref,
+    msg_in_ref, low_ref, upp_ref, w_in_ref, w_m_ref, jacobi_ref, base_ref, res_ref, back_ref, shi_ref, fhi_ref, slow_ref,
+    flow_ref,
+    pressure_h, momentum_h,
+    out_ref, sems,
 ):
-    low = [(low_ref, 16 * f) for f in range(4)]
-    upp = [(upp_ref, 16 * f) for f in range(4)]
-    sides, faces = take_values(4, sidx_ref, fidx_ref, msg_in_ref, low, upp, 8)
+    sides, faces = take_values(4, shi_ref, fhi_ref, slow_ref, flow_ref, msg_in_ref, low_ref, upp_ref, 8)
+    copies = []
     for f in range(4):
         held = w_in_ref[...] if f == 0 else w_m_ref[f - 1]
         w = add_back(chunks_of(held), sides[f], faces[f])
         applied = permute(back_ref[...], assemble_local(w))
         for c in range(4):
             lanes = slice(128 * c, 128 * c + 128)
+            value = applied[c]
             if f == 0:
-                pressure_ref[:, lanes] = base_ref[:, lanes] + 2.0 * RHO_NEXT / CHEB_DELTA * jacobi_ref[:, lanes] * (
-                    res_ref[:, lanes] - applied[c]
+                value = base_ref[:, lanes] + 2.0 * RHO_NEXT / CHEB_DELTA * jacobi_ref[:, lanes] * (
+                    res_ref[:, lanes] - value
                 )
-            else:
-                momentum_ref[f - 1, :, lanes] = applied[c]
+            out_ref[f, :, lanes] = value
+        copy = pltpu.make_async_copy(out_ref.at[f], pressure_h if f == 0 else momentum_h.at[f - 1], sems.at[f])
+        copy.start()
+        copies.append(copy)
+    for copy in copies:
+        copy.wait()
 
 
 def shape(*dims, dtype=F32):
     return jax.ShapeDtypeStruct(dims, dtype)
 
 
-def call(kernel, outs, args, scratch=(), name=None):
-    vmem = pl.BlockSpec(memory_space=pltpu.VMEM)
+def in_vmem():
+    return pl.BlockSpec(memory_space=pltpu.VMEM)
+
+
+def in_hbm():
+    return pl.BlockSpec(memory_space=pltpu.HBM)
+
+
+def call(kernel, outs, args, scratch=(), name=None, args_hbm=False, outs_hbm=False):
+    if args_hbm:
+        args = [pltpu.with_memory_space_constraint(x, pltpu.HBM) for x in args]
     return pl.pallas_call(
         kernel,
         out_shape=outs,
-        in_specs=[vmem] * len(args),
-        out_specs=[vmem] * len(outs),
+        in_specs=[in_hbm() if args_hbm else in_vmem() for _ in args],
+        out_specs=[in_hbm() if outs_hbm else in_vmem() for _ in outs],
         scratch_shapes=list(scratch),
         compiler_params=pltpu.CompilerParams(vmem_limit_bytes=VMEM_LIMIT),
         name=name,
     )(*args)
 
 
-def consts():
-    return [jnp.asarray(t) for t in const_tables()]
-
-
-def run_first(conn, peer, slot, node, counts, axial, pressure, geom):
-    return call(
+def like(x):
+    return jax.ShapeDtypeStruct(x.shape, x.dtype)
+
+
+def run_first(conn, peer, slot, node, counts, axial, pressure, geom, later):
+    fwd, bwd, coef = [jnp.asarray(t) for t in const_tables()]
+    held = [conn, peer, slot, node, counts, axial, fwd, bwd]
+    outs = call(
         first_kernel,
         [shape(64, 128), shape(16, 128), shape(16, 128), shape(64, 512), shape(64, 128, dtype=I32),
-         shape(32, 128, dtype=I32), shape(64, 192, dtype=BF16), shape(64, 192, dtype=BF16)],
-        [conn, peer, slot, node, counts, axial, pressure, geom, *consts()],
-        [pltpu.VMEM((HI, 256), F32), pltpu.VMEM((HI, 256), F32), pltpu.VMEM((16, 128), I32), pltpu.VMEM((16, 128), I32),
-         pltpu.VMEM((64, 128), I32), pltpu.VMEM((64, 128), I32), pltpu.VMEM((128, 128), F32)],
+         shape(32, 128, dtype=I32), shape(128, 8192, dtype=BF16), shape(128, 4096, dtype=BF16),
+         shape(64, 192, dtype=BF16), shape(64, 192, dtype=BF16), shape(768, 256, dtype=BF16), shape(768, 128, dtype=BF16),
+         like(coef), like(pressure), like(geom), *[like(x) for x in later]],
+        [conn, peer, slot, node, counts, axial, pressure, geom, fwd, bwd, coef, *later],
+        [*[pltpu.VMEM(x.shape, x.dtype) for x in held], pltpu.VMEM((32, 128), F32),
+         pltpu.SemaphoreType.DMA((11 + len(later),))],
         "first",
-    )
-
-
-def run_momentum(velocity, force, mass, metric, geom, perm, sidx, fidx):
+        args_hbm=True,
+    )
+    return outs[:4], outs[4:8], outs[8:10], outs[10:13], outs[13:15], outs[15:]
+
+
+def run_momentum(velocity, force, mass, metric, geom, tables, perm, lists):
     return call(
         momentum_kernel,
         [shape(192, 128), shape(48, 128), shape(48, 128), shape(3, 64, 512)],
-        [velocity, force, mass, metric, geom, *consts(), perm, sidx, fidx],
+        [velocity, force, mass, metric, geom, *tables, perm, *lists],
         name="momentum",
     )
 
 
-def run_second(msg, low, upp, w, pressure, rhs, jacobi, geom, perm, back, sidx, fidx, msg_m, up_m, down_m):
+def run_second(msg, low, upp, w, pressure, rhs, jacobi, geom, tables, perm, back, lists, msg_m, up_m, down_m):
     return call(
         second_kernel,
         [shape(256, 128), shape(64, 128), shape(64, 128), shape(64, 512), shape(64, 512), shape(64, 512)],
-        [msg, low, upp, w, pressure, rhs, jacobi, geom, *consts(), perm, back, sidx, fidx, msg_m, up_m, down_m],
+        [msg, low, upp, w, pressure, rhs, jacobi, geom, *tables, perm, back, *lists, msg_m, up_m, down_m],
         name="second",
     )
 
 
-def run_last(msg, low, upp, w, w_m, jacobi, base, res, back, sidx, fidx):
+def run_last(msg, low, upp, w, w_m, jacobi, base, res, back, lists):
     return call(
         last_kernel,
         [shape(64, 512), shape(3, 64, 512)],
-        [msg, low, upp, w, w_m, jacobi, base, res, back, sidx, fidx],
+        [msg, low, upp, w, w_m, jacobi, base, res, back, *lists],
+        [pltpu.VMEM((4, 64, 512), F32), pltpu.SemaphoreType.DMA((4,))],
         name="last",
+        outs_hbm=True,
     )
 
 
@@ -600,16 +637,19 @@
 def on_device(
     pressure, rhs, jacobi, geom, velocity, force, mass, metric, conn, ent_peer, ent_slot, ent_node, counts, axial_nodes
 ):
-    msg, up, down, w, sidx, fidx, perm, back = run_first(
-        conn, ent_peer, ent_slot, ent_node, counts, axial_nodes[0], pressure, geom
-    )
+    sent, lists, (perm, back), tables, (pressure, geom), later = run_first(
+        conn, ent_peer, ent_slot, ent_node, counts, axial_nodes, pressure, geom,
+        [velocity, force, mass, metric, rhs, jacobi],
+    )
+    velocity, force, mass, metric, rhs, jacobi = later
+    msg, up, down, w = sent
     got = exchange(msg, up, down)
-    msg_m, up_m, down_m, w_m = run_momentum(velocity, force, mass, metric, geom, perm, sidx, fidx)
+    msg_m, up_m, down_m, w_m = run_momentum(velocity, force, mass, metric, geom, tables, perm, lists)
     msg, up, down, w, base, res = run_second(
-        *got, w, pressure, rhs, jacobi, geom, perm, back, sidx, fidx, msg_m, up_m, down_m
+        *got, w, pressure, rhs, jacobi, geom, tables, perm, back, lists, msg_m, up_m, down_m
     )
     got = exchange(msg, up, down)
-    return tuple(run_last(*got, w, w_m, jacobi, base, res, back, sidx, fidx))
+    return tuple(run_last(*got, w, w_m, jacobi, base, res, back, lists))
 
 
 def solution(mesh):

time: 67 us -> 97.5 us (1.46)
  local copies, waits for them, and re-layouts: 11.7 us -> 47.6 us
  Pallas kernels: 23.7 us -> 18.6 us
  waiting for transfers between devices: 4.95 us -> 3.73 us
    unnamed x44 -> x128, local copies, waits for them, and re-layouts: 11.7 us -> 47.6 us
    pallas_call x4, Pallas kernels: 23.7 us -> 18.6 us  [call(): pl.pallas_call(kernel, out_shape=outs, in_specs=[in_hbm() if args_hbm els...]
    all_to_all x2, waiting for transfers between devices: 3.35 us -> 1.92 us  [exchange(): lax.all_to_all(msg.reshape(32, rows, 128), ('gy', 'gz'), split_axis=0, co...]
  transfers between devices with their start and end apart: 6 -> 6, of which waited for: 2 -> 2; matrix products, arithmetic and copies ran while one was open for 0% -> 0% of each run, Pallas kernels for 6% -> 4%
where the time goes in v2:
time: 97.5 us; the launch traced here: 95.8 us
  local copies, waits for them, and re-layouts  47.6 us (49%)
  starting transfers between devices  25 us (26%)
  Pallas kernels  18.6 us (19%)
  waiting for transfers between devices  3.73 us (4%)
    unnamed x128, local copies, waits for them, and re-layouts  47.6 us
    pallas_call x4, Pallas kernels, call(): pl.pallas_call(kernel, out_shape=outs, in_specs=[in_hbm() if args_hbm els...  18.6 us
    all_to_all x2, starting transfers between devices, exchange(): lax.all_to_all(msg.reshape(32, rows, 128), ('gy', 'gz'), split_axis=0, co...  16.3 us
    ppermute x2, starting transfers between devices, exchange(): lax.ppermute(down, 'gx', [((i + 1) % count, i) for i in range(count)])  6.87 us
  transfers between devices with their start and end apart: 6, of which 2 were waited for; matrix products, arithmetic and copies ran while one was open for 0% of the time, Pallas kernels for 4%

profile of v2, /device:TPU:1, one launch (start us, length us, event | category | flops | bytes accessed | tf_op | source)
XLA Modules:
  0.0 95.8 jit_solution(13664116054723265001)
XLA Ops:
  0.6 7.4 %first.1 = (f32[64,128]{1,0:T(8,128)S(1)}, f32[16,128]{1,0:T(8,128)S(1)}, f32[16,128]{1,0:T(8,128)S(1)}, f32[64,512]{1,0:T(8,128)S(1)}, s32[64,128]{1,0:T(8,128)...) custom-call(s32[64,512]{1,0:T(8,128)} %refs_0_.1, ...), custom_call_target="tpu_custom_call" | custom-call | tf_op jit(solution)/shard_map/first/pallas_call | solution.py:566
  19.1 8.6 %all-to-all-start = ((f32[32,2,128]{2,1,0:T(2,128)}), f32[32,2,128]{2,1,0:T(2,128)}, u32[]{:S(2)}, u32[]{:S(2)}) async-start(f32[32,2,128]{2,1,0:T(2,128)} %bitcast.6), calls=%async_computation | async-start | bytes 65536 | tf_op jit(solution)/shard_map/all_to_all | solution.py:630
  27.8 1.7 %collective-permute-start = (f32[16,128]{1,0:T(8,128)}, f32[16,128]{1,0:T(8,128)S(1)}, u32[]{:S(2)}, u32[]{:S(2)}) collective-permute-start(f32[16,128]{1,0:T(8,128)} %copy-done.63), channel_id=1, source_target_pairs={{0,32},{32,64},{64,96},{96,128},{128,160},{160,192},{192,224},{224... | collective-permute-start | bytes 24584 | tf_op jit(solution)/shard_map/ppermute | solution.py:632
  29.5 4.2 %collective-permute-start.1 = (f32[16,128]{1,0:T(8,128)}, f32[16,128]{1,0:T(8,128)S(1)}, u32[]{:S(2)}, u32[]{:S(2)}) collective-permute-start(f32[16,128]{1,0:T(8,128)} %copy-done.62), channel_id=1, source_target_pairs={{32,0},{64,32},{96,64},{128,96},{160,128},{192,160},{224,192},{0,2... | collective-permute-start | bytes 24584 | tf_op jit(solution)/shard_map/ppermute | solution.py:633
  33.7 1.0 %copy-done.1 = f32[3,64,512]{2,1,0:T(8,128)S(1)} copy-done((f32[3,64,512]{2,1,0:T(8,128)S(1)}, f32[3,64,512]{2,1,0:T(8,128)}, u32[]{:S(2)}) %copy-start.1) | copy-done | bytes 393240
  34.7 0.9 copy-done.4
  35.6 1.0 %copy-done.12 = f32[3,64,512]{2,1,0:T(8,128)S(1)} copy-done((f32[3,64,512]{2,1,0:T(8,128)S(1)}, f32[3,64,512]{2,1,0:T(8,128)}, u32[]{:S(2)}) %copy-start.12) | copy-done | bytes 393240
  36.6 1.0 %copy-done.14 = f32[3,64,512]{2,1,0:T(8,128)S(1)} copy-done((f32[3,64,512]{2,1,0:T(8,128)S(1)}, f32[3,64,512]{2,1,0:T(8,128)}, u32[]{:S(2)}) %copy-start.14) | copy-done | bytes 393240
  39.9 0.9 copy-done.41
  41.4 3.6 %momentum.1 = (f32[192,128]{1,0:T(8,128)S(1)}, f32[48,128]{1,0:T(8,128)S(1)}, f32[48,128]{1,0:T(8,128)S(1)}, f32[3,64,512]{2,1,0:T(8,128)S(1)}) custom-call(f32[3,64,512]{2,1,0:T(8,128)S(1)} %copy-done.12, f32[3,64,512]{2,1,0:T(8,128)S(1)} %copy-done.14, f32[64,512]{1,0:T(8,128)S(1)} %copy-done.41, f32[3,64]{1,0:T(4,128)S(1)} %copy-done.59, ...), custom_call_target="tpu_custom_call" | custom-call | tf_op jit(solution)/shard_map/momentum/pallas_call | solution.py:566
  48.8 1.0 %copy-done.2 = f32[3,64,512]{2,1,0:T(8,128)S(1)} copy-done((f32[3,64,512]{2,1,0:T(8,128)S(1)}, f32[3,64,512]{2,1,0:T(8,128)}, u32[]{:S(2)}) %copy-start.2) | copy-done | bytes 393240
  49.8 0.9 copy-done.5
  50.8 0.9 copy-done.7
  54.7 0.9 copy-done.29
  55.6 0.9 copy-done.31
  56.5 0.9 copy-done.33
  61.2 4.1 %second.1 = (f32[256,128]{1,0:T(8,128)S(1)}, f32[64,128]{1,0:T(8,128)S(1)}, f32[64,128]{1,0:T(8,128)S(1)}, f32[64,512]{1,0:T(8,128)S(1)}, f32[64,512]{1,0:T(8,128)S(1)}, /*index=5*/f32[64,512]{1,0:T(8,128)S(1)}) custom-call(f32[64,128]{1,0:T(8,128)} %bitcast.1.msg_in_ref, f32[16,128]{1,0:T(8,128)S(1)} %copy-done.55, f32[16,128]{1,0:T(8,128)S(1)} %copy-done.57, ...), custom_call_target="tpu_custom_call" | custom-call | tf_op jit(solution)/shard_map/second/pallas_call | solution.py:566
  69.1 7.7 %all-to-all-start.1 = ((f32[32,8,128]{2,1,0:T(8,128)}), f32[32,8,128]{2,1,0:T(8,128)S(1)}, u32[]{:S(2)}, u32[]{:S(2)}) async-start(f32[32,8,128]{2,1,0:T(8,128)} %bitcast.5), calls=%async_computation.1 | async-start | bytes 262144 | tf_op jit(solution)/shard_map/all_to_all | solution.py:630
  76.9 2.7 %collective-permute-start.3 = (f32[64,128]{1,0:T(8,128)}, f32[64,128]{1,0:T(8,128)S(1)}, u32[]{:S(2)}, u32[]{:S(2)}) collective-permute-start(f32[64,128]{1,0:T(8,128)} %copy-done.60), channel_id=1, source_target_pairs={{32,0},{64,32},{96,64},{128,96},{160,128},{192,160},{224,192},{0,2... | collective-permute-start | bytes 98312 | tf_op jit(solution)/shard_map/ppermute | solution.py:633
  79.6 1.8 %collective-permute-done.2.low_ref = f32[64,128]{1,0:T(8,128)S(1)} collective-permute-done((f32[64,128]{1,0:T(8,128)}, f32[64,128]{1,0:T(8,128)S(1)}, u32[]{:S(2)}, u32[]{:S(2)}) %collective-permute-start.2) | collective-permute-done | bytes 32800 | tf_op jit(solution)/shard_map/ppermute | solution.py:632
  82.6 1.9 %all-to-all-done.1 = f32[32,8,128]{2,1,0:T(8,128)S(1)} async-done(((f32[32,8,128]{2,1,0:T(8,128)}), f32[32,8,128]{2,1,0:T(8,128)S(1)}, u32[]{:S(2)}, u32[]{:S(2)}) %all-to-all-start.1) | async-done | bytes 131104 | tf_op jit(solution)/shard_map/all_to_all | solution.py:630
  84.5 0.9 copy-done.8
  85.4 1.0 %copy-done.10 = f32[3,64,512]{2,1,0:T(8,128)S(1)} copy-done((f32[3,64,512]{2,1,0:T(8,128)S(1)}, f32[3,64,512]{2,1,0:T(8,128)}, u32[]{:S(2)}) %copy-start.10) | copy-done | bytes 393240
  92.2 3.4 %last.1 = (f32[64,512]{1,0:T(8,128)}, f32[3,64,512]{2,1,0:T(8,128)}) custom-call(f32[256,128]{1,0:T(8,128)S(1)} %bitcast.4, f32[64,128]{1,0:T(8,128)S(1)} %copy-done.46, f32[64,128]{1,0:T(8,128)S(1)} %copy-done.48, f32[64,512]{1,0:T(8,128)S(1)} %copy-done.35, f32[3,64,512]{2,1,0:T(8,128)S(1)} %copy-done.10, f32[64,512]{1,0:T(8,128)S(1)} %copy-done.8, ...), custom_call_target="tpu_custom_call" | custom-call | tf_op jit(solution)/shard_map/last/pallas_call | solution.py:566
  (120 shorter events, 35.4 us)
Async XLA Ops:
  10.9 0.8 copy-start.13
  19.1 29.7 %all-to-all-start = ((f32[32,2,128]{2,1,0:T(2,128)}), f32[32,2,128]{2,1,0:T(2,128)}, u32[]{:S(2)}, u32[]{:S(2)}) async-start(f32[32,2,128]{2,1,0:T(2,128)} %bitcast.6), calls=%async_computation | async-start | bytes 65536 | tf_op jit(solution)/shard_map/all_to_all | solution.py:630
  27.8 19.9 %collective-permute-start = (f32[16,128]{1,0:T(8,128)}, f32[16,128]{1,0:T(8,128)S(1)}, u32[]{:S(2)}, u32[]{:S(2)}) collective-permute-start(f32[16,128]{1,0:T(8,128)} %copy-done.63), channel_id=1, source_target_pairs={{0,32},{32,64},{64,96},{96,128},{128,160},{160,192},{192,224},{224... | collective-permute-start | bytes 24584 | tf_op jit(solution)/shard_map/ppermute | solution.py:632
  29.5 18.8 %collective-permute-start.1 = (f32[16,128]{1,0:T(8,128)}, f32[16,128]{1,0:T(8,128)S(1)}, u32[]{:S(2)}, u32[]{:S(2)}) collective-permute-start(f32[16,128]{1,0:T(8,128)} %copy-done.62), channel_id=1, source_target_pairs={{32,0},{64,32},{96,64},{128,96},{160,128},{192,160},{224,192},{0,2... | collective-permute-start | bytes 24584 | tf_op jit(solution)/shard_map/ppermute | solution.py:633
  33.7 1.0 %copy-start.1 = (f32[3,64,512]{2,1,0:T(8,128)S(1)}, f32[3,64,512]{2,1,0:T(8,128)}, u32[]{:S(2)}) copy-start(f32[3,64,512]{2,1,0:T(8,128)} %copy-done) | copy-start | bytes 1179652
  34.7 0.9 copy-start.4
  35.6 1.0 %copy-start.12 = (f32[3,64,512]{2,1,0:T(8,128)S(1)}, f32[3,64,512]{2,1,0:T(8,128)}, u32[]{:S(2)}) copy-start(f32[3,64,512]{2,1,0:T(8,128)} %copy-done.11) | copy-start | bytes 1179652
  36.6 1.0 %copy-start.14 = (f32[3,64,512]{2,1,0:T(8,128)S(1)}, f32[3,64,512]{2,1,0:T(8,128)}, u32[]{:S(2)}) copy-start(f32[3,64,512]{2,1,0:T(8,128)} %copy-done.13) | copy-start | bytes 1179652
  39.9 0.9 copy-start.41
  48.8 1.0 %copy-start.2 = (f32[3,64,512]{2,1,0:T(8,128)S(1)}, f32[3,64,512]{2,1,0:T(8,128)}, u32[]{:S(2)}) copy-start(f32[3,64,512]{2,1,0:T(8,128)} %copy-done) | copy-start | bytes 1179652
  49.8 0.9 copy-start.5
  50.8 0.9 copy-start.7
  54.7 0.9 copy-start.29
  55.6 0.9 copy-start.31
  56.5 0.9 copy-start.33
  57.4 0.9 copy-start.44
  69.1 15.4 %all-to-all-start.1 = ((f32[32,8,128]{2,1,0:T(8,128)}), f32[32,8,128]{2,1,0:T(8,128)S(1)}, u32[]{:S(2)}, u32[]{:S(2)}) async-start(f32[32,8,128]{2,1,0:T(8,128)} %bitcast.5), calls=%async_computation.1 | async-start | bytes 262144 | tf_op jit(solution)/shard_map/all_to_all | solution.py:630
  76.8 4.6 %collective-permute-start.2 = (f32[64,128]{1,0:T(8,128)}, f32[64,128]{1,0:T(8,128)S(1)}, u32[]{:S(2)}, u32[]{:S(2)}) collective-permute-start(f32[64,128]{1,0:T(8,128)} %copy-done.61), channel_id=1, source_target_pairs={{0,32},{32,64},{64,96},{96,128},{128,160},{160,192},{192,224},{224... | collective-permute-start | bytes 98312 | tf_op jit(solution)/shard_map/ppermute | solution.py:632
  76.9 5.1 %collective-permute-start.3 = (f32[64,128]{1,0:T(8,128)}, f32[64,128]{1,0:T(8,128)S(1)}, u32[]{:S(2)}, u32[]{:S(2)}) collective-permute-start(f32[64,128]{1,0:T(8,128)} %copy-done.60), channel_id=1, source_target_pairs={{32,0},{64,32},{96,64},{128,96},{160,128},{192,160},{224,192},{0,2... | collective-permute-start | bytes 98312 | tf_op jit(solution)/shard_map/ppermute | solution.py:633
  84.5 0.9 copy-start.8
  85.4 1.0 %copy-start.10 = (f32[3,64,512]{2,1,0:T(8,128)S(1)}, f32[3,64,512]{2,1,0:T(8,128)}, u32[]{:S(2)}) copy-start(f32[3,64,512]{2,1,0:T(8,128)} %copy-done.9) | copy-start | bytes 1179652
  87.9 0.9 copy-start.35
  88.8 0.9 copy-start.37
  89.7 0.9 copy-start.39
  (46 other events, 31.0 us)

commit v3 on v2

--- a/solution.py
+++ b/solution.py
@@ -248,6 +248,13 @@
             spread = jnp.broadcast_to(part.astype(F32), (hi_count, 1024))
             parts.append(jnp.where(mask, spread, 0.0).astype(BF16))
     return dot_nt(jnp.concatenate(parts, axis=0), lows)
+
+
+def build_lows(slo_ref, flo_ref, slow_ref, flow_ref):
+    for g in range(8):
+        slow_ref[:, lanes_of(g)] = one_hot(block_row(slo_ref[rows_of(g), :]), 128)
+    for g in range(4):
+        flow_ref[:, lanes_of(g)] = one_hot(block_row(flo_ref[rows_of(g), :]), 128)
 
 
 def lanes_of(g):
@@ -393,7 +400,7 @@
     return table_s, table_f
 
 
-def side_lists(table_s, peer_ref, slot_ref, node_ref, counts, shi_ref, slow_ref):
+def side_lists(table_s, peer_ref, slot_ref, node_ref, counts, shi_ref, slo_ref):
     total = None
     for g in range(8):
         at = lanes_of(g)
@@ -406,26 +413,26 @@
     limit = jnp.sum(jnp.where(iota((64, 32), 1) == (iota((64, 32), 0) >> 1), counts, 0), axis=1, keepdims=True)
     slots = (iota((64, 128), 0) & 1) * 128 + iota((64, 128), 1)
     shi_ref[...] = jnp.where(slots < limit, row, -1)
-    for g in range(8):
-        slow_ref[:, lanes_of(g)] = one_hot(block_row(lane[rows_of(g)]), 128)
-
-
-def face_lists(table_f, axial_ref, coded_ref, fhi_ref, flow_ref):
+    slo_ref[...] = lane
+
+
+def face_lists(table_f, axial_ref, coded_ref, fhi_ref, flo_ref):
     for g in range(4):
         put_rows(coded_ref, 8 * g, look_up(table_f, axial_ref[0, g // 2 : g // 2 + 1, lanes_of(g % 2)]))
     row, lane = decode(coded_ref[...], 64)
     fhi_ref[...] = row
-    for g in range(4):
-        flow_ref[:, lanes_of(g)] = one_hot(block_row(lane[rows_of(g)]), 128)
+    flo_ref[...] = lane
 
 
 def first_kernel(*refs):
     (conn_h, peer_h, slot_h, node_h, counts_h, axial_h, pressure_h, geom_h, fwd_h, bwd_h, coef_h) = refs[:11]
     later_h = refs[11:17]
-    (msg_ref, up_ref, down_ref, w_ref, shi_ref, fhi_ref, slow_ref, flow_ref, perm_ref, back_ref) = refs[17:27]
+    (msg_ref, up_ref, down_ref, w_ref, shi_ref, fhi_ref, slo_ref, flo_ref, perm_ref, back_ref) = refs[17:27]
     (tab_f_ref, tab_b_ref, coef_ref, pressure_ref, geom_ref) = refs[27:32]
     later = refs[32:38]
-    (conn_ref, peer_ref, slot_ref, node_ref, counts_ref, axial_ref, fwd_ref, bwd_ref, coded_ref, sems) = refs[38:]
+    (conn_ref, peer_ref, slot_ref, node_ref, counts_ref, axial_ref, fwd_ref, bwd_ref, coded_ref, slow_ref, flow_ref, sems) = (
+        refs[38:]
+    )
     pairs = [
         (conn_h, conn_ref), (pressure_h, pressure_ref), (fwd_h, fwd_ref), (bwd_h, bwd_ref), (coef_h, coef_ref),
         (geom_h, geom_ref), (node_h, node_ref), (peer_h, peer_ref), (slot_h, slot_ref), (counts_h, counts_ref),
@@ -449,8 +456,9 @@
     w = permute(perm_ref[...], out)
     for c in range(4):
         w_ref[:, 128 * c : 128 * c + 128] = w[c]
-    side_lists(table_s, peer_ref, slot_ref, node_ref, counts_ref[...], shi_ref, slow_ref)
-    face_lists(table_f, axial_ref, coded_ref, fhi_ref, flow_ref)
+    side_lists(table_s, peer_ref, slot_ref, node_ref, counts_ref[...], shi_ref, slo_ref)
+    face_lists(table_f, axial_ref, coded_ref, fhi_ref, flo_ref)
+    build_lows(slo_ref, flo_ref, slow_ref, flow_ref)
     send_values([assemble_local(w)], shi_ref, fhi_ref, slow_ref, flow_ref, msg_ref, up_ref, down_ref, 2)
     for copy in copies[11:]:
         copy.wait()
@@ -458,9 +466,11 @@
 
 def momentum_kernel(
     velocity_ref, force_ref, mass_ref, metric_ref, geom_ref, tab_f_ref, tab_b_ref, coef_ref, perm_ref, shi_ref, fhi_ref,
+    slo_ref, flo_ref,
+    msg_ref, up_ref, down_ref, w_ref,
     slow_ref, flow_ref,
-    msg_ref, up_ref, down_ref, w_ref,
 ):
+    build_lows(slo_ref, flo_ref, slow_ref, flow_ref)
     parts = [chunks_of(velocity_ref[a]) for a in range(3)]
     stacked = [jnp.concatenate([parts[a][c] for a in range(3)], axis=0) for c in range(4)]
     grad = grads(stacked, tab_f_ref, coef_ref)
@@ -495,9 +505,11 @@
 
 def second_kernel(
     msg_in_ref, low_ref, upp_ref, w_in_ref, pressure_ref, rhs_ref, jacobi_ref, geom_ref, tab_f_ref, tab_b_ref, coef_ref,
-    perm_ref, back_ref, shi_ref, fhi_ref, slow_ref, flow_ref, msg_m_ref, up_m_ref, down_m_ref,
+    perm_ref, back_ref, shi_ref, fhi_ref, slo_ref, flo_ref, msg_m_ref, up_m_ref, down_m_ref,
     msg_ref, up_ref, down_ref, w_ref, base_ref, res_ref,
+    slow_ref, flow_ref,
 ):
+    build_lows(slo_ref, flo_ref, slow_ref, flow_ref)
     sides, faces = take_values(1, shi_ref, fhi_ref, slow_ref, flow_ref, msg_in_ref, low_ref, upp_ref, 2)
     w = add_back(chunks_of(w_in_ref[...]), sides[0], faces[0])
     applied = permute(back_ref[...], assemble_local(w))
@@ -522,11 +534,12 @@
 
 
 def last_kernel(
-    msg_in_ref, low_ref, upp_ref, w_in_ref, w_m_ref, jacobi_ref, base_ref, res_ref, back_ref, shi_ref, fhi_ref, slow_ref,
-    flow_ref,
+    msg_in_ref, low_ref, upp_ref, w_in_ref, w_m_ref, jacobi_ref, base_ref, res_ref, back_ref, shi_ref, fhi_ref, slo_ref,
+    flo_ref,
     pressure_h, momentum_h,
-    out_ref, sems,
+    out_ref, slow_ref, flow_ref, sems,
 ):
+    build_lows(slo_ref, flo_ref, slow_ref, flow_ref)
     sides, faces = take_values(4, shi_ref, fhi_ref, slow_ref, flow_ref, msg_in_ref, low_ref, upp_ref, 8)
     copies = []
     for f in range(4):
@@ -574,6 +587,10 @@
     )(*args)
 
 
+def lows():
+    return [pltpu.VMEM((128, 8192), BF16), pltpu.VMEM((128, 4096), BF16)]
+
+
 def like(x):
     return jax.ShapeDtypeStruct(x.shape, x.dtype)
 
@@ -584,11 +601,11 @@
     outs = call(
         first_kernel,
         [shape(64, 128), shape(16, 128), shape(16, 128), shape(64, 512), shape(64, 128, dtype=I32),
-         shape(32, 128, dtype=I32), shape(128, 8192, dtype=BF16), shape(128, 4096, dtype=BF16),
+         shape(32, 128, dtype=I32), shape(64, 128, dtype=I32), shape(32, 128, dtype=I32),
          shape(64, 192, dtype=BF16), shape(64, 192, dtype=BF16), shape(768, 256, dtype=BF16), shape(768, 128, dtype=BF16),
          like(coef), like(pressure), like(geom), *[like(x) for x in later]],
         [conn, peer, slot, node, counts, axial, pressure, geom, fwd, bwd, coef, *later],
-        [*[pltpu.VMEM(x.shape, x.dtype) for x in held], pltpu.VMEM((32, 128), F32),
+        [*[pltpu.VMEM(x.shape, x.dtype) for x in held], pltpu.VMEM((32, 128), F32), *lows(),
          pltpu.SemaphoreType.DMA((11 + len(later),))],
         "first",
         args_hbm=True,
@@ -601,6 +618,7 @@
         momentum_kernel,
         [shape(192, 128), shape(48, 128), shape(48, 128), shape(3, 64, 512)],
         [velocity, force, mass, metric, geom, *tables, perm, *lists],
+        lows(),
         name="momentum",
     )
 
@@ -610,6 +628,7 @@
         second_kernel,
         [shape(256, 128), shape(64, 128), shape(64, 128), shape(64, 512), shape(64, 512), shape(64, 512)],
         [msg, low, upp, w, pressure, rhs, jacobi, geom, *tables, perm, back, *lists, msg_m, up_m, down_m],
+        lows(),
         name="second",
     )
 
@@ -619,7 +638,7 @@
         last_kernel,
         [shape(64, 512), shape(3, 64, 512)],
         [msg, low, upp, w, w_m, jacobi, base, res, back, *lists],
-        [pltpu.VMEM((4, 64, 512), F32), pltpu.SemaphoreType.DMA((4,))],
+        [pltpu.VMEM((4, 64, 512), F32), *lows(), pltpu.SemaphoreType.DMA((4,))],
         name="last",
         outs_hbm=True,
     )

time: 97.5 us -> 50.2 us (0.51); the launches traced: 95.8 us -> 50 us
  local copies, waits for them, and re-layouts: 47.6 us -> 0 us
  waiting for transfers between devices: 3.73 us -> 4.95 us
    unnamed x128 -> x0, local copies, waits for them, and re-layouts: 47.6 us -> none
    all_to_all x2, waiting for transfers between devices: 1.92 us -> 3.35 us  [exchange(): lax.all_to_all(msg.reshape(32, rows, 128), ('gy', 'gz'), split_axis=0, co...]
  transfers between devices with their start and end apart: 6 -> 6, of which waited for: 2 -> 2; matrix products, arithmetic and copies ran while one was open for 0% -> 0% of each run, Pallas kernels for 4% -> 8%
where the time goes in v3:
time: 50.2 us; the launch traced here: 50 us
  starting transfers between devices  24.9 us (50%)
  Pallas kernels  19.2 us (38%)
  waiting for transfers between devices  4.95 us (10%)
  between operations  0.86 us (2%)
    pallas_call x4, Pallas kernels, call(): pl.pallas_call(kernel, out_shape=outs, in_specs=[in_hbm() if args_hbm els...  19.2 us
    all_to_all x2, starting transfers between devices, exchange(): lax.all_to_all(msg.reshape(32, rows, 128), ('gy', 'gz'), split_axis=0, co...  16.3 us
    ppermute x2, starting transfers between devices, exchange(): lax.ppermute(down, 'gx', [((i + 1) % count, i) for i in range(count)])  6.87 us
    all_to_all x2, waiting for transfers between devices, exchange(): lax.all_to_all(msg.reshape(32, rows, 128), ('gy', 'gz'), split_axis=0, co...  3.35 us
    ppermute x2, starting transfers between devices, exchange(): lax.ppermute(up, 'gx', [(i, (i + 1) % count) for i in range(count)])  1.79 us
    ppermute x2, waiting for transfers between devices, exchange(): lax.ppermute(up, 'gx', [(i, (i + 1) % count) for i in range(count)])  1.6 us
  transfers between devices with their start and end apart: 6, of which 2 were waited for; matrix products, arithmetic and copies ran while one was open for 0% of the time, Pallas kernels for 8%

profile of v3, /device:TPU:1, one launch (start us, length us, event | category | flops | bytes accessed | tf_op | source)
XLA Modules:
  0.0 50.0 jit_solution(16345635965495602844)
XLA Ops:
  0.6 7.8 %first.1 = (f32[64,128]{1,0:T(8,128)}, f32[16,128]{1,0:T(8,128)S(1)}, f32[16,128]{1,0:T(8,128)S(1)}, f32[64,512]{1,0:T(8,128)S(1)}, s32[64,128]{1,0:T(8,128)S(1)...) custom-call(s32[64,512]{1,0:T(8,128)} %refs_0_.1, ...), custom_call_target="tpu_custom_call" | custom-call | tf_op jit(solution)/shard_map/first/pallas_call | solution.py:579
  8.4 8.6 %all-to-all-start = ((f32[32,2,128]{2,1,0:T(2,128)}), f32[32,2,128]{2,1,0:T(2,128)S(1)}, u32[]{:S(2)}, u32[]{:S(2)}) async-start(f32[32,2,128]{2,1,0:T(2,128)} %bitcast), calls=%async_computation | async-start | bytes 65536 | tf_op jit(solution)/shard_map/all_to_all | solution.py:649
  17.0 1.7 %collective-permute-start = (f32[16,128]{1,0:T(8,128)S(1)}, f32[16,128]{1,0:T(8,128)S(1)}, u32[]{:S(2)}, u32[]{:S(2)}) collective-permute-start(f32[16,128]{1,0:T(8,128)S(1)} %get-tuple-element.34), channel_id=1, source_target_pairs={{0,32},{32,64},{64,96},{96,128},{128,160},{160,192},{192,224},{224... | collective-permute-start | bytes 24584 | tf_op jit(solution)/shard_map/ppermute | solution.py:651
  18.7 4.2 %collective-permute-start.1 = (f32[16,128]{1,0:T(8,128)S(1)}, f32[16,128]{1,0:T(8,128)S(1)}, u32[]{:S(2)}, u32[]{:S(2)}) collective-permute-start(f32[16,128]{1,0:T(8,128)S(1)} %get-tuple-element.35), channel_id=1, source_target_pairs={{32,0},{64,32},{96,64},{128,96},{160,128},{192,160},{224,192},{0,2... | collective-permute-start | bytes 24584 | tf_op jit(solution)/shard_map/ppermute | solution.py:652
  22.9 3.9 %momentum.1 = (f32[192,128]{1,0:T(8,128)S(1)}, f32[48,128]{1,0:T(8,128)S(1)}, f32[48,128]{1,0:T(8,128)S(1)}, f32[3,64,512]{2,1,0:T(8,128)S(1)}) custom-call(f32[3,64,512]{2,1,0:T(8,128)S(1)} %get-tuple-element.50.velocity_ref, f32[3,64,512]{2,1,0:T(8,128)S(1)} %get-tuple-element.51.force_ref, f32[64,512]{1,0:T(8,128)S(1)} %get-tuple-element.52.mass_ref, ...), custom_call_target="tpu_custom_call" | custom-call | tf_op jit(solution)/shard_map/momentum/pallas_call | solution.py:579
  26.8 0.0 collective-permute-done.low_ref
  26.8 0.0 collective-permute-done.1.upp_ref
  26.8 0.0 all-to-all-done
  26.8 4.1 %second.1 = (f32[256,128]{1,0:T(8,128)}, f32[64,128]{1,0:T(8,128)S(1)}, f32[64,128]{1,0:T(8,128)S(1)}, f32[64,512]{1,0:T(8,128)S(1)}, f32[64,512]{1,0:T(8,128)S(1)}, /*index=5*/f32[64,512]{1,0:T(8,128)S(1)}) custom-call(f32[64,128]{1,0:T(8,128)S(1)} %bitcast.5, f32[16,128]{1,0:T(8,128)S(1)} %collective-permute-done.low_ref, ...), custom_call_target="tpu_custom_call" | custom-call | tf_op jit(solution)/shard_map/second/pallas_call | solution.py:579
  31.0 7.7 %all-to-all-start.1 = ((f32[32,8,128]{2,1,0:T(8,128)}), f32[32,8,128]{2,1,0:T(8,128)S(1)}, u32[]{:S(2)}, u32[]{:S(2)}) async-start(f32[32,8,128]{2,1,0:T(8,128)} %bitcast.2), calls=%async_computation.1 | async-start | bytes 262144 | tf_op jit(solution)/shard_map/all_to_all | solution.py:649
  38.7 0.1 collective-permute-start.2
  38.8 2.7 %collective-permute-start.3 = (f32[64,128]{1,0:T(8,128)S(1)}, f32[64,128]{1,0:T(8,128)S(1)}, u32[]{:S(2)}, u32[]{:S(2)}) collective-permute-start(f32[64,128]{1,0:T(8,128)S(1)} %get-tuple-element.59), channel_id=1, source_target_pairs={{32,0},{64,32},{96,64},{128,96},{160,128},{192,160},{224,192},{0,2... | collective-permute-start | bytes 98312 | tf_op jit(solution)/shard_map/ppermute | solution.py:652
  41.4 1.6 %collective-permute-done.2.low_ref = f32[64,128]{1,0:T(8,128)S(1)} collective-permute-done((f32[64,128]{1,0:T(8,128)S(1)}, f32[64,128]{1,0:T(8,128)S(1)}, u32[]{:S(2)}, u32[]{:S(2)}) %collective-permute-start.2) | collective-permute-done | bytes 32800 | tf_op jit(solution)/shard_map/ppermute | solution.py:651
  43.0 0.0 collective-permute-done.3.upp_ref
  43.0 3.4 %all-to-all-done.1 = f32[32,8,128]{2,1,0:T(8,128)S(1)} async-done(((f32[32,8,128]{2,1,0:T(8,128)}), f32[32,8,128]{2,1,0:T(8,128)S(1)}, u32[]{:S(2)}, u32[]{:S(2)}) %all-to-all-start.1) | async-done | bytes 131104 | tf_op jit(solution)/shard_map/all_to_all | solution.py:649
  46.4 3.4 %last.1 = (f32[64,512]{1,0:T(8,128)}, f32[3,64,512]{2,1,0:T(8,128)}) custom-call(f32[256,128]{1,0:T(8,128)S(1)} %bitcast.4, f32[64,128]{1,0:T(8,128)S(1)} %collective-permute-done.2.low_ref, f32[64,128]{1,0:T(8,128)S(1)} %collective-permute-done.3.upp_ref, f32[64,512]{1,0:T(8,128)S(1)} %get-tuple-element.60.w_in_ref, ...), custom_call_target="tpu_custom_call" | custom-call | tf_op jit(solution)/shard_map/last/pallas_call | solution.py:579
Async XLA Ops:
  8.4 18.4 %all-to-all-start = ((f32[32,2,128]{2,1,0:T(2,128)}), f32[32,2,128]{2,1,0:T(2,128)S(1)}, u32[]{:S(2)}, u32[]{:S(2)}) async-start(f32[32,2,128]{2,1,0:T(2,128)} %bitcast), calls=%async_computation | async-start | bytes 65536 | tf_op jit(solution)/shard_map/all_to_all | solution.py:649
  17.0 9.8 %collective-permute-start = (f32[16,128]{1,0:T(8,128)S(1)}, f32[16,128]{1,0:T(8,128)S(1)}, u32[]{:S(2)}, u32[]{:S(2)}) collective-permute-start(f32[16,128]{1,0:T(8,128)S(1)} %get-tuple-element.34), channel_id=1, source_target_pairs={{0,32},{32,64},{64,96},{96,128},{128,160},{160,192},{192,224},{224... | collective-permute-start | bytes 24584 | tf_op jit(solution)/shard_map/ppermute | solution.py:651
  18.7 8.1 %collective-permute-start.1 = (f32[16,128]{1,0:T(8,128)S(1)}, f32[16,128]{1,0:T(8,128)S(1)}, u32[]{:S(2)}, u32[]{:S(2)}) collective-permute-start(f32[16,128]{1,0:T(8,128)S(1)} %get-tuple-element.35), channel_id=1, source_target_pairs={{32,0},{64,32},{96,64},{128,96},{160,128},{192,160},{224,192},{0,2... | collective-permute-start | bytes 24584 | tf_op jit(solution)/shard_map/ppermute | solution.py:652
  31.0 15.4 %all-to-all-start.1 = ((f32[32,8,128]{2,1,0:T(8,128)}), f32[32,8,128]{2,1,0:T(8,128)S(1)}, u32[]{:S(2)}, u32[]{:S(2)}) async-start(f32[32,8,128]{2,1,0:T(8,128)} %bitcast.2), calls=%async_computation.1 | async-start | bytes 262144 | tf_op jit(solution)/shard_map/all_to_all | solution.py:649
  38.7 4.3 %collective-permute-start.2 = (f32[64,128]{1,0:T(8,128)S(1)}, f32[64,128]{1,0:T(8,128)S(1)}, u32[]{:S(2)}, u32[]{:S(2)}) collective-permute-start(f32[64,128]{1,0:T(8,128)S(1)} %get-tuple-element.58), channel_id=1, source_target_pairs={{0,32},{32,64},{64,96},{96,128},{128,160},{160,192},{192,224},{224... | collective-permute-start | bytes 98312 | tf_op jit(solution)/shard_map/ppermute | solution.py:651
  38.8 4.3 %collective-permute-start.3 = (f32[64,128]{1,0:T(8,128)S(1)}, f32[64,128]{1,0:T(8,128)S(1)}, u32[]{:S(2)}, u32[]{:S(2)}) collective-permute-start(f32[64,128]{1,0:T(8,128)S(1)} %get-tuple-element.59), channel_id=1, source_target_pairs={{32,0},{64,32},{96,64},{128,96},{160,128},{192,160},{224,192},{0,2... | collective-permute-start | bytes 98312 | tf_op jit(solution)/shard_map/ppermute | solution.py:652

commit v4 on v3

--- a/solution.py
+++ b/solution.py
@@ -88,8 +88,22 @@
     return lax.dot_general(a, b, (((1,), (1,)), ((), ())), preferred_element_type=F32)
 
 
+def repeat_row(row, count):
+    pair = jnp.broadcast_to(row.astype(F32), (16, row.shape[1])).astype(BF16)
+    return jnp.concatenate([pair] * (count // 16), axis=0)
+
+
+def marks(row, count):
+    base = iota((count, 128), 0).astype(F32).astype(BF16)
+    return jnp.concatenate([base] * (row.shape[1] // 128), axis=1) == repeat_row(row, count)
+
+
+def choose(mask, value):
+    return jnp.where(mask, value, jnp.zeros(mask.shape, BF16))
+
+
 def one_hot(row, count):
-    return (iota((count, row.shape[1]), 0) == row).astype(F32).astype(BF16)
+    return choose(marks(row, count), jnp.ones((count, row.shape[1]), BF16))
 
 
 def chunks_of(x):
@@ -191,12 +205,17 @@
 
 
 def pack_faces(w):
-    kk = iota((64, 128), 1) & 7
-    face = jnp.zeros((64, 128), F32)
-    for c in range(4):
-        face = jnp.where(kk == 2 * c, pltpu.roll(w[c], 2 * c, 1), face)
-        face = jnp.where(kk == 2 * c + 1, pltpu.roll(w[c], (2 * c - 6) % 128, 1), face)
-    return face
+    kk = iota((32, 128), 1) & 7
+    faces = []
+    for k in (0, 7):
+        face = jnp.zeros((32, 128), F32)
+        for c in range(4):
+            for h in range(2):
+                face = jnp.where(
+                    kk == 4 * h + c, pltpu.roll(w[c][32 * h : 32 * h + 32], (4 * h + c - k) % 128, 1), face
+                )
+        faces.append(face)
+    return faces
 
 
 def add_back(w, side, face):
@@ -215,8 +234,9 @@
             x = x + jnp.where((sub == 0) & (lane < 64), x_rows, 0.0)
         if c == 3:
             x = x + jnp.where((sub == 7) & (lane >= 64), x_rows, 0.0)
-        x = x + jnp.where(kk == 0, pltpu.roll(face, (-2 * c) % 128, 1), 0.0)
-        x = x + jnp.where(kk == 7, pltpu.roll(face, (6 - 2 * c) % 128, 1), 0.0)
+        for k, part in zip((0, 7), face):
+            spread = [pltpu.roll(part, (k - 4 * h - c) % 128, 1) for h in range(2)]
+            x = x + jnp.where(kk == k, jnp.concatenate(spread, axis=0), 0.0)
         first = x[0:8] + jnp.where(jj == 0, pltpu.roll(y_side, (-16 * c) % 128, 1), 0.0)
         last = x[56:64] + jnp.where(jj == 7, pltpu.roll(y_side, (48 - 16 * c) % 128, 1), 0.0)
         out.append(jnp.concatenate([first, x[8:56], last], axis=0))
@@ -241,12 +261,11 @@
 
 
 def scatter_tables(rows, hi_block, lows, hi_count):
-    mask = iota((hi_count, 1024), 0) == block_row(hi_block)
+    mask = marks(block_row(hi_block), hi_count)
     parts = []
     for values in rows:
         for part in split(values, 2):
-            spread = jnp.broadcast_to(part.astype(F32), (hi_count, 1024))
-            parts.append(jnp.where(mask, spread, 0.0).astype(BF16))
+            parts.append(choose(mask, repeat_row(part, hi_count)))
     return dot_nt(jnp.concatenate(parts, axis=0), lows)
 
 
@@ -275,7 +294,7 @@
                 at = (8 * g + t) // 2 * stride + 2 * f + t % 2
                 msg_ref[at : at + 1, :] = values[:, 128 * t : 128 * t + 128]
     for g in range(4):
-        got = gather_tables(faces, fhi_ref[rows_of(g), :], flow_ref[:, lanes_of(g)], 64)
+        got = gather_tables([f[g // 2] for f in faces], fhi_ref[rows_of(g), :], flow_ref[:, lanes_of(g)], 32)
         out_ref = down_ref if g < 2 else up_ref
         for f, values in enumerate(got):
             for t in range(8):
@@ -295,14 +314,14 @@
             rows.append(jnp.concatenate(cells, axis=1))
         part = scatter_tables(rows, shi_ref[rows_of(g), :], slow_ref[:, lanes_of(g)], 16)
         side = part if side is None else side + part
-    face = None
+    face = [None, None]
     for g in range(4):
         ref = low_ref if g < 2 else upp_ref
         rows = [block_row(ref[16 * f + 8 * (g % 2) : 16 * f + 8 * (g % 2) + 8, :]) for f in range(count)]
-        part = scatter_tables(rows, fhi_ref[rows_of(g), :], flow_ref[:, lanes_of(g)], 64)
-        face = part if face is None else face + part
+        part = scatter_tables(rows, fhi_ref[rows_of(g), :], flow_ref[:, lanes_of(g)], 32)
+        face[g // 2] = part if face[g // 2] is None else face[g // 2] + part
     sides = [side[32 * f : 32 * f + 16] + side[32 * f + 16 : 32 * f + 32] for f in range(count)]
-    faces = [face[128 * f : 128 * f + 64] + face[128 * f + 64 : 128 * f + 128] for f in range(count)]
+    faces = [[x[64 * f : 64 * f + 32] + x[64 * f + 32 : 64 * f + 64] for x in face] for f in range(count)]
     return sides, faces
 
 
@@ -332,14 +351,14 @@
 
 
 def place_table(hi, lo, count):
-    lane = 1.0 + iota((128, 128), 1).astype(F32) * (1.0 / 128.0)
+    lane = 1.0 + iota((1, 128), 1).astype(F32) * (1.0 / 128.0)
     total = None
     for g in range(count // 8):
         top = one_hot(block_row(hi[rows_of(g)]), HI)
         low = []
         for t in range(8):
-            hit = iota((128, 128), 0) == lo[8 * g + t : 8 * g + t + 1]
-            low.append(jnp.where(hit, lane * (2.0 ** (8 * g + t - count // 2)), 0.0).astype(BF16))
+            hit = marks(lo[8 * g + t : 8 * g + t + 1], 128)
+            low.append(choose(hit, repeat_row(lane * (2.0 ** (8 * g + t - count // 2)), 128)))
         part = dot_nt(jnp.concatenate(low, axis=1), top)
         total = part if total is None else total + part
     return total.astype(BF16)
@@ -387,17 +406,18 @@
     i_y = 2 * (((lane8 >> 3) & 7) >> 1) + (lane8 >> 6)
     in_y = (i_y < 7) & ((row8 > 8) | (i_y > 0))
     keep_s = ((row8 < 8) & in_x) | ((row8 >= 8) & in_y)
-    lane = iota((64, 128), 1)
-    row = iota((64, 128), 0)
-    i_f = 2 * ((lane & 7) >> 1) + (lane >> 6)
+    lane = iota((32, 128), 1)
+    row = iota((32, 128), 0) + 32 * ((lane >> 2) & 1)
+    i_f = 2 * (lane & 3) + (lane >> 6)
     keep_f = ((i_f < 7) | ((row & 7) == 7)) & ((((lane >> 3) & 7) < 7) | ((row >> 3) == 7))
     table_s = place_table(
         jnp.where(keep_s, pack_sides(hi_c), -1.0).astype(I32), pack_sides(lo_c).astype(I32), 16
     )
-    table_f = place_table(
-        jnp.where(keep_f, pack_faces(hi_c), -1.0).astype(I32), pack_faces(lo_c).astype(I32), 64
-    )
-    return table_s, table_f
+    tables_f = [
+        place_table(jnp.where(keep_f, hi, -1.0).astype(I32), lo.astype(I32), 32)
+        for hi, lo in zip(pack_faces(hi_c), pack_faces(lo_c))
+    ]
+    return table_s, tables_f
 
 
 def side_lists(table_s, peer_ref, slot_ref, node_ref, counts, shi_ref, slo_ref):
@@ -406,8 +426,8 @@
         at = lanes_of(g)
         slot = slot_ref[:, at]
         places = look_up(table_s, node_ref[:, at])
-        hit = iota((64, 1024), 0) == (peer_ref[:, at] * 2 + (slot >> 7))
-        part = dot_nt(jnp.where(hit, places, 0.0).astype(BF16), one_hot(slot & 127, 128))
+        hit = marks(peer_ref[:, at] * 2 + (slot >> 7), 64)
+        part = dot_nt(choose(hit, repeat_row(places, 64)), one_hot(slot & 127, 128))
         total = part if total is None else total + part
     row, lane = decode(total, 16)
     limit = jnp.sum(jnp.where(iota((64, 32), 1) == (iota((64, 32), 0) >> 1), counts, 0), axis=1, keepdims=True)
@@ -416,10 +436,10 @@
     slo_ref[...] = lane
 
 
-def face_lists(table_f, axial_ref, coded_ref, fhi_ref, flo_ref):
+def face_lists(tables_f, axial_ref, coded_ref, fhi_ref, flo_ref):
     for g in range(4):
-        put_rows(coded_ref, 8 * g, look_up(table_f, axial_ref[0, g // 2 : g // 2 + 1, lanes_of(g % 2)]))
-    row, lane = decode(coded_ref[...], 64)
+        put_rows(coded_ref, 8 * g, look_up(tables_f[g // 2], axial_ref[0, g // 2 : g // 2 + 1, lanes_of(g % 2)]))
+    row, lane = decode(coded_ref[...], 32)
     fhi_ref[...] = row
     flo_ref[...] = lane
 
@@ -451,13 +471,13 @@
         tab_f_ref[128 * at : 128 * at + 128, :] = part
     for at, part in enumerate(split(bwd_ref[...], 3)):
         tab_b_ref[256 * at : 256 * at + 256, :] = part
-    table_s, table_f = node_places(conn, perm_ref[:, 0:64])
+    table_s, tables_f = node_places(conn, perm_ref[:, 0:64])
     out = laplace(chunks_of(pressure_ref[...]), geom_ref, tab_f_ref, tab_b_ref, coef_ref)
     w = permute(perm_ref[...], out)
     for c in range(4):
         w_ref[:, 128 * c : 128 * c + 128] = w[c]
     side_lists(table_s, peer_ref, slot_ref, node_ref, counts_ref[...], shi_ref, slo_ref)
-    face_lists(table_f, axial_ref, coded_ref, fhi_ref, flo_ref)
+    face_lists(tables_f, axial_ref, coded_ref, fhi_ref, flo_ref)
     build_lows(slo_ref, flo_ref, slow_ref, flow_ref)
     send_values([assemble_local(w)], shi_ref, fhi_ref, slow_ref, flow_ref, msg_ref, up_ref, down_ref, 2)
     for copy in copies[11:]:

time: 50.2 us -> 47.4 us (0.944)
  Pallas kernels: 19.2 us -> 16.6 us
    pallas_call x4, Pallas kernels: 19.2 us -> 16.6 us  [call(): pl.pallas_call(kernel, out_shape=outs, in_specs=[in_hbm() if args_hbm els...]
  transfers between devices with their start and end apart: 6 -> 6, of which waited for: 2 -> 2; matrix products, arithmetic and copies ran while one was open for 0% -> 0% of each run, Pallas kernels for 8% -> 7%
where the time goes in v4:
time: 47.4 us; the launch traced here: 47.2 us
  starting transfers between devices  24.9 us (53%)
  Pallas kernels  16.6 us (35%)
  waiting for transfers between devices  4.77 us (10%)
  between operations  0.86 us (2%)
    pallas_call x4, Pallas kernels, call(): pl.pallas_call(kernel, out_shape=outs, in_specs=[in_hbm() if args_hbm els...  16.6 us
    all_to_all x2, starting transfers between devices, exchange(): lax.all_to_all(msg.reshape(32, rows, 128), ('gy', 'gz'), split_axis=0, co...  16.3 us
    ppermute x2, starting transfers between devices, exchange(): lax.ppermute(down, 'gx', [((i + 1) % count, i) for i in range(count)])  6.69 us
    all_to_all x2, waiting for transfers between devices, exchange(): lax.all_to_all(msg.reshape(32, rows, 128), ('gy', 'gz'), split_axis=0, co...  3.17 us
    ppermute x2, starting transfers between devices, exchange(): lax.ppermute(up, 'gx', [(i, (i + 1) % count) for i in range(count)])  1.98 us
    ppermute x2, waiting for transfers between devices, exchange(): lax.ppermute(up, 'gx', [(i, (i + 1) % count) for i in range(count)])  1.6 us
  transfers between devices with their start and end apart: 6, of which 2 were waited for; matrix products, arithmetic and copies ran while one was open for 0% of the time, Pallas kernels for 7%

profile of v4, /device:TPU:1, one launch (start us, length us, event | category | flops | bytes accessed | tf_op | source)
XLA Modules:
  0.0 47.2 jit_solution(6499486011169822920)
XLA Ops:
  0.6 6.7 %first.1 = (f32[64,128]{1,0:T(8,128)}, f32[16,128]{1,0:T(8,128)S(1)}, f32[16,128]{1,0:T(8,128)S(1)}, f32[64,512]{1,0:T(8,128)S(1)}, s32[64,128]{1,0:T(8,128)S(1)...) custom-call(s32[64,512]{1,0:T(8,128)} %refs_0_.1, ...), custom_call_target="tpu_custom_call" | custom-call | tf_op jit(solution)/shard_map/first/pallas_call | solution.py:599
  7.3 8.6 %all-to-all-start = ((f32[32,2,128]{2,1,0:T(2,128)}), f32[32,2,128]{2,1,0:T(2,128)S(1)}, u32[]{:S(2)}, u32[]{:S(2)}) async-start(f32[32,2,128]{2,1,0:T(2,128)} %bitcast), calls=%async_computation | async-start | bytes 65536 | tf_op jit(solution)/shard_map/all_to_all | solution.py:669
  15.9 1.7 %collective-permute-start = (f32[16,128]{1,0:T(8,128)S(1)}, f32[16,128]{1,0:T(8,128)S(1)}, u32[]{:S(2)}, u32[]{:S(2)}) collective-permute-start(f32[16,128]{1,0:T(8,128)S(1)} %get-tuple-element.34), channel_id=1, source_target_pairs={{0,32},{32,64},{64,96},{96,128},{128,160},{160,192},{192,224},{224... | collective-permute-start | bytes 24584 | tf_op jit(solution)/shard_map/ppermute | solution.py:671
  17.6 4.0 %collective-permute-start.1 = (f32[16,128]{1,0:T(8,128)S(1)}, f32[16,128]{1,0:T(8,128)S(1)}, u32[]{:S(2)}, u32[]{:S(2)}) collective-permute-start(f32[16,128]{1,0:T(8,128)S(1)} %get-tuple-element.35), channel_id=1, source_target_pairs={{32,0},{64,32},{96,64},{128,96},{160,128},{192,160},{224,192},{0,2... | collective-permute-start | bytes 24584 | tf_op jit(solution)/shard_map/ppermute | solution.py:672
  21.7 3.2 %momentum.1 = (f32[192,128]{1,0:T(8,128)S(1)}, f32[48,128]{1,0:T(8,128)S(1)}, f32[48,128]{1,0:T(8,128)S(1)}, f32[3,64,512]{2,1,0:T(8,128)S(1)}) custom-call(f32[3,64,512]{2,1,0:T(8,128)S(1)} %get-tuple-element.50.velocity_ref, f32[3,64,512]{2,1,0:T(8,128)S(1)} %get-tuple-element.51.force_ref, f32[64,512]{1,0:T(8,128)S(1)} %get-tuple-element.52.mass_ref, ...), custom_call_target="tpu_custom_call" | custom-call | tf_op jit(solution)/shard_map/momentum/pallas_call | solution.py:599
  24.8 0.0 collective-permute-done.low_ref
  24.9 0.0 collective-permute-done.1.upp_ref
  24.9 0.0 all-to-all-done
  24.9 3.9 %second.1 = (f32[256,128]{1,0:T(8,128)}, f32[64,128]{1,0:T(8,128)S(1)}, f32[64,128]{1,0:T(8,128)S(1)}, f32[64,512]{1,0:T(8,128)S(1)}, f32[64,512]{1,0:T(8,128)S(1)}, /*index=5*/f32[64,512]{1,0:T(8,128)S(1)}) custom-call(f32[64,128]{1,0:T(8,128)S(1)} %bitcast.5, f32[16,128]{1,0:T(8,128)S(1)} %collective-permute-done.low_ref, ...), custom_call_target="tpu_custom_call" | custom-call | tf_op jit(solution)/shard_map/second/pallas_call | solution.py:599
  28.8 7.7 %all-to-all-start.1 = ((f32[32,8,128]{2,1,0:T(8,128)}), f32[32,8,128]{2,1,0:T(8,128)S(1)}, u32[]{:S(2)}, u32[]{:S(2)}) async-start(f32[32,8,128]{2,1,0:T(8,128)} %bitcast.2), calls=%async_computation.1 | async-start | bytes 262144 | tf_op jit(solution)/shard_map/all_to_all | solution.py:669
  36.5 0.3 collective-permute-start.2
  36.8 2.7 %collective-permute-start.3 = (f32[64,128]{1,0:T(8,128)S(1)}, f32[64,128]{1,0:T(8,128)S(1)}, u32[]{:S(2)}, u32[]{:S(2)}) collective-permute-start(f32[64,128]{1,0:T(8,128)S(1)} %get-tuple-element.59), channel_id=1, source_target_pairs={{32,0},{64,32},{96,64},{128,96},{160,128},{192,160},{224,192},{0,2... | collective-permute-start | bytes 98312 | tf_op jit(solution)/shard_map/ppermute | solution.py:672
  39.4 1.6 %collective-permute-done.2.low_ref = f32[64,128]{1,0:T(8,128)S(1)} collective-permute-done((f32[64,128]{1,0:T(8,128)S(1)}, f32[64,128]{1,0:T(8,128)S(1)}, u32[]{:S(2)}, u32[]{:S(2)}) %collective-permute-start.2) | collective-permute-done | bytes 32800 | tf_op jit(solution)/shard_map/ppermute | solution.py:671
  41.0 0.0 collective-permute-done.3.upp_ref
  41.0 3.2 %all-to-all-done.1 = f32[32,8,128]{2,1,0:T(8,128)S(1)} async-done(((f32[32,8,128]{2,1,0:T(8,128)}), f32[32,8,128]{2,1,0:T(8,128)S(1)}, u32[]{:S(2)}, u32[]{:S(2)}) %all-to-all-start.1) | async-done | bytes 131104 | tf_op jit(solution)/shard_map/all_to_all | solution.py:669
  44.2 2.8 %last.1 = (f32[64,512]{1,0:T(8,128)}, f32[3,64,512]{2,1,0:T(8,128)}) custom-call(f32[256,128]{1,0:T(8,128)S(1)} %bitcast.4, f32[64,128]{1,0:T(8,128)S(1)} %collective-permute-done.2.low_ref, f32[64,128]{1,0:T(8,128)S(1)} %collective-permute-done.3.upp_ref, f32[64,512]{1,0:T(8,128)S(1)} %get-tuple-element.60.w_in_ref, ...), custom_call_target="tpu_custom_call" | custom-call | tf_op jit(solution)/shard_map/last/pallas_call | solution.py:599
Async XLA Ops:
  7.3 17.6 %all-to-all-start = ((f32[32,2,128]{2,1,0:T(2,128)}), f32[32,2,128]{2,1,0:T(2,128)S(1)}, u32[]{:S(2)}, u32[]{:S(2)}) async-start(f32[32,2,128]{2,1,0:T(2,128)} %bitcast), calls=%async_computation | async-start | bytes 65536 | tf_op jit(solution)/shard_map/all_to_all | solution.py:669
  15.9 8.9 %collective-permute-start = (f32[16,128]{1,0:T(8,128)S(1)}, f32[16,128]{1,0:T(8,128)S(1)}, u32[]{:S(2)}, u32[]{:S(2)}) collective-permute-start(f32[16,128]{1,0:T(8,128)S(1)} %get-tuple-element.34), channel_id=1, source_target_pairs={{0,32},{32,64},{64,96},{96,128},{128,160},{160,192},{192,224},{224... | collective-permute-start | bytes 24584 | tf_op jit(solution)/shard_map/ppermute | solution.py:671
  17.6 7.2 %collective-permute-start.1 = (f32[16,128]{1,0:T(8,128)S(1)}, f32[16,128]{1,0:T(8,128)S(1)}, u32[]{:S(2)}, u32[]{:S(2)}) collective-permute-start(f32[16,128]{1,0:T(8,128)S(1)} %get-tuple-element.35), channel_id=1, source_target_pairs={{32,0},{64,32},{96,64},{128,96},{160,128},{192,160},{224,192},{0,2... | collective-permute-start | bytes 24584 | tf_op jit(solution)/shard_map/ppermute | solution.py:672
  28.8 15.4 %all-to-all-start.1 = ((f32[32,8,128]{2,1,0:T(8,128)}), f32[32,8,128]{2,1,0:T(8,128)S(1)}, u32[]{:S(2)}, u32[]{:S(2)}) async-start(f32[32,8,128]{2,1,0:T(8,128)} %bitcast.2), calls=%async_computation.1 | async-start | bytes 262144 | tf_op jit(solution)/shard_map/all_to_all | solution.py:669
  36.5 4.5 %collective-permute-start.2 = (f32[64,128]{1,0:T(8,128)S(1)}, f32[64,128]{1,0:T(8,128)S(1)}, u32[]{:S(2)}, u32[]{:S(2)}) collective-permute-start(f32[64,128]{1,0:T(8,128)S(1)} %get-tuple-element.58), channel_id=1, source_target_pairs={{0,32},{32,64},{64,96},{96,128},{128,160},{160,192},{192,224},{224... | collective-permute-start | bytes 98312 | tf_op jit(solution)/shard_map/ppermute | solution.py:671
  36.8 4.3 %collective-permute-start.3 = (f32[64,128]{1,0:T(8,128)S(1)}, f32[64,128]{1,0:T(8,128)S(1)}, u32[]{:S(2)}, u32[]{:S(2)}) collective-permute-start(f32[64,128]{1,0:T(8,128)S(1)} %get-tuple-element.59), channel_id=1, source_target_pairs={{32,0},{64,32},{96,64},{128,96},{160,128},{192,160},{224,192},{0,2... | collective-permute-start | bytes 98312 | tf_op jit(solution)/shard_map/ppermute | solution.py:672

commit v5 on v4

--- a/solution.py
+++ b/solution.py
@@ -218,10 +218,21 @@
     return faces
 
 
-def add_back(w, side, face):
+def add_faces(w, face):
+    kk = iota((64, 128), 1) & 7
+    out = []
+    for c in range(4):
+        x = w[c]
+        for k, part in zip((0, 7), face):
+            spread = [pltpu.roll(part, (k - 4 * h - c) % 128, 1) for h in range(2)]
+            x = x + jnp.where(kk == k, jnp.concatenate(spread, axis=0), 0.0)
+        out.append(x)
+    return out
+
+
+def add_sides(w, side):
     lane = iota((64, 128), 1)
     sub = iota((64, 128), 0) & 7
-    kk = lane & 7
     jj = (iota((8, 128), 1) >> 3) & 7
     x_rows = jnp.concatenate(
         [jnp.broadcast_to(side[by : by + 1], (8, 128)) for by in range(8)], axis=0
@@ -234,13 +245,21 @@
             x = x + jnp.where((sub == 0) & (lane < 64), x_rows, 0.0)
         if c == 3:
             x = x + jnp.where((sub == 7) & (lane >= 64), x_rows, 0.0)
-        for k, part in zip((0, 7), face):
-            spread = [pltpu.roll(part, (k - 4 * h - c) % 128, 1) for h in range(2)]
-            x = x + jnp.where(kk == k, jnp.concatenate(spread, axis=0), 0.0)
         first = x[0:8] + jnp.where(jj == 0, pltpu.roll(y_side, (-16 * c) % 128, 1), 0.0)
         last = x[56:64] + jnp.where(jj == 7, pltpu.roll(y_side, (48 - 16 * c) % 128, 1), 0.0)
         out.append(jnp.concatenate([first, x[8:56], last], axis=0))
     return out
+
+
+def on_all_copies(side):
+    lane = iota((8, 128), 1)
+    row = iota((8, 128), 0)
+    x_side, y_side = side[0:8], side[8:16]
+    x_next = pltpu.roll(pltpu.roll(x_side, 56, 1), 7, 0)
+    y_next = pltpu.roll(pltpu.roll(y_side, 112, 1), 7, 0)
+    x_side = jnp.where((((lane >> 3) & 7) == 7) & (row < 7), x_next, x_side)
+    y_side = jnp.where((lane >= 112) & (row < 7), y_next, y_side)
+    return jnp.concatenate([x_side, y_side], axis=0)
 
 
 def block_row(block):
@@ -269,11 +288,14 @@
     return dot_nt(jnp.concatenate(parts, axis=0), lows)
 
 
+def build_low(lo_ref, low_ref):
+    for g in range(lo_ref.shape[0] // 8):
+        low_ref[:, lanes_of(g)] = one_hot(block_row(lo_ref[rows_of(g), :]), 128)
+
+
 def build_lows(slo_ref, flo_ref, slow_ref, flow_ref):
-    for g in range(8):
-        slow_ref[:, lanes_of(g)] = one_hot(block_row(slo_ref[rows_of(g), :]), 128)
-    for g in range(4):
-        flow_ref[:, lanes_of(g)] = one_hot(block_row(flo_ref[rows_of(g), :]), 128)
+    build_low(slo_ref, slow_ref)
+    build_low(flo_ref, flow_ref)
 
 
 def lanes_of(g):
@@ -302,7 +324,7 @@
                 out_ref[at : at + 1, :] = values[:, 128 * t : 128 * t + 128]
 
 
-def take_values(count, shi_ref, fhi_ref, slow_ref, flow_ref, msg_ref, low_ref, upp_ref, stride):
+def take_sides(count, shi_ref, slow_ref, msg_ref, stride):
     side = None
     for g in range(8):
         rows = []
@@ -314,15 +336,17 @@
             rows.append(jnp.concatenate(cells, axis=1))
         part = scatter_tables(rows, shi_ref[rows_of(g), :], slow_ref[:, lanes_of(g)], 16)
         side = part if side is None else side + part
+    return [side[32 * f : 32 * f + 16] + side[32 * f + 16 : 32 * f + 32] for f in range(count)]
+
+
+def take_faces(count, fhi_ref, flow_ref, low_ref, upp_ref):
     face = [None, None]
     for g in range(4):
         ref = low_ref if g < 2 else upp_ref
         rows = [block_row(ref[16 * f + 8 * (g % 2) : 16 * f + 8 * (g % 2) + 8, :]) for f in range(count)]
         part = scatter_tables(rows, fhi_ref[rows_of(g), :], flow_ref[:, lanes_of(g)], 32)
         face[g // 2] = part if face[g // 2] is None else face[g // 2] + part
-    sides = [side[32 * f : 32 * f + 16] + side[32 * f + 16 : 32 * f + 32] for f in range(count)]
-    faces = [[x[64 * f : 64 * f + 32] + x[64 * f + 32 : 64 * f + 64] for x in face] for f in range(count)]
-    return sides, faces
+    return [[x[64 * f : 64 * f + 32] + x[64 * f + 32 : 64 * f + 64] for x in face] for f in range(count)]
 
 
 def chain_place(left):
@@ -365,9 +389,11 @@
 
 
 def look_up(table, row):
-    got = dot(table, one_hot(row >> 7, HI))
-    mask = iota((128, row.shape[1]), 0) == (row & 127)
-    return jnp.sum(jnp.where(mask, got, 0.0), axis=0, keepdims=True)
+    got = choose(marks(row & 127, 128), dot(table, one_hot(row >> 7, HI)).astype(BF16))
+    total = got[0:16]
+    for at in range(1, 8):
+        total = total + got[16 * at : 16 * at + 16]
+    return jnp.sum(total.astype(F32), axis=0, keepdims=True)
 
 
 def decode(x, count):
@@ -459,9 +485,11 @@
         (axial_h, axial_ref), *zip(later_h, later),
     ]
     copies = [pltpu.make_async_copy(src, dst, sems.at[at]) for at, (src, dst) in enumerate(pairs)]
-    for copy in copies:
+    for copy in copies[:11]:
         copy.start()
     copies[0].wait()
+    for copy in copies[11:]:
+        copy.start()
     conn = conn_ref[...]
     build_perm(conn, perm_ref, back_ref)
     for copy in copies[1:11]:
@@ -530,8 +558,9 @@
     slow_ref, flow_ref,
 ):
     build_lows(slo_ref, flo_ref, slow_ref, flow_ref)
-    sides, faces = take_values(1, shi_ref, fhi_ref, slow_ref, flow_ref, msg_in_ref, low_ref, upp_ref, 2)
-    w = add_back(chunks_of(w_in_ref[...]), sides[0], faces[0])
+    sides = take_sides(1, shi_ref, slow_ref, msg_in_ref, 2)
+    faces = take_faces(1, fhi_ref, flow_ref, low_ref, upp_ref)
+    w = add_sides(add_faces(chunks_of(w_in_ref[...]), faces[0]), sides[0])
     applied = permute(back_ref[...], assemble_local(w))
     step = []
     for c in range(4):
@@ -553,19 +582,26 @@
     down_ref[16:64, :] = down_m_ref[...]
 
 
+def faces_kernel(low_ref, upp_ref, w_in_ref, w_m_ref, fhi_ref, flo_ref, held_ref, flow_ref):
+    build_low(flo_ref, flow_ref)
+    faces = take_faces(4, fhi_ref, flow_ref, low_ref, upp_ref)
+    for f in range(4):
+        w = w_in_ref[...] if f == 0 else w_m_ref[f - 1]
+        w = assemble_local(add_faces(chunks_of(w), faces[f]))
+        for c in range(4):
+            held_ref[f, :, 128 * c : 128 * c + 128] = w[c]
+
+
 def last_kernel(
-    msg_in_ref, low_ref, upp_ref, w_in_ref, w_m_ref, jacobi_ref, base_ref, res_ref, back_ref, shi_ref, fhi_ref, slo_ref,
-    flo_ref,
+    msg_in_ref, held_ref, jacobi_ref, base_ref, res_ref, back_ref, shi_ref, slo_ref,
     pressure_h, momentum_h,
-    out_ref, slow_ref, flow_ref, sems,
+    out_ref, slow_ref, sems,
 ):
-    build_lows(slo_ref, flo_ref, slow_ref, flow_ref)
-    sides, faces = take_values(4, shi_ref, fhi_ref, slow_ref, flow_ref, msg_in_ref, low_ref, upp_ref, 8)
+    build_low(slo_ref, slow_ref)
+    sides = take_sides(4, shi_ref, slow_ref, msg_in_ref, 8)
     copies = []
     for f in range(4):
-        held = w_in_ref[...] if f == 0 else w_m_ref[f - 1]
-        w = add_back(chunks_of(held), sides[f], faces[f])
-        applied = permute(back_ref[...], assemble_local(w))
+        applied = permute(back_ref[...], add_sides(chunks_of(held_ref[f]), on_all_copies(sides[f])))
         for c in range(4):
             lanes = slice(128 * c, 128 * c + 128)
             value = applied[c]
@@ -653,12 +689,23 @@
     )
 
 
-def run_last(msg, low, upp, w, w_m, jacobi, base, res, back, lists):
+def run_faces(low, upp, w, w_m, lists):
+    (held,) = call(
+        faces_kernel,
+        [shape(4, 64, 512)],
+        [low, upp, w, w_m, lists[1], lists[3]],
+        [pltpu.VMEM((128, 4096), BF16)],
+        name="faces",
+    )
+    return held
+
+
+def run_last(msg, held, jacobi, base, res, back, lists):
     return call(
         last_kernel,
         [shape(64, 512), shape(3, 64, 512)],
-        [msg, low, upp, w, w_m, jacobi, base, res, back, *lists],
-        [pltpu.VMEM((4, 64, 512), F32), *lows(), pltpu.SemaphoreType.DMA((4,))],
+        [msg, held, jacobi, base, res, back, lists[0], lists[2]],
+        [pltpu.VMEM((4, 64, 512), F32), pltpu.VMEM((128, 8192), BF16), pltpu.SemaphoreType.DMA((4,))],
         name="last",
         outs_hbm=True,
     )
@@ -687,8 +734,9 @@
     msg, up, down, w, base, res = run_second(
         *got, w, pressure, rhs, jacobi, geom, tables, perm, back, lists, msg_m, up_m, down_m
     )
-    got = exchange(msg, up, down)
-    return tuple(run_last(*got, w, w_m, jacobi, base, res, back, lists))
+    msg, low, upp = exchange(msg, up, down)
+    held = run_faces(low, upp, w, w_m, lists)
+    return tuple(run_last(msg, held, jacobi, base, res, back, lists))
 
 
 def solution(mesh):

time: 47.4 us -> 46.7 us (0.985)
  waiting for transfers between devices: 4.77 us -> 3.51 us
  Pallas kernels: 16.6 us -> 17.2 us
    all_to_all x2, waiting for transfers between devices: 3.17 us -> 1.9 us  [exchange(): lax.all_to_all(msg.reshape(32, rows, 128), ('gy', 'gz'), split_axis=0, co...]
    pallas_call x4 -> x5, Pallas kernels: 16.6 us -> 17.2 us  [call(): pl.pallas_call(kernel, out_shape=outs, in_specs=[in_hbm() if args_hbm els...]
  transfers between devices with their start and end apart: 6 -> 6, of which waited for: 2 -> 2; matrix products, arithmetic and copies ran while one was open for 0% -> 0% of each run, Pallas kernels for 7% -> 10%
where the time goes in v5:
time: 46.7 us; the launch traced here: 46.5 us
  starting transfers between devices  24.9 us (53%)
  Pallas kernels  17.2 us (37%)
  waiting for transfers between devices  3.51 us (8%)
  between operations  0.87 us (2%)
    pallas_call x5, Pallas kernels, call(): pl.pallas_call(kernel, out_shape=outs, in_specs=[in_hbm() if args_hbm els...  17.2 us
    all_to_all x2, starting transfers between devices, exchange(): lax.all_to_all(msg.reshape(32, rows, 128), ('gy', 'gz'), split_axis=0, co...  16.3 us
    ppermute x2, starting transfers between devices, exchange(): lax.ppermute(down, 'gx', [((i + 1) % count, i) for i in range(count)])  6.69 us
    ppermute x2, starting transfers between devices, exchange(): lax.ppermute(up, 'gx', [(i, (i + 1) % count) for i in range(count)])  1.98 us
    all_to_all x2, waiting for transfers between devices, exchange(): lax.all_to_all(msg.reshape(32, rows, 128), ('gy', 'gz'), split_axis=0, co...  1.9 us
    ppermute x2, waiting for transfers between devices, exchange(): lax.ppermute(up, 'gx', [(i, (i + 1) % count) for i in range(count)])  1.6 us
  transfers between devices with their start and end apart: 6, of which 2 were waited for; matrix products, arithmetic and copies ran while one was open for 0% of the time, Pallas kernels for 10%

profile of v5, /device:TPU:1, one launch (start us, length us, event | category | flops | bytes accessed | tf_op | source)
XLA Modules:
  0.0 46.5 jit_solution(4965985440217409456)
XLA Ops:
  0.6 6.6 %first.1 = (f32[64,128]{1,0:T(8,128)}, f32[16,128]{1,0:T(8,128)S(1)}, f32[16,128]{1,0:T(8,128)S(1)}, f32[64,512]{1,0:T(8,128)S(1)}, s32[64,128]{1,0:T(8,128)S(1)...) custom-call(s32[64,512]{1,0:T(8,128)} %refs_0_.1, ...), custom_call_target="tpu_custom_call" | custom-call | tf_op jit(solution)/shard_map/first/pallas_call | solution.py:635
  7.2 8.6 %all-to-all-start = ((f32[32,2,128]{2,1,0:T(2,128)}), f32[32,2,128]{2,1,0:T(2,128)S(1)}, u32[]{:S(2)}, u32[]{:S(2)}) async-start(f32[32,2,128]{2,1,0:T(2,128)} %bitcast), calls=%async_computation | async-start | bytes 65536 | tf_op jit(solution)/shard_map/all_to_all | solution.py:716
  15.8 1.7 %collective-permute-start = (f32[16,128]{1,0:T(8,128)S(1)}, f32[16,128]{1,0:T(8,128)S(1)}, u32[]{:S(2)}, u32[]{:S(2)}) collective-permute-start(f32[16,128]{1,0:T(8,128)S(1)} %get-tuple-element.34), channel_id=1, source_target_pairs={{0,32},{32,64},{64,96},{96,128},{128,160},{160,192},{192,224},{224... | collective-permute-start | bytes 24584 | tf_op jit(solution)/shard_map/ppermute | solution.py:718
  17.5 4.0 %collective-permute-start.1 = (f32[16,128]{1,0:T(8,128)S(1)}, f32[16,128]{1,0:T(8,128)S(1)}, u32[]{:S(2)}, u32[]{:S(2)}) collective-permute-start(f32[16,128]{1,0:T(8,128)S(1)} %get-tuple-element.35), channel_id=1, source_target_pairs={{32,0},{64,32},{96,64},{128,96},{160,128},{192,160},{224,192},{0,2... | collective-permute-start | bytes 24584 | tf_op jit(solution)/shard_map/ppermute | solution.py:719
  21.6 3.2 %momentum.1 = (f32[192,128]{1,0:T(8,128)S(1)}, f32[48,128]{1,0:T(8,128)S(1)}, f32[48,128]{1,0:T(8,128)S(1)}, f32[3,64,512]{2,1,0:T(8,128)S(1)}) custom-call(f32[3,64,512]{2,1,0:T(8,128)S(1)} %get-tuple-element.50.velocity_ref, f32[3,64,512]{2,1,0:T(8,128)S(1)} %get-tuple-element.51.force_ref, f32[64,512]{1,0:T(8,128)S(1)} %get-tuple-element.52.mass_ref, ...), custom_call_target="tpu_custom_call" | custom-call | tf_op jit(solution)/shard_map/momentum/pallas_call | solution.py:635
  24.8 0.0 collective-permute-done.low_ref
  24.8 0.0 collective-permute-done.1.upp_ref
  24.8 0.0 all-to-all-done
  24.8 3.9 %second.1 = (f32[256,128]{1,0:T(8,128)}, f32[64,128]{1,0:T(8,128)S(1)}, f32[64,128]{1,0:T(8,128)S(1)}, f32[64,512]{1,0:T(8,128)S(1)}, f32[64,512]{1,0:T(8,128)S(1)}, /*index=5*/f32[64,512]{1,0:T(8,128)S(1)}) custom-call(f32[64,128]{1,0:T(8,128)S(1)} %bitcast.5, f32[16,128]{1,0:T(8,128)S(1)} %collective-permute-done.low_ref, ...), custom_call_target="tpu_custom_call" | custom-call | tf_op jit(solution)/shard_map/second/pallas_call | solution.py:635
  28.7 7.7 %all-to-all-start.1 = ((f32[32,8,128]{2,1,0:T(8,128)}), f32[32,8,128]{2,1,0:T(8,128)S(1)}, u32[]{:S(2)}, u32[]{:S(2)}) async-start(f32[32,8,128]{2,1,0:T(8,128)} %bitcast.2), calls=%async_computation.1 | async-start | bytes 262144 | tf_op jit(solution)/shard_map/all_to_all | solution.py:716
  36.4 0.3 collective-permute-start.2
  36.7 2.7 %collective-permute-start.3 = (f32[64,128]{1,0:T(8,128)S(1)}, f32[64,128]{1,0:T(8,128)S(1)}, u32[]{:S(2)}, u32[]{:S(2)}) collective-permute-start(f32[64,128]{1,0:T(8,128)S(1)} %get-tuple-element.59), channel_id=1, source_target_pairs={{32,0},{64,32},{96,64},{128,96},{160,128},{192,160},{224,192},{0,2... | collective-permute-start | bytes 98312 | tf_op jit(solution)/shard_map/ppermute | solution.py:719
  39.3 1.6 %collective-permute-done.2.low_ref = f32[64,128]{1,0:T(8,128)S(1)} collective-permute-done((f32[64,128]{1,0:T(8,128)S(1)}, f32[64,128]{1,0:T(8,128)S(1)}, u32[]{:S(2)}, u32[]{:S(2)}) %collective-permute-start.2) | collective-permute-done | bytes 32800 | tf_op jit(solution)/shard_map/ppermute | solution.py:718
  40.9 0.0 collective-permute-done.3.upp_ref
  40.9 1.3 %faces.1.held_ref = f32[4,64,512]{2,1,0:T(8,128)S(1)} custom-call(f32[64,128]{1,0:T(8,128)S(1)} %collective-permute-done.2.low_ref, f32[64,128]{1,0:T(8,128)S(1)} %collective-permute-done.3.upp_ref, f32[64,512]{1,0:T(8,128)S(1)} %get-tuple-element.60.w_in_ref, f32[3,64,512]{2,1,0:T(8,128)S(1)} %get-tuple-element.61.w_m_ref, ...), custom_call_target="tpu_custom_call" | custom-call | tf_op jit(solution)/shard_map/faces/pallas_call | solution.py:635
  42.2 1.9 %all-to-all-done.1 = f32[32,8,128]{2,1,0:T(8,128)S(1)} async-done(((f32[32,8,128]{2,1,0:T(8,128)}), f32[32,8,128]{2,1,0:T(8,128)S(1)}, u32[]{:S(2)}, u32[]{:S(2)}) %all-to-all-start.1) | async-done | bytes 131104 | tf_op jit(solution)/shard_map/all_to_all | solution.py:716
  44.1 2.3 %last.1 = (f32[64,512]{1,0:T(8,128)}, f32[3,64,512]{2,1,0:T(8,128)}) custom-call(f32[256,128]{1,0:T(8,128)S(1)} %bitcast.4, f32[4,64,512]{2,1,0:T(8,128)S(1)} %faces.1.held_ref, f32[64,512]{1,0:T(8,128)S(1)} %get-tuple-element.39.jacobi_ref, f32[64,512]{1,0:T(8,128)S(1)} %get-tuple-element.62.base_ref, f32[64,512]{1,0:T(8,128)S(1)} %get-tuple-element.63.res_ref, ...), custom_call_target="tpu_custom_call" | custom-call | tf_op jit(solution)/shard_map/last/pallas_call | solution.py:635
Async XLA Ops:
  7.2 17.6 %all-to-all-start = ((f32[32,2,128]{2,1,0:T(2,128)}), f32[32,2,128]{2,1,0:T(2,128)S(1)}, u32[]{:S(2)}, u32[]{:S(2)}) async-start(f32[32,2,128]{2,1,0:T(2,128)} %bitcast), calls=%async_computation | async-start | bytes 65536 | tf_op jit(solution)/shard_map/all_to_all | solution.py:716
  15.8 8.9 %collective-permute-start = (f32[16,128]{1,0:T(8,128)S(1)}, f32[16,128]{1,0:T(8,128)S(1)}, u32[]{:S(2)}, u32[]{:S(2)}) collective-permute-start(f32[16,128]{1,0:T(8,128)S(1)} %get-tuple-element.34), channel_id=1, source_target_pairs={{0,32},{32,64},{64,96},{96,128},{128,160},{160,192},{192,224},{224... | collective-permute-start | bytes 24584 | tf_op jit(solution)/shard_map/ppermute | solution.py:718
  17.5 7.2 %collective-permute-start.1 = (f32[16,128]{1,0:T(8,128)S(1)}, f32[16,128]{1,0:T(8,128)S(1)}, u32[]{:S(2)}, u32[]{:S(2)}) collective-permute-start(f32[16,128]{1,0:T(8,128)S(1)} %get-tuple-element.35), channel_id=1, source_target_pairs={{32,0},{64,32},{96,64},{128,96},{160,128},{192,160},{224,192},{0,2... | collective-permute-start | bytes 24584 | tf_op jit(solution)/shard_map/ppermute | solution.py:719
  28.7 15.4 %all-to-all-start.1 = ((f32[32,8,128]{2,1,0:T(8,128)}), f32[32,8,128]{2,1,0:T(8,128)S(1)}, u32[]{:S(2)}, u32[]{:S(2)}) async-start(f32[32,8,128]{2,1,0:T(8,128)} %bitcast.2), calls=%async_computation.1 | async-start | bytes 262144 | tf_op jit(solution)/shard_map/all_to_all | solution.py:716
  36.4 4.5 %collective-permute-start.2 = (f32[64,128]{1,0:T(8,128)S(1)}, f32[64,128]{1,0:T(8,128)S(1)}, u32[]{:S(2)}, u32[]{:S(2)}) collective-permute-start(f32[64,128]{1,0:T(8,128)S(1)} %get-tuple-element.58), channel_id=1, source_target_pairs={{0,32},{32,64},{64,96},{96,128},{128,160},{160,192},{192,224},{224... | collective-permute-start | bytes 98312 | tf_op jit(solution)/shard_map/ppermute | solution.py:718
  36.7 4.3 %collective-permute-start.3 = (f32[64,128]{1,0:T(8,128)S(1)}, f32[64,128]{1,0:T(8,128)S(1)}, u32[]{:S(2)}, u32[]{:S(2)}) collective-permute-start(f32[64,128]{1,0:T(8,128)S(1)} %get-tuple-element.59), channel_id=1, source_target_pairs={{32,0},{64,32},{96,64},{128,96},{160,128},{192,160},{224,192},{0,2... | collective-permute-start | bytes 98312 | tf_op jit(solution)/shard_map/ppermute | solution.py:719

commit v6 on v5

--- a/solution.py
+++ b/solution.py
@@ -285,7 +285,8 @@
     for values in rows:
         for part in split(values, 2):
             parts.append(choose(mask, repeat_row(part, hi_count)))
-    return dot_nt(jnp.concatenate(parts, axis=0), lows)
+    parts = jnp.concatenate(parts, axis=0)
+    return dot_nt(lows, parts) if hi_count == 16 else dot_nt(parts, lows)
 
 
 def build_low(lo_ref, low_ref):
@@ -336,6 +337,7 @@
             rows.append(jnp.concatenate(cells, axis=1))
         part = scatter_tables(rows, shi_ref[rows_of(g), :], slow_ref[:, lanes_of(g)], 16)
         side = part if side is None else side + part
+    side = side.T
     return [side[32 * f : 32 * f + 16] + side[32 * f + 16 : 32 * f + 32] for f in range(count)]
 
 
@@ -453,9 +455,9 @@
         slot = slot_ref[:, at]
         places = look_up(table_s, node_ref[:, at])
         hit = marks(peer_ref[:, at] * 2 + (slot >> 7), 64)
-        part = dot_nt(choose(hit, repeat_row(places, 64)), one_hot(slot & 127, 128))
+        part = dot_nt(one_hot(slot & 127, 128), choose(hit, repeat_row(places, 64)))
         total = part if total is None else total + part
-    row, lane = decode(total, 16)
+    row, lane = decode(total.T, 16)
     limit = jnp.sum(jnp.where(iota((64, 32), 1) == (iota((64, 32), 0) >> 1), counts, 0), axis=1, keepdims=True)
     slots = (iota((64, 128), 0) & 1) * 128 + iota((64, 128), 1)
     shi_ref[...] = jnp.where(slots < limit, row, -1)

time: 46.7 us -> 46.5 us (level)
  no operation moved by 1% of the time
where the time goes in v6:
time: 46.5 us; the launch traced here: 46.3 us
  starting transfers between devices  24.9 us (54%)
  Pallas kernels  17 us (37%)
  waiting for transfers between devices  3.48 us (7%)
  between operations  0.87 us (2%)
    pallas_call x5, Pallas kernels, call(): pl.pallas_call(kernel, out_shape=outs, in_specs=[in_hbm() if args_hbm els...  17 us
    all_to_all x2, starting transfers between devices, exchange(): lax.all_to_all(msg.reshape(32, rows, 128), ('gy', 'gz'), split_axis=0, co...  16.3 us
    ppermute x2, starting transfers between devices, exchange(): lax.ppermute(down, 'gx', [((i + 1) % count, i) for i in range(count)])  6.69 us
    ppermute x2, starting transfers between devices, exchange(): lax.ppermute(up, 'gx', [(i, (i + 1) % count) for i in range(count)])  1.98 us
    all_to_all x2, waiting for transfers between devices, exchange(): lax.all_to_all(msg.reshape(32, rows, 128), ('gy', 'gz'), split_axis=0, co...  1.88 us
    ppermute x2, waiting for transfers between devices, exchange(): lax.ppermute(up, 'gx', [(i, (i + 1) % count) for i in range(count)])  1.6 us
  transfers between devices with their start and end apart: 6, of which 2 were waited for; matrix products, arithmetic and copies ran while one was open for 0% of the time, Pallas kernels for 10%

profile of v6, /device:TPU:1, one launch (start us, length us, event | category | flops | bytes accessed | tf_op | source)
XLA Modules:
  0.0 46.3 jit_solution(13462639732005468135)
XLA Ops:
  0.6 6.5 %first.1 = (f32[64,128]{1,0:T(8,128)}, f32[16,128]{1,0:T(8,128)S(1)}, f32[16,128]{1,0:T(8,128)S(1)}, f32[64,512]{1,0:T(8,128)S(1)}, s32[64,128]{1,0:T(8,128)S(1)...) custom-call(s32[64,512]{1,0:T(8,128)} %refs_0_.1, ...), custom_call_target="tpu_custom_call" | custom-call | tf_op jit(solution)/shard_map/first/pallas_call | solution.py:637
  7.1 8.6 %all-to-all-start = ((f32[32,2,128]{2,1,0:T(2,128)}), f32[32,2,128]{2,1,0:T(2,128)S(1)}, u32[]{:S(2)}, u32[]{:S(2)}) async-start(f32[32,2,128]{2,1,0:T(2,128)} %bitcast), calls=%async_computation | async-start | bytes 65536 | tf_op jit(solution)/shard_map/all_to_all | solution.py:718
  15.7 1.7 %collective-permute-start = (f32[16,128]{1,0:T(8,128)S(1)}, f32[16,128]{1,0:T(8,128)S(1)}, u32[]{:S(2)}, u32[]{:S(2)}) collective-permute-start(f32[16,128]{1,0:T(8,128)S(1)} %get-tuple-element.34), channel_id=1, source_target_pairs={{0,32},{32,64},{64,96},{96,128},{128,160},{160,192},{192,224},{224... | collective-permute-start | bytes 24584 | tf_op jit(solution)/shard_map/ppermute | solution.py:720
  17.5 4.0 %collective-permute-start.1 = (f32[16,128]{1,0:T(8,128)S(1)}, f32[16,128]{1,0:T(8,128)S(1)}, u32[]{:S(2)}, u32[]{:S(2)}) collective-permute-start(f32[16,128]{1,0:T(8,128)S(1)} %get-tuple-element.35), channel_id=1, source_target_pairs={{32,0},{64,32},{96,64},{128,96},{160,128},{192,160},{224,192},{0,2... | collective-permute-start | bytes 24584 | tf_op jit(solution)/shard_map/ppermute | solution.py:721
  21.5 3.2 %momentum.1 = (f32[192,128]{1,0:T(8,128)S(1)}, f32[48,128]{1,0:T(8,128)S(1)}, f32[48,128]{1,0:T(8,128)S(1)}, f32[3,64,512]{2,1,0:T(8,128)S(1)}) custom-call(f32[3,64,512]{2,1,0:T(8,128)S(1)} %get-tuple-element.50.velocity_ref, f32[3,64,512]{2,1,0:T(8,128)S(1)} %get-tuple-element.51.force_ref, f32[64,512]{1,0:T(8,128)S(1)} %get-tuple-element.52.mass_ref, ...), custom_call_target="tpu_custom_call" | custom-call | tf_op jit(solution)/shard_map/momentum/pallas_call | solution.py:637
  24.7 0.0 collective-permute-done.low_ref
  24.7 0.0 collective-permute-done.1.upp_ref
  24.7 0.0 all-to-all-done
  24.7 4.0 %second.1 = (f32[256,128]{1,0:T(8,128)}, f32[64,128]{1,0:T(8,128)S(1)}, f32[64,128]{1,0:T(8,128)S(1)}, f32[64,512]{1,0:T(8,128)S(1)}, f32[64,512]{1,0:T(8,128)S(1)}, /*index=5*/f32[64,512]{1,0:T(8,128)S(1)}) custom-call(f32[64,128]{1,0:T(8,128)S(1)} %bitcast.5, f32[16,128]{1,0:T(8,128)S(1)} %collective-permute-done.low_ref, ...), custom_call_target="tpu_custom_call" | custom-call | tf_op jit(solution)/shard_map/second/pallas_call | solution.py:637
  28.7 7.7 %all-to-all-start.1 = ((f32[32,8,128]{2,1,0:T(8,128)}), f32[32,8,128]{2,1,0:T(8,128)S(1)}, u32[]{:S(2)}, u32[]{:S(2)}) async-start(f32[32,8,128]{2,1,0:T(8,128)} %bitcast.2), calls=%async_computation.1 | async-start | bytes 262144 | tf_op jit(solution)/shard_map/all_to_all | solution.py:718
  36.3 0.3 collective-permute-start.2
  36.6 2.7 %collective-permute-start.3 = (f32[64,128]{1,0:T(8,128)S(1)}, f32[64,128]{1,0:T(8,128)S(1)}, u32[]{:S(2)}, u32[]{:S(2)}) collective-permute-start(f32[64,128]{1,0:T(8,128)S(1)} %get-tuple-element.59), channel_id=1, source_target_pairs={{32,0},{64,32},{96,64},{128,96},{160,128},{192,160},{224,192},{0,2... | collective-permute-start | bytes 98312 | tf_op jit(solution)/shard_map/ppermute | solution.py:721
  39.3 1.6 %collective-permute-done.2.low_ref = f32[64,128]{1,0:T(8,128)S(1)} collective-permute-done((f32[64,128]{1,0:T(8,128)S(1)}, f32[64,128]{1,0:T(8,128)S(1)}, u32[]{:S(2)}, u32[]{:S(2)}) %collective-permute-start.2) | collective-permute-done | bytes 32800 | tf_op jit(solution)/shard_map/ppermute | solution.py:720
  40.9 0.0 collective-permute-done.3.upp_ref
  40.9 1.3 %faces.1.held_ref = f32[4,64,512]{2,1,0:T(8,128)S(1)} custom-call(f32[64,128]{1,0:T(8,128)S(1)} %collective-permute-done.2.low_ref, f32[64,128]{1,0:T(8,128)S(1)} %collective-permute-done.3.upp_ref, f32[64,512]{1,0:T(8,128)S(1)} %get-tuple-element.60.w_in_ref, f32[3,64,512]{2,1,0:T(8,128)S(1)} %get-tuple-element.61.w_m_ref, ...), custom_call_target="tpu_custom_call" | custom-call | tf_op jit(solution)/shard_map/faces/pallas_call | solution.py:637
  42.2 1.9 %all-to-all-done.1 = f32[32,8,128]{2,1,0:T(8,128)S(1)} async-done(((f32[32,8,128]{2,1,0:T(8,128)}), f32[32,8,128]{2,1,0:T(8,128)S(1)}, u32[]{:S(2)}, u32[]{:S(2)}) %all-to-all-start.1) | async-done | bytes 131104 | tf_op jit(solution)/shard_map/all_to_all | solution.py:718
  44.0 2.1 %last.1 = (f32[64,512]{1,0:T(8,128)}, f32[3,64,512]{2,1,0:T(8,128)}) custom-call(f32[256,128]{1,0:T(8,128)S(1)} %bitcast.4, f32[4,64,512]{2,1,0:T(8,128)S(1)} %faces.1.held_ref, f32[64,512]{1,0:T(8,128)S(1)} %get-tuple-element.39.jacobi_ref, f32[64,512]{1,0:T(8,128)S(1)} %get-tuple-element.62.base_ref, f32[64,512]{1,0:T(8,128)S(1)} %get-tuple-element.63.res_ref, ...), custom_call_target="tpu_custom_call" | custom-call | tf_op jit(solution)/shard_map/last/pallas_call | solution.py:637
Async XLA Ops:
  7.1 17.6 %all-to-all-start = ((f32[32,2,128]{2,1,0:T(2,128)}), f32[32,2,128]{2,1,0:T(2,128)S(1)}, u32[]{:S(2)}, u32[]{:S(2)}) async-start(f32[32,2,128]{2,1,0:T(2,128)} %bitcast), calls=%async_computation | async-start | bytes 65536 | tf_op jit(solution)/shard_map/all_to_all | solution.py:718
  15.7 8.9 %collective-permute-start = (f32[16,128]{1,0:T(8,128)S(1)}, f32[16,128]{1,0:T(8,128)S(1)}, u32[]{:S(2)}, u32[]{:S(2)}) collective-permute-start(f32[16,128]{1,0:T(8,128)S(1)} %get-tuple-element.34), channel_id=1, source_target_pairs={{0,32},{32,64},{64,96},{96,128},{128,160},{160,192},{192,224},{224... | collective-permute-start | bytes 24584 | tf_op jit(solution)/shard_map/ppermute | solution.py:720
  17.5 7.2 %collective-permute-start.1 = (f32[16,128]{1,0:T(8,128)S(1)}, f32[16,128]{1,0:T(8,128)S(1)}, u32[]{:S(2)}, u32[]{:S(2)}) collective-permute-start(f32[16,128]{1,0:T(8,128)S(1)} %get-tuple-element.35), channel_id=1, source_target_pairs={{32,0},{64,32},{96,64},{128,96},{160,128},{192,160},{224,192},{0,2... | collective-permute-start | bytes 24584 | tf_op jit(solution)/shard_map/ppermute | solution.py:721
  28.7 15.4 %all-to-all-start.1 = ((f32[32,8,128]{2,1,0:T(8,128)}), f32[32,8,128]{2,1,0:T(8,128)S(1)}, u32[]{:S(2)}, u32[]{:S(2)}) async-start(f32[32,8,128]{2,1,0:T(8,128)} %bitcast.2), calls=%async_computation.1 | async-start | bytes 262144 | tf_op jit(solution)/shard_map/all_to_all | solution.py:718
  36.3 4.5 %collective-permute-start.2 = (f32[64,128]{1,0:T(8,128)S(1)}, f32[64,128]{1,0:T(8,128)S(1)}, u32[]{:S(2)}, u32[]{:S(2)}) collective-permute-start(f32[64,128]{1,0:T(8,128)S(1)} %get-tuple-element.58), channel_id=1, source_target_pairs={{0,32},{32,64},{64,96},{96,128},{128,160},{160,192},{192,224},{224... | collective-permute-start | bytes 98312 | tf_op jit(solution)/shard_map/ppermute | solution.py:720
  36.6 4.3 %collective-permute-start.3 = (f32[64,128]{1,0:T(8,128)S(1)}, f32[64,128]{1,0:T(8,128)S(1)}, u32[]{:S(2)}, u32[]{:S(2)}) collective-permute-start(f32[64,128]{1,0:T(8,128)S(1)} %get-tuple-element.59), channel_id=1, source_target_pairs={{32,0},{64,32},{96,64},{128,96},{160,128},{192,160},{224,192},{0,2... | collective-permute-start | bytes 98312 | tf_op jit(solution)/shard_map/ppermute | solution.py:721
